TPU v7x, 32 devices: a whole 2x2x4 slice. The times are simulated.
32 devices in a mesh: dp: 8 (over y, x, core), expert: 4 (over z).
Axes of the slice: x: 2, y: 2, z: 4, core: 2. Of those that a mesh axis runs over, the one named last changes fastest.
Arguments:
- tokens: bfloat16 [512, 2048], P(('dp', 'expert')), may hold values from -6 to 6
- route: int32 [512, 8], P(('dp', 'expert')), may hold values from 0 to 15, all different within a row; in each aligned block of 16 rows (0 to 15, 16 to 31, ...) at most 12 rows name the same one
- probs: float32 [512, 8], P(('dp', 'expert')), may hold values from 0.03 to 0.3
- cotangent: bfloat16 [512, 2048], P(('dp', 'expert')), may hold values from -6 to 6
- gate_weight: bfloat16 [32, 2048, 384], P(('dp', 'expert')), may hold values from -0.125 to 0.125
- up_weight: bfloat16 [32, 2048, 384], P(('dp', 'expert')), may hold values from -0.125 to 0.125
- down_weight: bfloat16 [32, 384, 2048], P(('dp', 'expert')), may hold values from -0.21875 to 0.21875
Outputs:
- mixed: bfloat16 [512, 2048], P(('dp', 'expert'))
- token_grad: bfloat16 [512, 2048], P(('dp', 'expert'))
- gate_grad: bfloat16 [32, 2048, 384], P(('dp', 'expert'))
- up_grad: bfloat16 [32, 2048, 384], P(('dp', 'expert'))
- down_grad: bfloat16 [32, 384, 2048], P(('dp', 'expert'))
Inputs may be any that keep to these rules, and one draw needn't show every extreme that they name: `route`: each row names 8 different experts. In each aligned block of 16 rows (the rows of one device) no expert is named by more than 12 rows, a bound that some block reaches.
All inputs are finite; a program needn't handle non-finite values.
Results may differ from a plain program's by a relative error of at most 0.0065.
Values may be sent and summed in bfloat16 or wider, within the bound.
No kernel may reach another device: no remote copies, remote signals or barrier semaphores. Data moves between devices by JAX's collectives and lax.ppermute only.
A program may use at most 64 MiB of HBM per device.

v0:
```python
import jax
import jax.numpy as jnp
from jax import lax
from jax.sharding import PartitionSpec as P

TOP = 8


def from_partner(x, axis, apart):
    return lax.ppermute(x, axis, [(i, i ^ 1 << apart) for i in range(lax.axis_size(axis))])


def slot_tables(route_block, prob_block, experts, capacity):
    row_count, top_count = route_block.shape
    flat_ids = route_block.reshape(-1)
    onehot = (flat_ids[:, None] == jnp.arange(experts, dtype=jnp.int32)[None, :]).astype(jnp.int32)
    before = jnp.cumsum(onehot, axis=0) - onehot
    position = jnp.sum(before * onehot, axis=1)
    slot_ids = flat_ids * capacity + position
    matches = (
        slot_ids[:, None] == jnp.arange(experts * capacity, dtype=jnp.int32)[None, :]
    ).astype(jnp.float32)
    matches = matches.reshape(row_count, top_count, experts * capacity)
    return (jnp.sum(matches, axis=1), jnp.sum(matches * prob_block[:, :, None], axis=1))


def contract_last(left, right):
    return lax.dot_general(
        left, right, (((1,), (1,)), ((), ())), preferred_element_type=jnp.float32
    )


def contract_first(left, right):
    return lax.dot_general(
        left, right, (((0,), (0,)), ((), ())), preferred_element_type=jnp.float32
    )


def slice_work(slot_rows, out_cot, w_gate, w_up, w_down):
    gate_val = jnp.dot(slot_rows, w_gate, preferred_element_type=jnp.float32)
    up_val = jnp.dot(slot_rows, w_up, preferred_element_type=jnp.float32)
    sigmoid_val = jax.nn.sigmoid(gate_val)
    act_val = (gate_val * sigmoid_val * up_val).astype(jnp.bfloat16)
    out_part = jnp.dot(act_val, w_down, preferred_element_type=jnp.float32)
    act_cot = contract_last(out_cot, w_down)
    gate_cot = (act_cot * up_val * sigmoid_val * (1.0 + gate_val * (1.0 - sigmoid_val))).astype(
        jnp.bfloat16
    )
    up_cot = (act_cot * gate_val * sigmoid_val).astype(jnp.bfloat16)
    cot_part = contract_last(gate_cot, w_gate) + contract_last(up_cot, w_up)
    grad_gate = contract_first(slot_rows, gate_cot)
    grad_up = contract_first(slot_rows, up_cot)
    grad_down = contract_first(act_val, out_cot)
    return (out_part, cot_part, grad_gate, grad_up, grad_down)


def body(tokens, route, probs, cotangent, gate_weight, up_weight, down_weight):
    highest = lax.Precision.HIGHEST
    devices = lax.axis_size("dp") * lax.axis_size("expert")
    experts = devices // 2
    tok_rows, feature_width = tokens.shape
    capacity = 2 * max(1, 3 * tok_rows * TOP // (4 * experts))
    half_cap = capacity // 2
    spread, weighted = slot_tables(route, probs, experts, capacity)
    spread_half = spread.astype(jnp.bfloat16)
    send_rows = jnp.einsum("ts,td->sd", spread_half, tokens, preferred_element_type=jnp.float32)
    send_rows = send_rows.astype(jnp.bfloat16)
    send_cot = jnp.einsum("ts,td->sd", weighted, cotangent.astype(jnp.float32), precision=highest)
    send_cot = send_cot.astype(jnp.bfloat16)
    w_gate, w_up, w_down = (gate_weight[0], up_weight[0], down_weight[0])
    arrived_rows, arrived_cot = (
        lax.all_to_all(
            send_rows.reshape(devices, half_cap, feature_width),
            ("dp", "expert"),
            split_axis=0,
            concat_axis=0,
            tiled=True,
        ),
        lax.all_to_all(
            send_cot.reshape(devices, half_cap, feature_width),
            ("dp", "expert"),
            split_axis=0,
            concat_axis=0,
            tiled=True,
        ),
    )
    own_stack = jnp.stack((arrived_rows, arrived_cot))
    other_stack = from_partner(own_stack, "expert", 0)
    is_lower = lax.axis_index("expert") % 2 == 0
    lower_stack = jnp.where(is_lower, own_stack, other_stack)
    upper_stack = jnp.where(is_lower, other_stack, own_stack)
    joined = jnp.concatenate((lower_stack, upper_stack), axis=2)
    out_part, cot_part, grad_gate, grad_up, grad_down = slice_work(
        joined[0].reshape(-1, feature_width),
        joined[1].reshape(-1, feature_width),
        w_gate,
        w_up,
        w_down,
    )
    part_stack = jnp.stack(
        (
            out_part.reshape(devices, capacity, feature_width),
            cot_part.reshape(devices, capacity, feature_width),
        )
    )
    lower_part = part_stack[:, :, :half_cap]
    upper_part = part_stack[:, :, half_cap:]
    given_part = jnp.where(is_lower, upper_part, lower_part)
    kept_part = jnp.where(is_lower, lower_part, upper_part)
    taken_part = from_partner(given_part, "expert", 0)
    summed = (kept_part + taken_part).astype(jnp.bfloat16)
    back_out, back_cot = (
        lax.all_to_all(summed[0], ("dp", "expert"), split_axis=0, concat_axis=0, tiled=True),
        lax.all_to_all(summed[1], ("dp", "expert"), split_axis=0, concat_axis=0, tiled=True),
    )
    back_out = back_out.reshape(experts, capacity, feature_width)
    back_cot = back_cot.reshape(experts, capacity, feature_width)
    out_rows = back_out.reshape(-1, feature_width)
    rows_cot = back_cot.reshape(-1, feature_width)
    mixed = jnp.einsum(
        "ts,sd->td", weighted, out_rows.astype(jnp.float32), precision=highest
    ).astype(jnp.bfloat16)
    token_grad = jnp.einsum(
        "ts,sd->td", spread_half, rows_cot, preferred_element_type=jnp.float32
    ).astype(jnp.bfloat16)
    return (
        mixed,
        token_grad,
        grad_gate[None].astype(jnp.bfloat16),
        grad_up[None].astype(jnp.bfloat16),
        grad_down[None].astype(jnp.bfloat16),
    )


def solution(mesh):
    in_specs = (
        P(("dp", "expert"), None),
        P(("dp", "expert"), None),
        P(("dp", "expert"), None),
        P(("dp", "expert"), None),
        P(("dp", "expert"), None, None),
        P(("dp", "expert"), None, None),
        P(("dp", "expert"), None, None),
    )
    out_specs = (
        P(("dp", "expert"), None),
        P(("dp", "expert"), None),
        P(("dp", "expert"), None, None),
        P(("dp", "expert"), None, None),
        P(("dp", "expert"), None, None),
    )
    return jax.shard_map(body, mesh=mesh, in_specs=in_specs, out_specs=out_specs, check_vma=False)
```

profile of v0, /device:TPU:0, one launch (start us, length us, event | category | flops | bytes accessed | tf_op | source)
XLA Modules:
  0.0 277.0 jit_solution(11429366404899873260)
XLA Ops:
  3.1 1.7 convolution_convert_fusion.3
  6.0 7.3 %all-to-all-start.1 = ((bf16[32,6,2048]{2,1,0:T(8,128)(2,1)}), bf16[32,6,2048]{2,1,0:T(8,128)(2,1)S(1)}, u32[]{:S(2)}, u32[]{:S(2)}) async-start(bf16[32,6,2048]{2,1,0:T(8,128)(2,1)} %reshape.46), calls=%async_computation.1 | async-start | bytes 2097152 | tf_op jit(solution)/shard_map/all_to_all | solution.py:79
  13.7 1.2 reshape.45
  14.9 23.4 %all-to-all-done.1 = bf16[32,6,2048]{2,1,0:T(8,128)(2,1)S(1)} async-done(((bf16[32,6,2048]{2,1,0:T(8,128)(2,1)}), bf16[32,6,2048]{2,1,0:T(8,128)(2,1)S(1)}, u32[]{:S(2)}, u32[]{:S(2)}) %all-to-all-start.1) | async-done | bytes 786464 | tf_op jit(solution)/shard_map/all_to_all | solution.py:79
  38.4 4.6 %all-to-all-start = ((bf16[32,6,2048]{2,1,0:T(8,128)(2,1)}), bf16[32,6,2048]{2,1,0:T(8,128)(2,1)}, u32[]{:S(2)}, u32[]{:S(2)}) async-start(bf16[32,6,2048]{2,1,0:T(8,128)(2,1)} %reshape.45), calls=%async_computation | async-start | bytes 2097152 | tf_op jit(solution)/shard_map/all_to_all | solution.py:72
  43.4 24.6 %all-to-all-done = bf16[32,6,2048]{2,1,0:T(8,128)(2,1)} async-done(((bf16[32,6,2048]{2,1,0:T(8,128)(2,1)}), bf16[32,6,2048]{2,1,0:T(8,128)(2,1)}, u32[]{:S(2)}, u32[]{:S(2)}) %all-to-all-start) | async-done | bytes 786464 | tf_op jit(solution)/shard_map/all_to_all | solution.py:72
  68.0 1.7 copy.56
  69.6 1.3 pad_maximum_fusion.2
  70.9 3.1 %collective-permute-start = (bf16[2,32,6,2048]{3,1,2,0:T(8,128)(2,1)}, bf16[2,32,6,2048]{3,1,2,0:T(8,128)(2,1)}, u32[]{:S(2)}, u32[]{:S(2)}) collective-permute-start(bf16[2,32,6,2048]{3,1,2,0:T(8,128)(2,1)} %pad_maximum_fusion.2), channel_id=1, source_target_pairs={{0,1},{1,0},{2,3},{3,2},{4,5},{5,4},{6,7},{7,6},{8,9},{9,8},{10,11... | collective-permute-start | bytes 4718600 | tf_op jit(solution)/shard_map/ppermute | solution.py:10
  74.0 35.1 %collective-permute-done = bf16[2,32,6,2048]{3,1,2,0:T(8,128)(2,1)} collective-permute-done((bf16[2,32,6,2048]{3,1,2,0:T(8,128)(2,1)}, bf16[2,32,6,2048]{3,1,2,0:T(8,128)(2,1)}, u32[]{:S(2)}, u32[]{:S(2)}) %collective-permute-start) | collective-permute-done | bytes 1572896 | tf_op jit(solution)/shard_map/ppermute | solution.py:10
  109.1 1.6 broadcast_select_fusion.1
  111.0 2.2 copy.45
  113.2 3.6 %reshape_squeeze.6 = bf16[384,2048]{1,0:T(8,128)(2,1)} reshape(bf16[1,32,12,2048]{3,2,1,0:T(8,128)(2,1)} %copy.45) | data formatting | bytes 3145728 | tf_op jit(solution)/shard_map/reshape;squeeze | solution.py:94
  116.8 2.2 copy.47
  119.1 3.7 %reshape_squeeze.7 = bf16[384,2048]{1,0:T(8,128)(2,1)} reshape(bf16[1,32,12,2048]{3,2,1,0:T(8,128)(2,1)} %copy.47) | data formatting | bytes 3145728 | tf_op jit(solution)/shard_map/reshape;squeeze | solution.py:95
  122.8 2.5 fusion.13
  126.8 1.9 multiply_convert_fusion.2
  129.7 2.7 convolution_add_fusion
  132.4 4.6 %stack_reshape.4 = f32[1,32,12,2048]{3,2,1,0:T(8,128)} reshape(f32[384,2048]{1,0:T(8,128)} %convolution_add_fusion) | data formatting | bytes 6291456 | tf_op jit(solution)/shard_map/stack;reshape | solution.py:100
  137.0 4.0 %copy.48 = f32[1,32,12,2048]{3,1,2,0:T(8,128)S(1)} copy(f32[1,32,12,2048]{3,2,1,0:T(8,128)} %stack_reshape.4) | data formatting | bytes 6291456 | tf_op jit(solution)/shard_map/stack;reshape | solution.py:100
  142.0 2.4 convolution_bitcast_fusion
  145.3 69.4 %collective-permute-done.1 = f32[2,32,6,2048]{3,1,2,0:T(8,128)S(1)} collective-permute-done((f32[2,32,6,2048]{3,1,2,0:T(8,128)S(1)}, f32[2,32,6,2048]{3,1,2,0:T(8,128)S(1)}, u32[]{:S(2)}, u32[]{:S(2)}) %collective-permute-start.1) | collective-permute-done | bytes 3145760 | tf_op jit(solution)/shard_map/ppermute | solution.py:10
  215.9 1.4 copy.50
  217.3 2.6 all-to-all-start.3
  220.0 1.4 copy.49
  221.4 23.6 %all-to-all-done.3 = bf16[32,6,2048]{2,1,0:T(8,128)(2,1)S(1)} async-done(((bf16[32,6,2048]{2,1,0:T(8,128)(2,1)}), bf16[32,6,2048]{2,1,0:T(8,128)(2,1)S(1)}, u32[]{:S(2)}, u32[]{:S(2)}) %all-to-all-start.3) | async-done | bytes 786464 | tf_op jit(solution)/shard_map/all_to_all | solution.py:114
  245.0 4.5 %all-to-all-start.2 = ((bf16[32,6,2048]{2,1,0:T(8,128)(2,1)}), bf16[32,6,2048]{2,1,0:T(8,128)(2,1)}, u32[]{:S(2)}, u32[]{:S(2)}) async-start(bf16[32,6,2048]{2,1,0:T(8,128)(2,1)} %copy.49), calls=%async_computation.2 | async-start | bytes 2097152 | tf_op jit(solution)/shard_map/all_to_all | solution.py:113
  249.6 2.2 fusion.3
  251.8 2.3 fusion.1
  254.1 2.3 fusion.2
  257.9 16.6 %all-to-all-done.2 = bf16[32,6,2048]{2,1,0:T(8,128)(2,1)} async-done(((bf16[32,6,2048]{2,1,0:T(8,128)(2,1)}), bf16[32,6,2048]{2,1,0:T(8,128)(2,1)}, u32[]{:S(2)}, u32[]{:S(2)}) %all-to-all-start.2) | async-done | bytes 786464 | tf_op jit(solution)/shard_map/all_to_all | solution.py:113
  274.6 1.4 reshape_reshape.6
  (55 shorter events, 12.9 us)
Async XLA Ops:
  0.6 125.7 %copy-start = (bf16[1,2048,384]{2,1,0:T(8,128)(2,1)S(1)}, bf16[1,2048,384]{2,1,0:T(8,128)(2,1)}, u32[]{:S(2)}) copy-start(bf16[1,2048,384]{2,1,0:T(8,128)(2,1)} %param.12) | copy-start | bytes 4718596
  3.1 10.2 %copy-start.13 = (bf16[16,192]{1,0:T(8,128)(2,1)}, bf16[16,192]{1,0:T(8,128)(2,1)S(1)}, u32[]{:S(2)}) copy-start(bf16[16,192]{1,0:T(8,128)(2,1)S(1)} %get-tuple-element.5) | copy-start | bytes 18436
  4.8 8.6 %copy-start.15 = (bf16[16,2048]{1,0:T(8,128)(2,1)S(1)}, bf16[16,2048]{1,0:T(8,128)(2,1)}, u32[]{:S(2)}) copy-start(bf16[16,2048]{1,0:T(8,128)(2,1)} %param.7) | copy-start | bytes 196612
  6.0 32.4 %all-to-all-start.1 = ((bf16[32,6,2048]{2,1,0:T(8,128)(2,1)}), bf16[32,6,2048]{2,1,0:T(8,128)(2,1)S(1)}, u32[]{:S(2)}, u32[]{:S(2)}) async-start(bf16[32,6,2048]{2,1,0:T(8,128)(2,1)} %reshape.46), calls=%async_computation.1 | async-start | bytes 2097152 | tf_op jit(solution)/shard_map/all_to_all | solution.py:79
  38.4 29.6 %all-to-all-start = ((bf16[32,6,2048]{2,1,0:T(8,128)(2,1)}), bf16[32,6,2048]{2,1,0:T(8,128)(2,1)}, u32[]{:S(2)}, u32[]{:S(2)}) async-start(bf16[32,6,2048]{2,1,0:T(8,128)(2,1)} %reshape.45), calls=%async_computation | async-start | bytes 2097152 | tf_op jit(solution)/shard_map/all_to_all | solution.py:72
  70.9 38.2 %collective-permute-start = (bf16[2,32,6,2048]{3,1,2,0:T(8,128)(2,1)}, bf16[2,32,6,2048]{3,1,2,0:T(8,128)(2,1)}, u32[]{:S(2)}, u32[]{:S(2)}) collective-permute-start(bf16[2,32,6,2048]{3,1,2,0:T(8,128)(2,1)} %pad_maximum_fusion.2), channel_id=1, source_target_pairs={{0,1},{1,0},{2,3},{3,2},{4,5},{5,4},{6,7},{7,6},{8,9},{9,8},{10,11... | collective-permute-start | bytes 4718600 | tf_op jit(solution)/shard_map/ppermute | solution.py:10
  119.1 3.7 %copy-start.2 = (bf16[1,2048,384]{2,1,0:T(8,128)(2,1)S(1)}, bf16[1,2048,384]{2,1,0:T(8,128)(2,1)}, u32[]{:S(2)}) copy-start(bf16[1,2048,384]{2,1,0:T(8,128)(2,1)} %param.11) | copy-start | bytes 4718596
  122.8 2.5 copy-start.3
  122.8 2.6 copy-start.6
  125.4 1.4 copy-start.4
  128.7 1.0 copy-start.10
  128.7 1.0 copy-start.8
  144.9 69.8 %collective-permute-start.1 = (f32[2,32,6,2048]{3,1,2,0:T(8,128)S(1)}, f32[2,32,6,2048]{3,1,2,0:T(8,128)S(1)}, u32[]{:S(2)}, u32[]{:S(2)}) collective-permute-start(f32[2,32,6,2048]{3,1,2,0:T(8,128)S(1)} %broadcast_select_fusion), channel_id=1, source_target_pairs={{0,1},{1,0},{2,3},{3,2},{4,5},{5,4},{6,7},{7,6},{8,9},{9,8},{10,11... | collective-permute-start | bytes 9437192 | tf_op jit(solution)/shard_map/ppermute | solution.py:10
  217.3 27.7 %all-to-all-start.3 = ((bf16[32,6,2048]{2,1,0:T(8,128)(2,1)}), bf16[32,6,2048]{2,1,0:T(8,128)(2,1)S(1)}, u32[]{:S(2)}, u32[]{:S(2)}) async-start(bf16[32,6,2048]{2,1,0:T(8,128)(2,1)} %copy.50), calls=%async_computation.3 | async-start | bytes 2097152 | tf_op jit(solution)/shard_map/all_to_all | solution.py:114
  220.0 29.6 %copy-start.12 = (bf16[384,384]{1,0:T(8,128)(2,1)S(1)}, bf16[384,384]{1,0:T(8,128)(2,1)}, u32[]{:S(2)}) copy-start(bf16[384,384]{1,0:T(8,128)(2,1)} %get-tuple-element.13) | copy-start | bytes 884740
  221.4 28.1 %copy-start.7 = (bf16[384,2048]{1,0:T(8,128)(2,1)S(1)}, bf16[384,2048]{1,0:T(8,128)(2,1)}, u32[]{:S(2)}) copy-start(bf16[384,2048]{1,0:T(8,128)(2,1)} %reshape_squeeze.7) | copy-start | bytes 4718596
  245.0 29.6 %all-to-all-start.2 = ((bf16[32,6,2048]{2,1,0:T(8,128)(2,1)}), bf16[32,6,2048]{2,1,0:T(8,128)(2,1)}, u32[]{:S(2)}, u32[]{:S(2)}) async-start(bf16[32,6,2048]{2,1,0:T(8,128)(2,1)} %copy.49), calls=%async_computation.2 | async-start | bytes 2097152 | tf_op jit(solution)/shard_map/all_to_all | solution.py:113
  249.6 2.2 copy-start.5
  249.6 2.2 copy-start.11
  251.8 2.3 copy-start.9
  256.4 0.7 copy-start.14
  256.4 20.6 %copy-start.1 = (bf16[1,2048,384]{2,1,0:T(8,128)(2,1)S(1)}, bf16[1,2048,384]{2,1,0:T(8,128)(2,1)}, u32[]{:S(2)}) copy-start(bf16[1,2048,384]{2,1,0:T(8,128)(2,1)} %param.12) | copy-start | bytes 4718596
where the time goes:
time: 279 us; the launch traced here: 277 us
  waiting for transfers between devices  193 us (69%)
  local copies, waits for them, and re-layouts  33.3 us (12%)
  starting transfers between devices  22.5 us (8%)
  matrix products  22.3 us (8%)
  other arithmetic  5.34 us (2%)
    ppermute x2, waiting for transfers between devices, from_partner(): lax.ppermute(x, axis, [(i, i ^ 1 << apart) for i in range(lax.axis_size(a...  104 us
    all_to_all x1, waiting for transfers between devices, body(): lax.all_to_all(send_rows.reshape(devices, half_cap, feature_width), ('dp'...  24.6 us
    all_to_all x1, waiting for transfers between devices, body(): lax.all_to_all(summed[1], ('dp', 'expert'), split_axis=0, concat_axis=0,...  23.6 us
    all_to_all x1, waiting for transfers between devices, body(): lax.all_to_all(send_cot.reshape(devices, half_cap, feature_width), ('dp',...  23.4 us
    all_to_all x1, waiting for transfers between devices, body(): lax.all_to_all(summed[0], ('dp', 'expert'), split_axis=0, concat_axis=0,...  16.6 us
    another operation x2, local copies, waits for them, and re-layouts, body(): jnp.stack((out_part.reshape(devices, capacity, feature_width), cot_part.r...  8.59 us
    all_to_all x1, starting transfers between devices, body(): lax.all_to_all(send_cot.reshape(devices, half_cap, feature_width), ('dp',...  7.3 us
    dot_general x3, matrix products, contract_first(): lax.dot_general(left, right, (((0,), (0,)), ((), ())), preferred_element_...  6.79 us
  transfers between devices with their start and end apart: 6, of which 6 were waited for; matrix products, arithmetic and copies ran while one was open for 4% of the time, Pallas kernels for 0%

commit v1 on v0

v1 whole, which is shorter than its diff:
```python
import jax
import jax.numpy as jnp
from jax import lax
from jax.sharding import PartitionSpec as P

AXES = ("dp", "expert")
F32, BF16 = jnp.float32, jnp.bfloat16


def permutes(n_dp, n_ex):
    def pairs(to):
        out = []
        for d in range(n_dp):
            for z in range(n_ex):
                e, y = to(d, z)
                out.append((d * n_ex + z, e * n_ex + y))
        return out

    def mixed(step, bits):
        def to(d, z):
            bit = step if d % 2 == 0 else bits - 1 - step
            return d ^ (2 << bit), z

        return pairs(to)

    bits = n_dp.bit_length() - 2
    core = pairs(lambda d, z: (d ^ 1, z))
    plane = [mixed(s, bits) for s in range(bits)]
    both, back_both = [], []
    for j in range(1, n_ex - 1, 2):
        both.append(pairs(lambda d, z, j=j: (d, (z + j + d % 2) % n_ex)))
        back_both.append(pairs(lambda d, z, j=j: (d, (z - j - d % 2) % n_ex)))
    last = pairs(lambda d, z: (d, (z + n_ex - 1) % n_ex))
    back_last = pairs(lambda d, z: (d, (z + 1) % n_ex))
    return core, plane, both, back_both, last, back_last


def send(x, pairs):
    return lax.ppermute(x, AXES, pairs)


def gather_lane(own, perms):
    core, plane, both, _, last, _ = perms
    chip = jnp.concatenate((own, send(own, core)))
    lane = [own] + [send(chip, p) for p in both] + [send(own, last)]
    lane = jnp.concatenate(lane)
    for p in plane:
        lane = jnp.concatenate((lane, send(lane, p)))
    return lane


def add(a, b):
    return a.astype(F32) + b.astype(F32)


def reduce_back(kept, given, rows, perms):
    core, plane, _, back_both, _, back_last = perms
    lane = add(kept, send(given, core))
    for p in reversed(plane):
        lane = lane.astype(BF16)
        half = lane.shape[0] // 2
        lane = add(lane[:half], send(lane[half:], p))
    lane = lane.astype(BF16)
    total = lane[:rows].astype(F32)
    given = jnp.zeros_like(total)
    at = rows
    for p in back_both:
        back = send(lane[at : at + 2 * rows], p).astype(F32)
        total, given = total + back[:rows], given + back[rows:]
        at += 2 * rows
    total = total + send(lane[at:], back_last).astype(F32)
    return (total + send(given, core)).astype(BF16)


def contract_last(left, right):
    return lax.dot_general(left, right, (((1,), (1,)), ((), ())), preferred_element_type=F32)


def contract_first(left, right):
    return lax.dot_general(left, right, (((0,), (0,)), ((), ())), preferred_element_type=F32)


def dot(left, right):
    return jnp.dot(left, right, preferred_element_type=F32)


def weight_table(route, probs, experts):
    hit = route[:, :, None] == jnp.arange(experts, dtype=jnp.int32)
    table = jnp.sum(jnp.where(hit, probs[:, :, None], 0.0), axis=1)
    parts = []
    for _ in range(3):
        part = lax.reduce_precision(table, 8, 7)
        parts.append(part.astype(BF16))
        table = table - part
    table = jnp.concatenate(parts, axis=1)
    return jnp.pad(table, ((0, 0), (0, -table.shape[1] % 128)))


def body(tokens, route, probs, cotangent, gate_weight, up_weight, down_weight):
    n_dp, n_ex = lax.axis_size("dp"), lax.axis_size("expert")
    experts = n_dp * n_ex // 2
    rows, width = tokens.shape
    perms = permutes(n_dp, n_ex)
    core = perms[0]
    w_gate, w_up, w_down = gate_weight[0], up_weight[0], down_weight[0]

    lane_rows = gather_lane(jnp.concatenate((tokens, weight_table(route, probs, experts)), axis=1), perms)
    lane_cot = gather_lane(cotangent, perms)
    all_rows = jnp.concatenate((lane_rows, send(lane_rows, core)))
    all_cot = jnp.concatenate((lane_cot, send(lane_cot, core)))

    expert = (lax.axis_index("dp") * n_ex + lax.axis_index("expert")) // 2
    table = all_rows[:, width:].astype(F32)
    columns = jnp.arange(table.shape[1], dtype=jnp.int32)
    mine = (columns % experts == expert) & (columns < 3 * experts)
    p = jnp.sum(jnp.where(mine, table, 0.0), axis=1, keepdims=True)
    x = all_rows[:, :width]
    out_cot = (p * all_cot.astype(F32)).astype(BF16)

    gate_val, up_val = dot(x, w_gate), dot(x, w_up)
    s = jax.nn.sigmoid(gate_val)
    act = (gate_val * s * up_val).astype(BF16)
    half = act.shape[0] // 2
    mixed = reduce_back(
        (p[:half] * dot(act[:half], w_down)).astype(BF16),
        (p[half:] * dot(act[half:], w_down)).astype(BF16),
        rows,
        perms,
    )
    act_cot = contract_last(out_cot, w_down)
    gate_cot = (act_cot * up_val * s * (1.0 + gate_val * (1.0 - s))).astype(BF16)
    up_cot = (act_cot * gate_val * s).astype(BF16)
    kept, given = (
        (contract_last(g, w_gate) + contract_last(u, w_up)).astype(BF16)
        for g, u in ((gate_cot[:half], up_cot[:half]), (gate_cot[half:], up_cot[half:]))
    )
    token_grad = reduce_back(kept, given, rows, perms)
    return (
        mixed,
        token_grad,
        contract_first(x, gate_cot).astype(BF16)[None],
        contract_first(x, up_cot).astype(BF16)[None],
        contract_first(act, out_cot).astype(BF16)[None],
    )


def solution(mesh):
    two, three = P(AXES, None), P(AXES, None, None)
    return jax.shard_map(
        body,
        mesh=mesh,
        in_specs=(two, two, two, two, three, three, three),
        out_specs=(two, two, three, three, three),
        check_vma=False,
    )
```

time: 279 us -> 100 us (0.36)
  waiting for transfers between devices: 193 us -> 33.2 us
  local copies, waits for them, and re-layouts: 33.3 us -> 14.4 us
  matrix products: 22.3 us -> 17.4 us
  starting transfers between devices: 22.5 us -> 26.8 us
    all_to_all x4 -> x0, waiting for transfers between devices: 88.2 us -> none  [the longest x1 24.6 us: body(): lax.all_to_all(send_rows.reshape(devices, half_cap, feature_width), ('dp'...]
    ppermute x2 -> x24, waiting for transfers between devices: 104 us -> 33.2 us  [send(): return lax.ppermute(x, AXES, pairs)]
    ppermute x2 -> x24, starting transfers between devices: 3.44 us -> 26.8 us  [send(): return lax.ppermute(x, AXES, pairs)]
    all_to_all x4 -> x0, starting transfers between devices: 19.1 us -> none  [the longest x1 7.3 us: body(): lax.all_to_all(send_cot.reshape(devices, half_cap, feature_width), ('dp',...]
    another operation x7 -> x0, local copies, waits for them, and re-layouts: 18.6 us -> none  [the longest x2 8.59 us: body(): jnp.stack((out_part.reshape(devices, capacity, feature_width), cot_part.r...]
    unnamed x34 -> x27, local copies, waits for them, and re-layouts: 2.53 us -> 8.85 us
    concatenate x0 -> x4, local copies, waits for them, and re-layouts: none -> 5.33 us  [the longest x1 2.43 us: body(): all_cot = jnp.concatenate((lane_cot, send(lane_cot, core)))]
    dot_general x7 -> x4, matrix products: 10.7 us -> 5.74 us  [dot(): return jnp.dot(left, right, preferred_element_type=F32)]
  transfers between devices with their start and end apart: 6 -> 24, of which waited for: 6 -> 11; matrix products, arithmetic and copies ran while one was open for 4% -> 28% of each run, Pallas kernels for 0% -> 0%
where the time goes in v1:
time: 100 us; the launch traced here: 99.9 us
  waiting for transfers between devices  33.2 us (33%)
  starting transfers between devices  26.8 us (27%)
  matrix products  17.4 us (17%)
  local copies, waits for them, and re-layouts  14.4 us (14%)
  other arithmetic  7.12 us (7%)
  between operations  1 us (1%)
    ppermute x24, waiting for transfers between devices, send(): return lax.ppermute(x, AXES, pairs)  33.2 us
    ppermute x24, starting transfers between devices, send(): return lax.ppermute(x, AXES, pairs)  26.8 us
    unnamed x27, local copies, waits for them, and re-layouts  8.85 us
    dot_general x3, matrix products, contract_first(): lax.dot_general(left, right, (((0,), (0,)), ((), ())), preferred_element_...  7.13 us
    dot_general x4, matrix products, dot(): return jnp.dot(left, right, preferred_element_type=F32)  5.74 us
    dot_general x5, matrix products, contract_last(): lax.dot_general(left, right, (((1,), (1,)), ((), ())), preferred_element_...  4.56 us
    concatenate x1, local copies, waits for them, and re-layouts, body(): all_cot = jnp.concatenate((lane_cot, send(lane_cot, core)))  2.43 us
  transfers between devices with their start and end apart: 24, of which 11 were waited for; matrix products, arithmetic and copies ran while one was open for 28% of the time, Pallas kernels for 0%

profile of v1, /device:TPU:0, one launch (start us, length us, event | category | flops | bytes accessed | tf_op | source)
XLA Modules:
  0.0 99.9 jit_solution(15596029126647168223)
XLA Ops:
  0.7 5.1 %collective-permute-start.14 = (bf16[16,2048]{1,0:T(8,128)(2,1)}, bf16[16,2048]{1,0:T(8,128)(2,1)S(1)}, u32[]{:S(2)}, u32[]{:S(2)}) collective-permute-start(bf16[16,2048]{1,0:T(8,128)(2,1)} %param.10), channel_id=1, source_target_pairs={{0,3},{1,0},{2,1},{3,2},{4,7},{5,4},{6,5},{7,6},{8,11},{9,8},{10,9... | collective-permute-start | bytes 196616 | tf_op jit(solution)/shard_map/ppermute | solution.py:39
  7.5 1.5 %constant_dynamic-update-slice_fusion.4 = (bf16[256,2176]{1,0:T(8,128)(2,1)}, bf16[512,2176]{1,0:T(8,128)(2,1)S(1)}, bf16[16,2176]{1,0:T(8,128)(2,1)S(1)}) fusion(bf16[16,128]{1,0:T(8,128)(2,1)S(1)} %fusion.49, bf16[16,2048]{1,0:T(8,128)(2,1)} %param.7), kind=kLoop, calls=%fused_computation.73 | loop fusion | flops 139262 | bytes 278528
  9.9 1.5 %constant_dynamic-update-slice_fusion.15 = (bf16[256,2048]{1,0:T(8,128)(2,1)}, bf16[512,2048]{1,0:T(8,128)(2,1)S(1)}) fusion(bf16[16,2048]{1,0:T(8,128)(2,1)} %param.10), kind=kLoop, calls=%fused_computation.84 | loop fusion | bytes 196608
  12.3 1.6 %collective-permute-start.13 = (bf16[32,2048]{1,0:T(8,128)(2,1)S(1)}, bf16[32,2048]{1,0:T(8,128)(2,1)S(1)}, u32[]{:S(2)}, u32[]{:S(2)}) collective-permute-start(bf16[32,2048]{1,0:T(8,128)(2,1)S(1)} %pad_maximum_fusion.5), channel_id=1, source_target_pairs={{0,1},{1,2},{2,3},{3,0},{4,6},{5,7},{6,4},{7,5},{8,9},{9,10},{10,1... | collective-permute-start | bytes 393224 | tf_op jit(solution)/shard_map/ppermute | solution.py:39
  14.8 5.7 %collective-permute-done.13 = bf16[32,2048]{1,0:T(8,128)(2,1)S(1)} collective-permute-done((bf16[32,2048]{1,0:T(8,128)(2,1)S(1)}, bf16[32,2048]{1,0:T(8,128)(2,1)S(1)}, u32[]{:S(2)}, u32[]{:S(2)}) %collective-permute-start.13) | collective-permute-done | bytes 131104 | tf_op jit(solution)/shard_map/ppermute | solution.py:39
  21.4 1.6 %collective-permute-start.15 = (bf16[64,2048]{1,0:T(8,128)(2,1)S(1)}, bf16[64,2048]{1,0:T(8,128)(2,1)S(1)}, u32[]{:S(2)}, u32[]{:S(2)}) collective-permute-start(bf16[64,2048]{1,0:T(8,128)(2,1)S(1)} %pad_maximum_fusion.3), channel_id=1, source_target_pairs={{0,8},{1,9},{2,10},{3,11},{4,20},{5,21},{6,22},{7,23},{8,0},{9,1},... | collective-permute-start | bytes 786440 | tf_op jit(solution)/shard_map/ppermute | solution.py:39
  26.3 1.6 %collective-permute-done.15 = bf16[64,2048]{1,0:T(8,128)(2,1)S(1)} collective-permute-done((bf16[64,2048]{1,0:T(8,128)(2,1)S(1)}, bf16[64,2048]{1,0:T(8,128)(2,1)S(1)}, u32[]{:S(2)}, u32[]{:S(2)}) %collective-permute-start.15) | collective-permute-done | bytes 262176 | tf_op jit(solution)/shard_map/ppermute | solution.py:39
  27.9 1.6 %collective-permute-start.16 = (bf16[128,2048]{1,0:T(8,128)(2,1)S(1)}, bf16[128,2048]{1,0:T(8,128)(2,1)S(1)}, u32[]{:S(2)}, u32[]{:S(2)}) collective-permute-start(bf16[128,2048]{1,0:T(8,128)(2,1)S(1)} %pad_maximum_fusion.1), channel_id=1, source_target_pairs={{0,16},{1,17},{2,18},{3,19},{4,12},{5,13},{6,14},{7,15},{8,24},{9,... | collective-permute-start | bytes 1572872 | tf_op jit(solution)/shard_map/ppermute | solution.py:39
  31.0 1.6 %collective-permute-start.4 = (bf16[128,2176]{1,0:T(8,128)(2,1)S(1)}, bf16[128,2176]{1,0:T(8,128)(2,1)S(1)}, u32[]{:S(2)}, u32[]{:S(2)}) collective-permute-start(bf16[128,2176]{1,0:T(8,128)(2,1)S(1)} %pad_maximum_fusion), channel_id=1, source_target_pairs={{0,16},{1,17},{2,18},{3,19},{4,12},{5,13},{6,14},{7,15},{8,24},{9,... | collective-permute-start | bytes 1671176 | tf_op jit(solution)/shard_map/ppermute | solution.py:39
  33.3 4.2 %collective-permute-done.16 = bf16[128,2048]{1,0:T(8,128)(2,1)S(1)} collective-permute-done((bf16[128,2048]{1,0:T(8,128)(2,1)S(1)}, bf16[128,2048]{1,0:T(8,128)(2,1)S(1)}, u32[]{:S(2)}, u32[]{:S(2)}) %collective-permute-start.16) | collective-permute-done | bytes 524320 | tf_op jit(solution)/shard_map/ppermute | solution.py:39
  37.5 0.9 constant_dynamic-update-slice_fusion.11
  38.4 5.0 %collective-permute-done.4 = bf16[128,2176]{1,0:T(8,128)(2,1)S(1)} collective-permute-done((bf16[128,2176]{1,0:T(8,128)(2,1)S(1)}, bf16[128,2176]{1,0:T(8,128)(2,1)S(1)}, u32[]{:S(2)}, u32[]{:S(2)}) %collective-permute-start.4) | collective-permute-done | bytes 557088 | tf_op jit(solution)/shard_map/ppermute | solution.py:39
  44.3 1.4 %copy-done.5 = bf16[512,2176]{1,0:T(8,128)(2,1)} copy-done((bf16[512,2176]{1,0:T(8,128)(2,1)}, bf16[512,2176]{1,0:T(8,128)(2,1)S(1)}, u32[]{:S(2)}) %copy-start.5) | copy-done | bytes 2228248
  45.8 2.4 %constant_dynamic-update-slice_fusion.16 = bf16[512,2048]{1,0:T(8,128)(2,1)} fusion(bf16[512,2048]{1,0:T(8,128)(2,1)} %copy-done.7, bf16[256,2048]{1,0:T(8,128)(2,1)} %collective-permute-done.17), kind=kLoop, calls=%fused_computation.85 | loop fusion | bytes 2097152 | tf_op jit(solution)/shard_map/concatenate | solution.py:110
  48.7 1.1 %constant_dynamic-update-slice_fusion.5 = bf16[512,2176]{1,0:T(8,128)(2,1)} fusion(bf16[512,2176]{1,0:T(8,128)(2,1)} %copy-done.5, bf16[256,2176]{1,0:T(8,128)(2,1)S(1)} %collective-permute-done.5), kind=kLoop, calls=%fused_computation.74 | loop fusion | bytes 2228224 | tf_op jit(solution)/shard_map/concatenate | solution.py:109
  49.8 1.0 %select_reduce_fusion = f32[512]{0:T(512)S(1)} fusion(bf16[512,2176]{1,0:T(8,128)(2,1)} %constant_dynamic-update-slice_fusion.5, pred[128]{0:T(512)(128)(4,1)S(1)} %compare_and_fusion), kind=kLoop, calls=%fused_computation.49 | loop fusion | flops 196096 | bytes 133248 | tf_op jit(solution)/shard_map/reduce_sum | solution.py:116
  50.9 3.0 %fusion.17 = f32[512,384]{1,0:T(8,128)S(1)} fusion(bf16[1,2048,384]{2,1,0:T(8,128)(2,1)S(1)} %copy-done.2, bf16[512,2176]{1,0:T(8,128)(2,1)} %constant_dynamic-update-slice_fusion.5), kind=kOutput, calls=%fused_computation.25 | convolution fusion | flops 805306368 | bytes 4456448 | tf_op jit(solution)/shard_map/dot_general | solution.py:84
  53.9 1.3 %fusion.25 = f32[512,384]{1,0:T(8,128)S(1)} fusion(bf16[1,2048,384]{2,1,0:T(8,128)(2,1)S(1)} %copy-done.1, bf16[512,2176]{1,0:T(8,128)(2,1)S(1)} %copy-done.6), kind=kOutput, calls=%fused_computation.31 | convolution fusion | flops 805306368 | bytes 4456448 | tf_op jit(solution)/shard_map/dot_general | solution.py:84
  55.5 1.5 %multiply_convert_fusion.3 = (bf16[512,384]{1,0:T(8,128)(2,1)S(1)}, bf16[512,384]{1,0:T(8,128)(2,1)S(1)}, bf16[512,384]{1,0:T(8,128)(2,1)S(1)}) fusion(f32[512,384]{1,0:T(8,128)S(1)} %fusion.25, f32[512,384]{1,0:T(8,128)S(1)} %fusion.17, bf16[1,384,2048]{2,1,0:T(8,128)(2,1)S(1)} %copy-done, bf16[512,2048]{1,0:T(8,128)(2,1)S(1)} %copy-done.8, ...), kind=kOutput, calls=%fused_computation.39 | convolution fusion | flops 811597824 | bytes 6424576 | tf_op jit(solution)/shard_map/dot_general | solution.py:76
  60.7 2.4 %fusion.1 = bf16[1,2048,384]{2,1,0:T(8,128)(2,1)} fusion(bf16[512,384]{1,0:T(8,128)(2,1)S(1)} %get-tuple-element.5, bf16[512,2176]{1,0:T(8,128)(2,1)S(1)} %copy-done.6), kind=kOutput, calls=%fused_computation.9 | convolution fusion | flops 806092800 | bytes 4063232 | tf_op jit(solution)/shard_map/dot_general | solution.py:80
  63.9 1.6 %collective-permute-start.7 = (bf16[128,2048]{1,0:T(8,128)(2,1)S(1)}, bf16[128,2048]{1,0:T(8,128)(2,1)S(1)}, u32[]{:S(2)}, u32[]{:S(2)}) collective-permute-start(bf16[128,2048]{1,0:T(8,128)(2,1)S(1)} %slice.119), channel_id=1, source_target_pairs={{0,16},{1,17},{2,18},{3,19},{4,12},{5,13},{6,14},{7,15},{8,24},{9,... | collective-permute-start | bytes 1572872 | tf_op jit(solution)/shard_map/ppermute | solution.py:39
  66.9 2.4 %fusion = bf16[1,2048,384]{2,1,0:T(8,128)(2,1)} fusion(bf16[512,384]{1,0:T(8,128)(2,1)S(1)} %get-tuple-element.6, bf16[512,2176]{1,0:T(8,128)(2,1)S(1)} %copy-done.6), kind=kOutput, calls=%fused_computation.8 | convolution fusion | flops 806092800 | bytes 4063232 | tf_op jit(solution)/shard_map/dot_general | solution.py:80
  69.3 3.8 %collective-permute-done.7 = bf16[128,2048]{1,0:T(8,128)(2,1)S(1)} collective-permute-done((bf16[128,2048]{1,0:T(8,128)(2,1)S(1)}, bf16[128,2048]{1,0:T(8,128)(2,1)S(1)}, u32[]{:S(2)}, u32[]{:S(2)}) %collective-permute-start.7) | collective-permute-done | bytes 524320 | tf_op jit(solution)/shard_map/ppermute | solution.py:39
  73.3 1.6 %collective-permute-start.8 = (bf16[64,2048]{1,0:T(8,128)(2,1)S(1)}, bf16[64,2048]{1,0:T(8,128)(2,1)S(1)}, u32[]{:S(2)}, u32[]{:S(2)}) collective-permute-start(bf16[64,2048]{1,0:T(8,128)(2,1)S(1)} %slice.121), channel_id=1, source_target_pairs={{0,8},{1,9},{2,10},{3,11},{4,20},{5,21},{6,22},{7,23},{8,0},{9,1},... | collective-permute-start | bytes 786440 | tf_op jit(solution)/shard_map/ppermute | solution.py:39
  74.9 6.7 %collective-permute-done.19 = bf16[128,2048]{1,0:T(8,128)(2,1)S(1)} collective-permute-done((bf16[128,2048]{1,0:T(8,128)(2,1)S(1)}, bf16[128,2048]{1,0:T(8,128)(2,1)S(1)}, u32[]{:S(2)}, u32[]{:S(2)}) %collective-permute-start.19) | collective-permute-done | bytes 524320 | tf_op jit(solution)/shard_map/ppermute | solution.py:39
  81.7 1.6 %collective-permute-start.20 = (bf16[64,2048]{1,0:T(8,128)(2,1)S(1)}, bf16[64,2048]{1,0:T(8,128)(2,1)S(1)}, u32[]{:S(2)}, u32[]{:S(2)}) collective-permute-start(bf16[64,2048]{1,0:T(8,128)(2,1)S(1)} %slice.134), channel_id=1, source_target_pairs={{0,8},{1,9},{2,10},{3,11},{4,20},{5,21},{6,22},{7,23},{8,0},{9,1},... | collective-permute-start | bytes 786440 | tf_op jit(solution)/shard_map/ppermute | solution.py:39
  83.5 3.8 %collective-permute-start.9 = (bf16[32,2048]{1,0:T(8,128)(2,1)S(1)}, bf16[32,2048]{1,0:T(8,128)(2,1)S(1)}, u32[]{:S(2)}, u32[]{:S(2)}) collective-permute-start(bf16[32,2048]{1,0:T(8,128)(2,1)S(1)} %slice.123), channel_id=1, source_target_pairs={{0,3},{1,0},{2,1},{3,2},{4,6},{5,7},{6,4},{7,5},{8,11},{9,8},{10,9... | collective-permute-start | bytes 393224 | tf_op jit(solution)/shard_map/ppermute | solution.py:39
  87.3 0.9 collective-permute-done.20
  88.3 1.5 %collective-permute-done.9 = bf16[32,2048]{1,0:T(8,128)(2,1)S(1)} collective-permute-done((bf16[32,2048]{1,0:T(8,128)(2,1)S(1)}, bf16[32,2048]{1,0:T(8,128)(2,1)S(1)}, u32[]{:S(2)}, u32[]{:S(2)}) %collective-permute-start.9) | collective-permute-done | bytes 131104 | tf_op jit(solution)/shard_map/ppermute | solution.py:39
  90.7 2.3 %fusion.2 = bf16[1,384,2048]{2,1,0:T(8,128)(2,1)} fusion(bf16[512,384]{1,0:T(8,128)(2,1)S(1)} %get-tuple-element.7, bf16[512,2048]{1,0:T(8,128)(2,1)S(1)} %copy-done.8, f32[512]{0:T(512)S(1)} %select_reduce_fusion), kind=kOutput, calls=%fused_computation.10 | convolution fusion | flops 809238528 | bytes 4065280 | tf_op jit(solution)/shard_map/dot_general | solution.py:80
  93.0 2.8 %collective-permute-start.22 = (bf16[16,2048]{1,0:T(8,128)(2,1)S(1)}, bf16[16,2048]{1,0:T(8,128)(2,1)S(1)}, u32[]{:S(2)}, u32[]{:S(2)}) collective-permute-start(bf16[16,2048]{1,0:T(8,128)(2,1)S(1)} %slice.138), channel_id=1, source_target_pairs={{0,1},{1,2},{2,3},{3,0},{4,5},{5,6},{6,7},{7,4},{8,9},{9,10},{10,1... | collective-permute-start | bytes 196616 | tf_op jit(solution)/shard_map/ppermute | solution.py:39
  96.8 2.5 %collective-permute-done.22 = bf16[16,2048]{1,0:T(8,128)(2,1)S(1)} collective-permute-done((bf16[16,2048]{1,0:T(8,128)(2,1)S(1)}, bf16[16,2048]{1,0:T(8,128)(2,1)S(1)}, u32[]{:S(2)}, u32[]{:S(2)}) %collective-permute-start.22) | collective-permute-done | bytes 65568 | tf_op jit(solution)/shard_map/ppermute | solution.py:39
  (90 shorter events, 21.5 us)
Async XLA Ops:
  0.6 54.5 %copy-start = (bf16[1,384,2048]{2,1,0:T(8,128)(2,1)S(1)}, bf16[1,384,2048]{2,1,0:T(8,128)(2,1)}, u32[]{:S(2)}) copy-start(bf16[1,384,2048]{2,1,0:T(8,128)(2,1)} %param.13) | copy-start | bytes 4718596
  0.6 27.2 %copy-start.4 = (bf16[16,2048]{1,0:T(8,128)(2,1)S(1)}, bf16[16,2048]{1,0:T(8,128)(2,1)}, u32[]{:S(2)}) copy-start(bf16[16,2048]{1,0:T(8,128)(2,1)} %param.10) | copy-start | bytes 196612
  0.7 23.6 %copy-start.3 = (bf16[16,2048]{1,0:T(8,128)(2,1)S(1)}, bf16[16,2048]{1,0:T(8,128)(2,1)}, u32[]{:S(2)}) copy-start(bf16[16,2048]{1,0:T(8,128)(2,1)} %param.7) | copy-start | bytes 196612
  0.7 14.2 %collective-permute-start.14 = (bf16[16,2048]{1,0:T(8,128)(2,1)}, bf16[16,2048]{1,0:T(8,128)(2,1)S(1)}, u32[]{:S(2)}, u32[]{:S(2)}) collective-permute-start(bf16[16,2048]{1,0:T(8,128)(2,1)} %param.10), channel_id=1, source_target_pairs={{0,3},{1,0},{2,1},{3,2},{4,7},{5,4},{6,5},{7,6},{8,11},{9,8},{10,9... | collective-permute-start | bytes 196616 | tf_op jit(solution)/shard_map/ppermute | solution.py:39
  5.8 5.7 %collective-permute-start.12 = (bf16[16,2048]{1,0:T(8,128)(2,1)}, bf16[16,2048]{1,0:T(8,128)(2,1)S(1)}, u32[]{:S(2)}, u32[]{:S(2)}) collective-permute-start(bf16[16,2048]{1,0:T(8,128)(2,1)} %param.10), channel_id=1, source_target_pairs={{0,4},{1,5},{2,6},{3,7},{4,0},{5,1},{6,2},{7,3},{8,12},{9,13},{10,... | collective-permute-start | bytes 196616 | tf_op jit(solution)/shard_map/ppermute | solution.py:39
  9.0 4.9 %collective-permute-start = (bf16[16,2176]{1,0:T(8,128)(2,1)S(1)}, bf16[16,2176]{1,0:T(8,128)(2,1)S(1)}, u32[]{:S(2)}, u32[]{:S(2)}) collective-permute-start(bf16[16,2176]{1,0:T(8,128)(2,1)S(1)} %get-tuple-element.24), channel_id=1, source_target_pairs={{0,4},{1,5},{2,6},{3,7},{4,0},{5,1},{6,2},{7,3},{8,12},{9,13},{10,... | collective-permute-start | bytes 208904 | tf_op jit(solution)/shard_map/ppermute | solution.py:39
  9.5 14.8 %collective-permute-start.2 = (bf16[16,2176]{1,0:T(8,128)(2,1)S(1)}, bf16[16,2176]{1,0:T(8,128)(2,1)S(1)}, u32[]{:S(2)}, u32[]{:S(2)}) collective-permute-start(bf16[16,2176]{1,0:T(8,128)(2,1)S(1)} %get-tuple-element.24), channel_id=1, source_target_pairs={{0,3},{1,0},{2,1},{3,2},{4,7},{5,4},{6,5},{7,6},{8,11},{9,8},{10,9... | collective-permute-start | bytes 208904 | tf_op jit(solution)/shard_map/ppermute | solution.py:39
  12.3 8.3 %collective-permute-start.13 = (bf16[32,2048]{1,0:T(8,128)(2,1)S(1)}, bf16[32,2048]{1,0:T(8,128)(2,1)S(1)}, u32[]{:S(2)}, u32[]{:S(2)}) collective-permute-start(bf16[32,2048]{1,0:T(8,128)(2,1)S(1)} %pad_maximum_fusion.5), channel_id=1, source_target_pairs={{0,1},{1,2},{2,3},{3,0},{4,6},{5,7},{6,4},{7,5},{8,9},{9,10},{10,1... | collective-permute-start | bytes 393224 | tf_op jit(solution)/shard_map/ppermute | solution.py:39
  14.8 9.5 %collective-permute-start.1 = (bf16[32,2176]{1,0:T(8,128)(2,1)S(1)}, bf16[32,2176]{1,0:T(8,128)(2,1)S(1)}, u32[]{:S(2)}, u32[]{:S(2)}) collective-permute-start(bf16[32,2176]{1,0:T(8,128)(2,1)S(1)} %pad_maximum_fusion.4), channel_id=1, source_target_pairs={{0,1},{1,2},{2,3},{3,0},{4,6},{5,7},{6,4},{7,5},{8,9},{9,10},{10,1... | collective-permute-start | bytes 417800 | tf_op jit(solution)/shard_map/ppermute | solution.py:39
  21.4 6.4 %collective-permute-start.15 = (bf16[64,2048]{1,0:T(8,128)(2,1)S(1)}, bf16[64,2048]{1,0:T(8,128)(2,1)S(1)}, u32[]{:S(2)}, u32[]{:S(2)}) collective-permute-start(bf16[64,2048]{1,0:T(8,128)(2,1)S(1)} %pad_maximum_fusion.3), channel_id=1, source_target_pairs={{0,8},{1,9},{2,10},{3,11},{4,20},{5,21},{6,22},{7,23},{8,0},{9,1},... | collective-permute-start | bytes 786440 | tf_op jit(solution)/shard_map/ppermute | solution.py:39
  24.3 6.6 %collective-permute-start.3 = (bf16[64,2176]{1,0:T(8,128)(2,1)S(1)}, bf16[64,2176]{1,0:T(8,128)(2,1)S(1)}, u32[]{:S(2)}, u32[]{:S(2)}) collective-permute-start(bf16[64,2176]{1,0:T(8,128)(2,1)S(1)} %pad_maximum_fusion.2), channel_id=1, source_target_pairs={{0,8},{1,9},{2,10},{3,11},{4,20},{5,21},{6,22},{7,23},{8,0},{9,1},... | collective-permute-start | bytes 835592 | tf_op jit(solution)/shard_map/ppermute | solution.py:39
  27.9 9.6 %collective-permute-start.16 = (bf16[128,2048]{1,0:T(8,128)(2,1)S(1)}, bf16[128,2048]{1,0:T(8,128)(2,1)S(1)}, u32[]{:S(2)}, u32[]{:S(2)}) collective-permute-start(bf16[128,2048]{1,0:T(8,128)(2,1)S(1)} %pad_maximum_fusion.1), channel_id=1, source_target_pairs={{0,16},{1,17},{2,18},{3,19},{4,12},{5,13},{6,14},{7,15},{8,24},{9,... | collective-permute-start | bytes 1572872 | tf_op jit(solution)/shard_map/ppermute | solution.py:39
  31.0 12.5 %collective-permute-start.4 = (bf16[128,2176]{1,0:T(8,128)(2,1)S(1)}, bf16[128,2176]{1,0:T(8,128)(2,1)S(1)}, u32[]{:S(2)}, u32[]{:S(2)}) collective-permute-start(bf16[128,2176]{1,0:T(8,128)(2,1)S(1)} %pad_maximum_fusion), channel_id=1, source_target_pairs={{0,16},{1,17},{2,18},{3,19},{4,12},{5,13},{6,14},{7,15},{8,24},{9,... | collective-permute-start | bytes 1671176 | tf_op jit(solution)/shard_map/ppermute | solution.py:39
  38.4 7.3 %copy-start.7 = (bf16[512,2048]{1,0:T(8,128)(2,1)}, bf16[512,2048]{1,0:T(8,128)(2,1)S(1)}, u32[]{:S(2)}) copy-start(bf16[512,2048]{1,0:T(8,128)(2,1)S(1)} %get-tuple-element.11) | copy-start | bytes 6291460
  38.4 7.3 %collective-permute-start.17 = (bf16[256,2048]{1,0:T(8,128)(2,1)}, bf16[256,2048]{1,0:T(8,128)(2,1)}, u32[]{:S(2)}, u32[]{:S(2)}) collective-permute-start(bf16[256,2048]{1,0:T(8,128)(2,1)} %get-tuple-element.10), channel_id=1, source_target_pairs={{0,4},{1,5},{2,6},{3,7},{4,0},{5,1},{6,2},{7,3},{8,12},{9,13},{10,... | collective-permute-start | bytes 3145736 | tf_op jit(solution)/shard_map/ppermute | solution.py:39
  45.7 3.0 %collective-permute-start.5 = (bf16[256,2176]{1,0:T(8,128)(2,1)}, bf16[256,2176]{1,0:T(8,128)(2,1)S(1)}, u32[]{:S(2)}, u32[]{:S(2)}) collective-permute-start(bf16[256,2176]{1,0:T(8,128)(2,1)} %get-tuple-element.8), channel_id=1, source_target_pairs={{0,4},{1,5},{2,6},{3,7},{4,0},{5,1},{6,2},{7,3},{8,12},{9,13},{10,... | collective-permute-start | bytes 3342344 | tf_op jit(solution)/shard_map/ppermute | solution.py:39
  45.7 5.1 %copy-start.2 = (bf16[1,2048,384]{2,1,0:T(8,128)(2,1)S(1)}, bf16[1,2048,384]{2,1,0:T(8,128)(2,1)}, u32[]{:S(2)}) copy-start(bf16[1,2048,384]{2,1,0:T(8,128)(2,1)} %param.12) | copy-start | bytes 4718596
  50.8 3.0 %copy-start.1 = (bf16[1,2048,384]{2,1,0:T(8,128)(2,1)S(1)}, bf16[1,2048,384]{2,1,0:T(8,128)(2,1)}, u32[]{:S(2)}) copy-start(bf16[1,2048,384]{2,1,0:T(8,128)(2,1)} %param.11) | copy-start | bytes 4718596
  50.8 3.0 %copy-start.6 = (bf16[512,2176]{1,0:T(8,128)(2,1)S(1)}, bf16[512,2176]{1,0:T(8,128)(2,1)}, u32[]{:S(2)}) copy-start(bf16[512,2176]{1,0:T(8,128)(2,1)} %constant_dynamic-update-slice_fusion.5) | copy-start | bytes 6684676
  53.9 1.6 %copy-start.8 = (bf16[512,2048]{1,0:T(8,128)(2,1)S(1)}, bf16[512,2048]{1,0:T(8,128)(2,1)}, u32[]{:S(2)}) copy-start(bf16[512,2048]{1,0:T(8,128)(2,1)} %constant_dynamic-update-slice_fusion.16) | copy-start | bytes 6291460
  57.7 5.3 %collective-permute-start.6 = (bf16[256,2048]{1,0:T(8,128)(2,1)S(1)}, bf16[256,2048]{1,0:T(8,128)(2,1)S(1)}, u32[]{:S(2)}, u32[]{:S(2)}) collective-permute-start(bf16[256,2048]{1,0:T(8,128)(2,1)S(1)} %fusion.5), channel_id=1, source_target_pairs={{0,4},{1,5},{2,6},{3,7},{4,0},{5,1},{6,2},{7,3},{8,12},{9,13},{10,... | collective-permute-start | bytes 3145736 | tf_op jit(solution)/shard_map/ppermute | solution.py:39
  59.5 6.0 %collective-permute-start.18 = (bf16[256,2048]{1,0:T(8,128)(2,1)S(1)}, bf16[256,2048]{1,0:T(8,128)(2,1)S(1)}, u32[]{:S(2)}, u32[]{:S(2)}) collective-permute-start(bf16[256,2048]{1,0:T(8,128)(2,1)S(1)} %fusion.8), channel_id=1, source_target_pairs={{0,4},{1,5},{2,6},{3,7},{4,0},{5,1},{6,2},{7,3},{8,12},{9,13},{10,... | collective-permute-start | bytes 3145736 | tf_op jit(solution)/shard_map/ppermute | solution.py:39
  63.9 9.2 %collective-permute-start.7 = (bf16[128,2048]{1,0:T(8,128)(2,1)S(1)}, bf16[128,2048]{1,0:T(8,128)(2,1)S(1)}, u32[]{:S(2)}, u32[]{:S(2)}) collective-permute-start(bf16[128,2048]{1,0:T(8,128)(2,1)S(1)} %slice.119), channel_id=1, source_target_pairs={{0,16},{1,17},{2,18},{3,19},{4,12},{5,13},{6,14},{7,15},{8,24},{9,... | collective-permute-start | bytes 1572872 | tf_op jit(solution)/shard_map/ppermute | solution.py:39
  66.3 15.2 %collective-permute-start.19 = (bf16[128,2048]{1,0:T(8,128)(2,1)S(1)}, bf16[128,2048]{1,0:T(8,128)(2,1)S(1)}, u32[]{:S(2)}, u32[]{:S(2)}) collective-permute-start(bf16[128,2048]{1,0:T(8,128)(2,1)S(1)} %slice.132), channel_id=1, source_target_pairs={{0,16},{1,17},{2,18},{3,19},{4,12},{5,13},{6,14},{7,15},{8,24},{9,... | collective-permute-start | bytes 1572872 | tf_op jit(solution)/shard_map/ppermute | solution.py:39
  73.3 10.0 %collective-permute-start.8 = (bf16[64,2048]{1,0:T(8,128)(2,1)S(1)}, bf16[64,2048]{1,0:T(8,128)(2,1)S(1)}, u32[]{:S(2)}, u32[]{:S(2)}) collective-permute-start(bf16[64,2048]{1,0:T(8,128)(2,1)S(1)} %slice.121), channel_id=1, source_target_pairs={{0,8},{1,9},{2,10},{3,11},{4,20},{5,21},{6,22},{7,23},{8,0},{9,1},... | collective-permute-start | bytes 786440 | tf_op jit(solution)/shard_map/ppermute | solution.py:39
  81.7 6.4 %collective-permute-start.20 = (bf16[64,2048]{1,0:T(8,128)(2,1)S(1)}, bf16[64,2048]{1,0:T(8,128)(2,1)S(1)}, u32[]{:S(2)}, u32[]{:S(2)}) collective-permute-start(bf16[64,2048]{1,0:T(8,128)(2,1)S(1)} %slice.134), channel_id=1, source_target_pairs={{0,8},{1,9},{2,10},{3,11},{4,20},{5,21},{6,22},{7,23},{8,0},{9,1},... | collective-permute-start | bytes 786440 | tf_op jit(solution)/shard_map/ppermute | solution.py:39
  83.4 12.7 %collective-permute-start.10 = (bf16[16,2048]{1,0:T(8,128)(2,1)S(1)}, bf16[16,2048]{1,0:T(8,128)(2,1)S(1)}, u32[]{:S(2)}, u32[]{:S(2)}) collective-permute-start(bf16[16,2048]{1,0:T(8,128)(2,1)S(1)} %slice.125), channel_id=1, source_target_pairs={{0,1},{1,2},{2,3},{3,0},{4,5},{5,6},{6,7},{7,4},{8,9},{9,10},{10,1... | collective-permute-start | bytes 196616 | tf_op jit(solution)/shard_map/ppermute | solution.py:39
  83.5 6.3 %collective-permute-start.9 = (bf16[32,2048]{1,0:T(8,128)(2,1)S(1)}, bf16[32,2048]{1,0:T(8,128)(2,1)S(1)}, u32[]{:S(2)}, u32[]{:S(2)}) collective-permute-start(bf16[32,2048]{1,0:T(8,128)(2,1)S(1)} %slice.123), channel_id=1, source_target_pairs={{0,3},{1,0},{2,1},{3,2},{4,6},{5,7},{6,4},{7,5},{8,11},{9,8},{10,9... | collective-permute-start | bytes 393224 | tf_op jit(solution)/shard_map/ppermute | solution.py:39
  88.3 7.5 %collective-permute-start.21 = (bf16[32,2048]{1,0:T(8,128)(2,1)S(1)}, bf16[32,2048]{1,0:T(8,128)(2,1)S(1)}, u32[]{:S(2)}, u32[]{:S(2)}) collective-permute-start(bf16[32,2048]{1,0:T(8,128)(2,1)S(1)} %slice.136), channel_id=1, source_target_pairs={{0,3},{1,0},{2,1},{3,2},{4,6},{5,7},{6,4},{7,5},{8,11},{9,8},{10,9... | collective-permute-start | bytes 393224 | tf_op jit(solution)/shard_map/ppermute | solution.py:39
  89.8 6.3 %collective-permute-start.11 = (f32[16,2048]{1,0:T(8,128)S(1)}, f32[16,2048]{1,0:T(8,128)S(1)}, u32[]{:S(2)}, u32[]{:S(2)}) collective-permute-start(f32[16,2048]{1,0:T(8,128)S(1)} %slice.126), channel_id=1, source_target_pairs={{0,4},{1,5},{2,6},{3,7},{4,0},{5,1},{6,2},{7,3},{8,12},{9,13},{10,... | collective-permute-start | bytes 393224 | tf_op jit(solution)/shard_map/ppermute | solution.py:39
  93.0 6.3 %collective-permute-start.22 = (bf16[16,2048]{1,0:T(8,128)(2,1)S(1)}, bf16[16,2048]{1,0:T(8,128)(2,1)S(1)}, u32[]{:S(2)}, u32[]{:S(2)}) collective-permute-start(bf16[16,2048]{1,0:T(8,128)(2,1)S(1)} %slice.138), channel_id=1, source_target_pairs={{0,1},{1,2},{2,3},{3,0},{4,5},{5,6},{6,7},{7,4},{8,9},{9,10},{10,1... | collective-permute-start | bytes 196616 | tf_op jit(solution)/shard_map/ppermute | solution.py:39
  95.7 3.5 %collective-permute-start.23 = (f32[16,2048]{1,0:T(8,128)S(1)}, f32[16,2048]{1,0:T(8,128)S(1)}, u32[]{:S(2)}, u32[]{:S(2)}) collective-permute-start(f32[16,2048]{1,0:T(8,128)S(1)} %slice.139), channel_id=1, source_target_pairs={{0,4},{1,5},{2,6},{3,7},{4,0},{5,1},{6,2},{7,3},{8,12},{9,13},{10,... | collective-permute-start | bytes 393224 | tf_op jit(solution)/shard_map/ppermute | solution.py:39
  (1 other events, 1.4 us)

commit v2 on v1

v2 whole, which is shorter than its diff:
```python
import functools

import jax
import jax.numpy as jnp
from jax import lax
from jax.experimental import pallas as pl
from jax.experimental.pallas import tpu as pltpu
from jax.sharding import PartitionSpec as P

AXES = ("dp", "expert")
F32, BF16 = jnp.float32, jnp.bfloat16
BLOCK = 128


def permutes(n_dp, n_ex):
    def pairs(to):
        out = []
        for d in range(n_dp):
            for z in range(n_ex):
                e, y = to(d, z)
                out.append((d * n_ex + z, e * n_ex + y))
        return out

    def mixed(step, bits):
        def to(d, z):
            bit = step if d % 2 == 0 else bits - 1 - step
            return d ^ (2 << bit), z

        return pairs(to)

    bits = n_dp.bit_length() - 2
    core = pairs(lambda d, z: (d ^ 1, z))
    plane = [mixed(s, bits) for s in range(bits)]
    line = [pairs(lambda d, z, j=j: (d, (z + j) % n_ex)) for j in range(1, n_ex)]
    back = [pairs(lambda d, z, j=j: (d, (z - j) % n_ex)) for j in range(1, n_ex)]
    return core, plane, line, back


def send(x, pairs):
    return lax.ppermute(x, AXES, pairs)


def after(x, *others):
    return lax.optimization_barrier((x, *others))[0]


def add(*terms):
    return functools.reduce(lambda a, b: a + b, [t.astype(F32) for t in terms])


def nt(left, right):
    return lax.dot_general(left, right, (((1,), (1,)), ((), ())), preferred_element_type=F32)


def tn(left, right):
    return lax.dot_general(left, right, (((0,), (0,)), ((), ())), preferred_element_type=F32)


def dot(left, right):
    return jnp.dot(left, right, preferred_element_type=F32)


def shaped(*arrays):
    return [jax.ShapeDtypeStruct(s, t) for s, t in arrays]


def params(mib):
    return pltpu.CompilerParams(vmem_limit_bytes=mib << 20)


def cost(microseconds):
    return pl.CostEstimate(flops=int(microseconds * 1.15e9), bytes_accessed=0, transcendentals=0)


WHOLE = pl.BlockSpec(memory_space=pltpu.VMEM)
ANY = pl.BlockSpec(memory_space=pltpu.HBM)


def payload_kernel(experts, tokens, cotangent, route_in, probs_in, out, cot, route, probs, sems):
    rows, width = tokens.shape
    copies = [
        pltpu.make_async_copy(a, b, sems.at[i])
        for i, (a, b) in enumerate(
            ((route_in, route), (probs_in, probs), (tokens, out.at[:, :width]), (cotangent, cot))
        )
    ]
    for copy in copies:
        copy.start()
    for copy in copies[:2]:
        copy.wait()
    extra = out.shape[1] - width
    column = lax.broadcasted_iota(jnp.int32, (extra, rows), 0)
    named, part = column, jnp.zeros_like(column)
    for _ in range(2):
        over = named >= experts
        named, part = jnp.where(over, named - experts, named), part + over.astype(jnp.int32)
    table = jnp.zeros((extra, rows), F32)
    for k in range(route.shape[0]):
        table = table + jnp.where(route[k : k + 1, :] == named, probs[k : k + 1, :], 0.0)
    high = table.astype(BF16).astype(F32)
    middle = (table - high).astype(BF16).astype(F32)
    low = table - high - middle
    table = jnp.where(part == 0, high, jnp.where(part == 1, middle, low))
    out[:, width:] = jnp.transpose(table).astype(BF16)
    for copy in copies[2:]:
        copy.wait()


def payload(tokens, cotangent, route, probs, experts):
    rows, width = tokens.shape
    extra = -(-3 * experts // 128) * 128
    return pl.pallas_call(
        functools.partial(payload_kernel, experts),
        in_specs=[ANY] * 4,
        out_specs=[WHOLE] * 2,
        out_shape=[pltpu.VMEM((rows, width + extra), BF16), pltpu.VMEM((rows, width), BF16)],
        scratch_shapes=[
            pltpu.VMEM(route.shape[::-1], jnp.int32),
            pltpu.VMEM(probs.shape[::-1], F32),
            pltpu.SemaphoreType.DMA((4,)),
        ],
        compiler_params=params(60),
    )(tokens, cotangent, route.T, probs.T)


def stage_kernel(*refs):
    count = len(refs) // 2
    copies = [pltpu.make_async_copy(refs[i], refs[count + i], refs[-1].at[i]) for i in range(count)]
    for copy in copies:
        copy.start()
    for copy in copies:
        copy.wait()


def stage(*arrays):
    return pl.pallas_call(
        stage_kernel,
        in_specs=[ANY] * len(arrays),
        out_specs=[WHOLE] * len(arrays),
        out_shape=[pltpu.VMEM(a.shape, a.dtype) for a in arrays],
        scratch_shapes=[pltpu.SemaphoreType.DMA((len(arrays),))],
        compiler_params=params(50),
    )(*arrays)


def join_kernel(*refs):
    at = 0
    for ref in refs[:-1]:
        refs[-1][at : at + ref.shape[0], :] = ref[...]
        at += ref.shape[0]


def join(*arrays, length=0.0):
    rows = sum(a.shape[0] for a in arrays)
    return pl.pallas_call(
        join_kernel,
        in_specs=[WHOLE] * len(arrays),
        out_specs=WHOLE,
        out_shape=pltpu.VMEM((rows, arrays[0].shape[1]), BF16),
        compiler_params=params(4),
        cost_estimate=cost(length),
    )(*arrays)


def grid_specs(block, arrays, whole):
    specs = [pl.BlockSpec((block * f, w), lambda i: (i, 0)) for f, w in arrays]
    return specs + [pl.BlockSpec(w.shape, lambda i: (0, 0, 0)) for w in whole]


def over_rows(kernel, n, scalars, taken, weights, given, length=0.0):
    block = min(n, BLOCK)
    if block == n:
        call = dict(in_specs=[WHOLE] * (len(taken) + len(weights)), out_specs=[WHOLE] * len(given))
    else:
        call = dict(
            grid=(n // block,),
            in_specs=grid_specs(block, [(f, a.shape[1]) for f, a in taken], weights),
            out_specs=grid_specs(block, [(f, w) for f, w, _ in given], []),
        )
    call["in_specs"] = [pl.BlockSpec(memory_space=pltpu.SMEM)] * len(scalars) + call["in_specs"]
    return pl.pallas_call(
        kernel,
        out_shape=shaped(*[((f * n, w), t) for f, w, t in given]),
        compiler_params=params(12 if block == n else 40),
        cost_estimate=cost(length),
        **call,
    )(*scalars, *[a for _, a in taken], *weights)


def expert_weight(experts, expert, table):
    column = lax.broadcasted_iota(jnp.int32, table.shape, 1)
    mine = expert[0, 0]
    mine = (column == mine) | (column == mine + experts) | (column == mine + 2 * experts)
    return jnp.sum(jnp.where(mine, table.astype(F32), 0.0), axis=1, keepdims=True)


def hidden_units(x, w_gate, w_up, act, gate_f, up_f):
    gate, up = dot(x, w_gate[0]), dot(x, w_up[0])
    s = jax.nn.sigmoid(gate)
    gate_s = gate * s
    act_val = (gate_s * up).astype(BF16)
    act[...] = act_val
    up_f[...] = gate_s
    gate_f[...] = up * s * (1.0 + gate * (1.0 - s))
    return act_val


def forward_pair_kernel(experts, expert, a, b, w_gate, w_up, w_down, kept, given, act, gate_f, up_f, weight):
    n, width = a.shape[0], w_gate.shape[1]
    x = jnp.concatenate((a[:, :width], b[:, :width]))
    p = expert_weight(experts, expert, jnp.concatenate((a[:, width:], b[:, width:])))
    weight[...] = jnp.broadcast_to(p, weight.shape)
    act_val = hidden_units(x, w_gate, w_up, act, gate_f, up_f)
    out = p * dot(act_val, w_down[0])
    kept[...] = out[:n].astype(BF16)
    given[...] = out[n:].astype(BF16)


def forward_pair(a, b, weights, expert, experts, length=0.0):
    width, hidden = weights[0].shape[1:]
    given = [(1, width, BF16)] * 2 + [(2, hidden, BF16), (2, hidden, F32), (2, hidden, F32), (2, 128, F32)]
    kernel = functools.partial(forward_pair_kernel, experts)
    return over_rows(kernel, a.shape[0], [expert], [(1, a), (1, b)], weights, given, length)


def forward_hidden_kernel(experts, expert, a, w_gate, w_up, act, gate_f, up_f, weight):
    width = w_gate.shape[1]
    weight[...] = jnp.broadcast_to(expert_weight(experts, expert, a[:, width:]), weight.shape)
    hidden_units(a[:, :width], w_gate, w_up, act, gate_f, up_f)


def forward_out_kernel(act, weight, w_down, out):
    out[...] = (weight[:, :1] * dot(act[...], w_down[0])).astype(BF16)


def forward_full_kernel(experts, expert, a, w_gate, w_up, w_down, act, gate_f, up_f, weight, out):
    width = w_gate.shape[1]
    p = expert_weight(experts, expert, a[:, width:])
    weight[...] = jnp.broadcast_to(p, weight.shape)
    act_val = hidden_units(a[:, :width], w_gate, w_up, act, gate_f, up_f)
    out[...] = (p * dot(act_val, w_down[0])).astype(BF16)


def forward_one(kernel, a, weights, expert, experts, outs, length=0.0):
    width, hidden = weights[0].shape[1:]
    given = [(1, hidden, BF16), (1, hidden, F32), (1, hidden, F32), (1, 128, F32)] + [(1, width, BF16)] * outs
    return over_rows(functools.partial(kernel, experts), a.shape[0], [expert], [(1, a)], weights, given, length)


def hidden_cots(cot, weight, gate_f, up_f, w_down, gate_cot, up_cot, out_cot):
    out = (cot.astype(F32) * weight[:, :1]).astype(BF16)
    out_cot[...] = out
    act_cot = nt(out, w_down[0])
    gate = (act_cot * gate_f[...]).astype(BF16)
    up = (act_cot * up_f[...]).astype(BF16)
    gate_cot[...], up_cot[...] = gate, up
    return gate, up


def row_cots(gate, up, w_gate, w_up):
    return nt(gate, w_gate[0]) + nt(up, w_up[0])


def backward_pair_kernel(a, b, weight, gate_f, up_f, w_gate, w_up, w_down, kept, given, gate_cot, up_cot, out_cot):
    n = a.shape[0]
    cot = jnp.concatenate((a[...], b[...]))
    gate, up = hidden_cots(cot, weight, gate_f, up_f, w_down, gate_cot, up_cot, out_cot)
    part = row_cots(gate, up, w_gate, w_up)
    kept[...] = part[:n].astype(BF16)
    given[...] = part[n:].astype(BF16)


def backward_pair(a, b, weight, gate_f, up_f, weights, length=0.0):
    n, width = a.shape
    hidden = weights[0].shape[2]
    taken = [(1, a), (1, b), (2, weight), (2, gate_f), (2, up_f)]
    given = [(1, width, BF16)] * 2 + [(2, hidden, BF16)] * 2 + [(2, width, BF16)]
    return over_rows(backward_pair_kernel, n, [], taken, weights, given, length)


def backward_hidden_kernel(cot, weight, gate_f, up_f, w_down, gate_cot, up_cot, out_cot):
    hidden_cots(cot[...], weight, gate_f, up_f, w_down, gate_cot, up_cot, out_cot)


def backward_rows_kernel(gate, up, w_gate, w_up, out):
    out[...] = row_cots(gate[...], up[...], w_gate, w_up).astype(BF16)


def backward_full_kernel(cot, weight, gate_f, up_f, w_gate, w_up, w_down, gate_cot, up_cot, out_cot, out):
    gate, up = hidden_cots(cot[...], weight, gate_f, up_f, w_down, gate_cot, up_cot, out_cot)
    out[...] = row_cots(gate, up, w_gate, w_up).astype(BF16)


def backward_one(kernel, cot, weight, gate_f, up_f, weights, outs, length=0.0):
    n, width = cot.shape
    hidden = gate_f.shape[1]
    taken = [(1, cot), (1, weight), (1, gate_f), (1, up_f)]
    given = [(1, hidden, BF16)] * 2 + [(1, width, BF16)] * (1 + outs)
    return over_rows(kernel, n, [], taken, weights, given, length)


def gradient_kernel(width, counts, *refs):
    joined = []
    for count in counts:
        joined.append(jnp.concatenate([r[...] for r in refs[:count]]))
        refs = refs[count:]
    outs, total = refs[:-1], refs[-1]
    part = tn(joined[0][:, :width], jnp.concatenate(joined[1:], axis=1))

    def write(value):
        hidden = value.shape[1] // len(outs)
        for i, out in enumerate(outs):
            out[0] = value[:, i * hidden : (i + 1) * hidden].astype(BF16)

    if total.shape[0] == 8:
        write(part)
        return
    step = pl.program_id(0)

    @pl.when(step == 0)
    def _():
        total[...] = part

    @pl.when(step > 0)
    def _():
        total[...] += part

    @pl.when(step == pl.num_programs(0) - 1)
    def _():
        write(total[...])


def gradients(left, rights, width, steps):
    hidden = rights[0][0].shape[1]
    groups = [left, *rights]
    flat = [piece for group in groups for piece in group]
    if steps == 1:
        specs = [WHOLE] * len(flat)
    else:
        specs = [pl.BlockSpec((a.shape[0] // steps, a.shape[1]), lambda i: (i, 0)) for a in flat]
    total = (8, 128) if steps == 1 else (width, len(rights) * hidden)
    return pl.pallas_call(
        functools.partial(gradient_kernel, width, [len(g) for g in groups]),
        grid=(steps,),
        in_specs=specs,
        out_specs=[pl.BlockSpec((1, width, hidden), lambda i: (0, 0, 0))] * len(rights),
        out_shape=shaped(*[((1, width, hidden), BF16)] * len(rights)),
        scratch_shapes=[pltpu.VMEM(total, F32)],
        compiler_params=params(24 if steps == 1 else 48),
        cost_estimate=cost(10.0),
    )(*flat)


def body(tokens, route, probs, cotangent, gate_weight, up_weight, down_weight):
    n_dp, n_ex = lax.axis_size("dp"), lax.axis_size("expert")
    experts = n_dp * n_ex // 2
    rows, width = tokens.shape
    core, plane, line, back = permutes(n_dp, n_ex)
    expert = lax.shift_right_logical(lax.axis_index(AXES).astype(jnp.int32), 1).reshape(1, 1)
    expert, tokens = lax.optimization_barrier((expert, tokens))

    own, cot = payload(tokens, cotangent, route, probs, experts)
    row_lane = join(own, *[send(own, p) for p in line])
    weights = (gate_weight, up_weight, down_weight)
    if row_lane.shape[0] * 2 <= BLOCK:
        weights = stage(*(after(w, row_lane) for w in weights))
    w_gate, w_up, w_down = weights
    cot_lane = join(after(cot, w_gate), *[send(cot, p) for p in line], length=10.0)
    for p in plane[:-2]:
        row_lane = join(row_lane, send(row_lane, p))
        cot_lane = join(cot_lane, send(cot_lane, p))
    row_lane = join(row_lane, after(send(row_lane, plane[-2]), cot_lane))
    row_late = send(row_lane, plane[-1])
    row_other = send(row_lane, core)
    f_early = forward_pair(row_lane, row_other, weights, expert, experts, 10.0)
    cot_lane = join(cot_lane, after(send(cot_lane, plane[-2]), f_early[0]))
    cot_late = send(cot_lane, plane[-1])
    cot_other = send(cot_lane, core)

    def halve(kept, received):
        return add(kept, received).astype(BF16)

    row_late = after(row_late, cot_lane)
    row_late_other = send(row_late, core)
    f_own = forward_one(forward_hidden_kernel, row_late, (w_gate, w_up), expert, experts, 0, 10.0)
    f_other = forward_one(forward_full_kernel, row_late_other, weights, expert, experts, 1, 10.0)
    o_other = send(f_other[4], core)
    (o_own,) = over_rows(
        forward_out_kernel, row_late.shape[0], [], [(1, f_own[0]), (1, after(f_own[3], f_other[0]))], (w_down,), [(1, width, BF16)], 10.0
    )
    o_late = halve(o_own, o_other)
    o_early_other = send(f_early[1], core)
    o_back = send(o_late, plane[-1])

    cot_late = after(cot_late, o_late)
    cot_late_other = send(cot_late, core)
    b_own = backward_one(backward_hidden_kernel, cot_late, f_own[3], f_own[1], f_own[2], (w_down,), 0, 10.0)
    b_other = backward_one(
        backward_full_kernel, cot_late_other, f_other[3], f_other[1], f_other[2], weights, 1, 10.0
    )
    g_other = send(b_other[3], core)
    (g_own,) = over_rows(
        backward_rows_kernel, cot_late.shape[0], [], [(1, b_own[0]), (1, after(b_own[1], b_other[0]))], (w_gate, w_up), [(1, width, BF16)], 10.0
    )
    g_late = halve(g_own, g_other)
    cot_other = after(cot_other, g_late)
    b_early = backward_pair(cot_lane, cot_other, f_early[5], f_early[3], f_early[4], weights, 10.0)
    g_early_other = send(b_early[1], core)
    g_back = send(g_late, plane[-1])
    o_back = after(o_back, g_late)

    def finish(lane):
        for p in reversed(plane[:-1]):
            half = lane.shape[0] // 2
            lane = halve(lane[:half], send(lane[half:], p))
        terms = [lane[:rows]]
        for j, p in enumerate(back, 1):
            terms.append(send(lane[j * rows : (j + 1) * rows], p))
        return add(*terms).astype(BF16)

    mixed = finish(add(f_early[0], o_early_other, o_back).astype(BF16))
    token_grad = finish(add(b_early[0], g_early_other, g_back).astype(BF16))

    steps = max(1, row_late.shape[0] // BLOCK)
    lefts = [after(row_lane, g_late), row_other, row_late, row_late_other]
    gate_cots, up_cots, out_cots = zip(b_early[2:5], b_own[:3], b_other[:3])
    gate_grad, up_grad = gradients(lefts, [gate_cots, up_cots], width, steps)
    (down_grad,) = gradients([after(f_early[2], g_late), f_own[0], f_other[0]], [out_cots], f_own[0].shape[1], steps)
    return mixed, token_grad, gate_grad, up_grad, down_grad


def solution(mesh):
    two, three = P(AXES, None), P(AXES, None, None)
    return jax.shard_map(
        body,
        mesh=mesh,
        in_specs=(two, two, two, two, three, three, three),
        out_specs=(two, two, three, three, three),
        check_vma=False,
    )
```

time: 100 us -> 76 us (0.76)
  Pallas kernels: 0 us -> 18.8 us
  matrix products: 17.4 us -> 0 us
  waiting for transfers between devices: 33.2 us -> 17.7 us
  local copies, waits for them, and re-layouts: 14.4 us -> 0.07 us
  starting transfers between devices: 26.8 us -> 36.2 us
  other arithmetic: 7.12 us -> 2.22 us
    pallas_call x0 -> x16, Pallas kernels: none -> 18.8 us  [the longest x8 9.66 us: over_rows(): pl.pallas_call(kernel, out_shape=shaped(*[((f * n, w), t) for f, w, t in...]
    dot_general x12 -> x0, matrix products: 17.4 us -> none  [the longest x3 7.13 us: contract_first(): lax.dot_general(left, right, (((0,), (0,)), ((), ())), preferred_element_...]
    ppermute x24 -> x28, waiting for transfers between devices: 33.2 us -> 17.7 us  [send(): return lax.ppermute(x, AXES, pairs)]
    ppermute x24 -> x28, starting transfers between devices: 26.8 us -> 36.2 us  [send(): return lax.ppermute(x, AXES, pairs)]
    unnamed x27 -> x0, local copies, waits for them, and re-layouts: 8.85 us -> none
    concatenate x4 -> x0, local copies, waits for them, and re-layouts: 5.33 us -> none  [the longest x1 2.43 us: body(): all_cot = jnp.concatenate((lane_cot, send(lane_cot, core)))]
    concatenate x7 -> x0, other arithmetic: 2.75 us -> none  [the longest x2 1.7 us: gather_lane(): chip = jnp.concatenate((own, send(own, core)))]
    unnamed x1 -> x0, other arithmetic: 1.49 us -> none
  transfers between devices with their start and end apart: 24 -> 28, of which waited for: 11 -> 15; matrix products, arithmetic and copies ran while one was open for 28% -> 2% of each run, Pallas kernels for 0% -> 23%
where the time goes in v2:
time: 76 us; the launch traced here: 75.8 us
  starting transfers between devices  36.2 us (48%)
  Pallas kernels  18.8 us (25%)
  waiting for transfers between devices  17.7 us (23%)
  other arithmetic  2.22 us (3%)
  between operations  0.84 us (1%)
    ppermute x28, starting transfers between devices, send(): return lax.ppermute(x, AXES, pairs)  36.2 us
    ppermute x28, waiting for transfers between devices, send(): return lax.ppermute(x, AXES, pairs)  17.7 us
    pallas_call x8, Pallas kernels, over_rows(): pl.pallas_call(kernel, out_shape=shaped(*[((f * n, w), t) for f, w, t in...  9.66 us
    pallas_call x2, Pallas kernels, gradients(): pl.pallas_call(functools.partial(gradient_kernel, width, [len(g) for g in...  5.66 us
    pallas_call x1, Pallas kernels, stage(): pl.pallas_call(stage_kernel, in_specs=[ANY] * len(arrays), out_specs=[WHO...  2.38 us
  transfers between devices with their start and end apart: 28, of which 15 were waited for; matrix products, arithmetic and copies ran while one was open for 2% of the time, Pallas kernels for 23%

profile of v2, /device:TPU:0, one launch (start us, length us, event | category | flops | bytes accessed | tf_op | source)
XLA Modules:
  0.0 75.8 jit_solution(4756108844820322757)
XLA Ops:
  1.6 3.1 %collective-permute-start = (bf16[16,2176]{1,0:T(8,128)(2,1)S(1)}, bf16[16,2176]{1,0:T(8,128)(2,1)S(1)}, u32[]{:S(2)}, u32[]{:S(2)}) collective-permute-start(bf16[16,2176]{1,0:T(8,128)(2,1)S(1)} %get-tuple-element.57.refs_0_), channel_id=1, source_target_pairs={{0,1},{1,2},{2,3},{3,0},{4,5},{5,6},{6,7},{7,4},{8,9},{9,10},{10,1... | collective-permute-start | bytes 208904 | tf_op jit(solution)/shard_map/ppermute | solution.py:40
  4.7 2.6 %collective-permute-start.1 = (bf16[16,2176]{1,0:T(8,128)(2,1)S(1)}, bf16[16,2176]{1,0:T(8,128)(2,1)S(1)}, u32[]{:S(2)}, u32[]{:S(2)}) collective-permute-start(bf16[16,2176]{1,0:T(8,128)(2,1)S(1)} %get-tuple-element.57.refs_0_), channel_id=1, source_target_pairs={{0,2},{1,3},{2,0},{3,1},{4,6},{5,7},{6,4},{7,5},{8,10},{9,11},{10,... | collective-permute-start | bytes 208904 | tf_op jit(solution)/shard_map/ppermute | solution.py:40
  7.3 1.3 %collective-permute-start.2 = (bf16[16,2176]{1,0:T(8,128)(2,1)S(1)}, bf16[16,2176]{1,0:T(8,128)(2,1)S(1)}, u32[]{:S(2)}, u32[]{:S(2)}) collective-permute-start(bf16[16,2176]{1,0:T(8,128)(2,1)S(1)} %get-tuple-element.57.refs_0_), channel_id=1, source_target_pairs={{0,3},{1,0},{2,1},{3,2},{4,7},{5,4},{6,5},{7,6},{8,11},{9,8},{10,9... | collective-permute-start | bytes 208904 | tf_op jit(solution)/shard_map/ppermute | solution.py:40
  9.6 2.8 %collective-permute-start.6 = (bf16[16,2048]{1,0:T(8,128)(2,1)S(1)}, bf16[16,2048]{1,0:T(8,128)(2,1)S(1)}, u32[]{:S(2)}, u32[]{:S(2)}) collective-permute-start(bf16[16,2048]{1,0:T(8,128)(2,1)S(1)} %get-tuple-element.63.refs_0_), channel_id=1, source_target_pairs={{0,3},{1,0},{2,1},{3,2},{4,7},{5,4},{6,5},{7,6},{8,11},{9,8},{10,9... | collective-permute-start | bytes 196616 | tf_op jit(solution)/shard_map/ppermute | solution.py:40
  12.6 1.4 %collective-permute-start.3 = (bf16[64,2176]{1,0:T(8,128)(2,1)S(1)}, bf16[64,2176]{1,0:T(8,128)(2,1)S(1)}, u32[]{:S(2)}, u32[]{:S(2)}) collective-permute-start(bf16[64,2176]{1,0:T(8,128)(2,1)S(1)} %shard_map.111.refs_0_), channel_id=1, source_target_pairs={{0,8},{1,9},{2,10},{3,11},{4,20},{5,21},{6,22},{7,23},{8,0},{9,1},... | collective-permute-start | bytes 835592 | tf_op jit(solution)/shard_map/ppermute | solution.py:40
  14.0 2.4 %shard_map.112 = (bf16[1,2048,384]{2,1,0:T(8,128)(2,1)S(1)}, bf16[1,2048,384]{2,1,0:T(8,128)(2,1)S(1)}, bf16[1,384,2048]{2,1,0:T(8,128)(2,1)S(1)}) custom-call(bf16[1,2048,384]{2,1,0:T(8,128)(2,1)} %refs_0_, bf16[1,2048,384]{2,1,0:T(8,128)(2,1)} %refs_1_, bf16[1,384,2048]{2,1,0:T(8,128)(2,1)} %refs_2_), custom_call_target="tpu_custom_call" | custom-call | tf_op jit(solution)/shard_map/pallas_call | solution.py:136
  16.4 1.2 %collective-permute-done.5.refs_2_ = bf16[16,2048]{1,0:T(8,128)(2,1)S(1)} collective-permute-done((bf16[16,2048]{1,0:T(8,128)(2,1)S(1)}, bf16[16,2048]{1,0:T(8,128)(2,1)S(1)}, u32[]{:S(2)}, u32[]{:S(2)}) %collective-permute-start.5) | collective-permute-done | bytes 65568 | tf_op jit(solution)/shard_map/ppermute | solution.py:40
  17.7 1.5 %collective-permute-done.3.refs_1_ = bf16[64,2176]{1,0:T(8,128)(2,1)S(1)} collective-permute-done((bf16[64,2176]{1,0:T(8,128)(2,1)S(1)}, bf16[64,2176]{1,0:T(8,128)(2,1)S(1)}, u32[]{:S(2)}, u32[]{:S(2)}) %collective-permute-start.3) | collective-permute-done | bytes 278560 | tf_op jit(solution)/shard_map/ppermute | solution.py:40
  19.4 1.4 %collective-permute-start.10 = (bf16[64,2048]{1,0:T(8,128)(2,1)S(1)}, bf16[64,2048]{1,0:T(8,128)(2,1)S(1)}, u32[]{:S(2)}, u32[]{:S(2)}) collective-permute-start(bf16[64,2048]{1,0:T(8,128)(2,1)S(1)} %shard_map.113.refs_0_), channel_id=1, source_target_pairs={{0,8},{1,9},{2,10},{3,11},{4,20},{5,21},{6,22},{7,23},{8,0},{9,1},... | collective-permute-start | bytes 786440 | tf_op jit(solution)/shard_map/ppermute | solution.py:40
  20.8 1.5 %collective-permute-start.9 = (bf16[128,2176]{1,0:T(8,128)(2,1)S(1)}, bf16[128,2176]{1,0:T(8,128)(2,1)S(1)}, u32[]{:S(2)}, u32[]{:S(2)}) collective-permute-start(bf16[128,2176]{1,0:T(8,128)(2,1)S(1)} %shard_map.114.a.refs_0_), channel_id=1, source_target_pairs={{0,16},{1,17},{2,18},{3,19},{4,12},{5,13},{6,14},{7,15},{8,24},{9,... | collective-permute-start | bytes 1671176 | tf_op jit(solution)/shard_map/ppermute | solution.py:40
  22.3 1.9 %shard_map.115 = (bf16[128,2048]{1,0:T(8,128)(2,1)S(1)}, bf16[128,2048]{1,0:T(8,128)(2,1)S(1)}, bf16[256,384]{1,0:T(8,128)(2,1)S(1)}, f32[256,384]{1,0:T(8,128)S...) custom-call(s32[1,1]{1,0:T(1,128)} %bitcast.expert, bf16[128,2176]{1,0:T(8,128)(2,1)S(1)} %shard_map.114.a.refs_0_, ...), custom_call_target="tpu_custom_call" | custom-call | flops 11500000256 | tf_op jit(solution)/shard_map/pallas_call | solution.py:181
  24.2 3.9 %collective-permute-done.10.refs_1_ = bf16[64,2048]{1,0:T(8,128)(2,1)S(1)} collective-permute-done((bf16[64,2048]{1,0:T(8,128)(2,1)S(1)}, bf16[64,2048]{1,0:T(8,128)(2,1)S(1)}, u32[]{:S(2)}, u32[]{:S(2)}) %collective-permute-start.10) | collective-permute-done | bytes 262176 | tf_op jit(solution)/shard_map/ppermute | solution.py:40
  28.1 1.9 %collective-permute-start.14 = (bf16[128,2048]{1,0:T(8,128)(2,1)S(1)}, bf16[128,2048]{1,0:T(8,128)(2,1)S(1)}, u32[]{:S(2)}, u32[]{:S(2)}) collective-permute-start(bf16[128,2048]{1,0:T(8,128)(2,1)S(1)} %shard_map.116.a), channel_id=1, source_target_pairs={{0,16},{1,17},{2,18},{3,19},{4,12},{5,13},{6,14},{7,15},{8,24},{9,... | collective-permute-start | bytes 1572872 | tf_op jit(solution)/shard_map/ppermute | solution.py:40
  30.1 1.1 %collective-permute-done.9.a.refs_2_ = bf16[128,2176]{1,0:T(8,128)(2,1)S(1)} collective-permute-done((bf16[128,2176]{1,0:T(8,128)(2,1)S(1)}, bf16[128,2176]{1,0:T(8,128)(2,1)S(1)}, u32[]{:S(2)}, u32[]{:S(2)}) %collective-permute-start.9) | collective-permute-done | bytes 557088 | tf_op jit(solution)/shard_map/ppermute | solution.py:40
  33.2 1.1 %shard_map.118 = (bf16[128,384]{1,0:T(8,128)(2,1)S(1)}, f32[128,384]{1,0:T(8,128)S(1)}, f32[128,384]{1,0:T(8,128)S(1)}, f32[128,128]{1,0:T(8,128)S(1)}, bf16[128,2048]{1,0:T(8,128)(2,1)S(1)}) custom-call(s32[1,1]{1,0:T(1,128)} %bitcast.expert, bf16[128,2176]{1,0:T(8,128)(2,1)S(1)} %collective-permute-done.11.a.refs_3_, ...), custom_call_target="tpu_custom_call" | custom-call | flops 11500000256 | tf_op jit(solution)/shard_map/pallas_call | solution.py:181
  35.1 1.1 %collective-permute-done.12 = bf16[128,2048]{1,0:T(8,128)(2,1)S(1)} collective-permute-done((bf16[128,2048]{1,0:T(8,128)(2,1)S(1)}, bf16[128,2048]{1,0:T(8,128)(2,1)S(1)}, u32[]{:S(2)}, u32[]{:S(2)}) %collective-permute-start.12) | collective-permute-done | bytes 524320 | tf_op jit(solution)/shard_map/ppermute | solution.py:40
  36.4 1.4 %collective-permute-start.13 = (bf16[128,2048]{1,0:T(8,128)(2,1)S(1)}, bf16[128,2048]{1,0:T(8,128)(2,1)S(1)}, u32[]{:S(2)}, u32[]{:S(2)}) collective-permute-start(bf16[128,2048]{1,0:T(8,128)(2,1)S(1)} %add_convert_fusion.3), channel_id=1, source_target_pairs={{0,16},{1,17},{2,18},{3,19},{4,12},{5,13},{6,14},{7,15},{8,24},{9,... | collective-permute-start | bytes 1572872 | tf_op jit(solution)/shard_map/ppermute | solution.py:40
  38.6 1.2 %collective-permute-done.15.cot = bf16[128,2048]{1,0:T(8,128)(2,1)S(1)} collective-permute-done((bf16[128,2048]{1,0:T(8,128)(2,1)S(1)}, bf16[128,2048]{1,0:T(8,128)(2,1)S(1)}, u32[]{:S(2)}, u32[]{:S(2)}) %collective-permute-start.15) | collective-permute-done | bytes 524320 | tf_op jit(solution)/shard_map/ppermute | solution.py:40
  39.8 1.8 %shard_map.121 = (bf16[128,384]{1,0:T(8,128)(2,1)S(1)}, bf16[128,384]{1,0:T(8,128)(2,1)S(1)}, bf16[128,2048]{1,0:T(8,128)(2,1)S(1)}, bf16[128,2048]{1,0:T(8,128)(2,1)S(1)}) custom-call(bf16[128,2048]{1,0:T(8,128)(2,1)S(1)} %collective-permute-done.15.cot, f32[128,128]{1,0:T(8,128)S(1)} %get-tuple-element.81.weight, f32[128,384]{1,0:T(8,128)S(1)} %get-tuple-element.82.gate_f, ...), custom_call_target="tpu_custom_call" | custom-call | flops 11500000256 | tf_op jit(solution)/shard_map/pallas_call | solution.py:181
  41.7 1.1 %shard_map.122 = bf16[128,2048]{1,0:T(8,128)(2,1)S(1)} custom-call(bf16[128,384]{1,0:T(8,128)(2,1)S(1)} %get-tuple-element.79.gate.refs_5_, bf16[128,384]{1,0:T(8,128)(2,1)S(1)} %get-tuple-element.85.up.refs_8_, bf16[1,2048,384]{2,1,0:T(8,128)(2,1)S(1)} %get-tuple-element.62.w_gate, bf16[1,2048,384]{2,1,0:T(8,128)(2,1)S(1)} %get-tuple-element.65.w_up), custom_call_target="tpu_custom_call" | custom-call | flops 11500000256 | tf_op jit(solution)/shard_map/pallas_call | solution.py:181
  43.7 1.5 %collective-permute-start.23 = (bf16[128,2048]{1,0:T(8,128)(2,1)S(1)}, bf16[128,2048]{1,0:T(8,128)(2,1)S(1)}, u32[]{:S(2)}, u32[]{:S(2)}) collective-permute-start(bf16[128,2048]{1,0:T(8,128)(2,1)S(1)} %add_convert_fusion.2), channel_id=1, source_target_pairs={{0,16},{1,17},{2,18},{3,19},{4,12},{5,13},{6,14},{7,15},{8,24},{9,... | collective-permute-start | bytes 1572872 | tf_op jit(solution)/shard_map/ppermute | solution.py:40
  45.9 1.4 %collective-permute-start.17 = (bf16[64,2048]{1,0:T(8,128)(2,1)S(1)}, bf16[64,2048]{1,0:T(8,128)(2,1)S(1)}, u32[]{:S(2)}, u32[]{:S(2)}) collective-permute-start(bf16[64,2048]{1,0:T(8,128)(2,1)S(1)} %slice.49), channel_id=1, source_target_pairs={{0,8},{1,9},{2,10},{3,11},{4,20},{5,21},{6,22},{7,23},{8,0},{9,1},... | collective-permute-start | bytes 786440 | tf_op jit(solution)/shard_map/ppermute | solution.py:40
  47.3 2.0 %shard_map.123 = (bf16[128,2048]{1,0:T(8,128)(2,1)S(1)}, bf16[128,2048]{1,0:T(8,128)(2,1)S(1)}, bf16[256,384]{1,0:T(8,128)(2,1)S(1)}, bf16[256,384]{1,0:T(8,128)(2,1)S(1)}, bf16[256,2048]{1,0:T(8,128)(2,1)S(1)}) custom-call(bf16[128,2048]{1,0:T(8,128)(2,1)S(1)} %shard_map.116.a, bf16[128,2048]{1,0:T(8,128)(2,1)S(1)} %collective-permute-done.21.b, ...), custom_call_target="tpu_custom_call" | custom-call | flops 11500000256 | tf_op jit(solution)/shard_map/pallas_call | solution.py:181
  49.4 2.2 %shard_map.125 = bf16[1,384,2048]{2,1,0:T(8,128)(2,1)} custom-call(bf16[256,384]{1,0:T(8,128)(2,1)S(1)} %get-tuple-element.101.refs_0_, bf16[128,384]{1,0:T(8,128)(2,1)S(1)} %get-tuple-element.71.act.refs_1_, bf16[128,384]{1,0:T(8,128)(2,1)S(1)} %get-tuple-element.73.refs_2_, bf16[256,2048]{1,0:T(8,128)(2,1)S(1)} %get-tuple-element.102.refs_3_, ...), custom_call_target="tpu_custom_call" | custom-call | flops 11500000256 | tf_op jit(solution)/shard_map/pallas_call | solution.py:342
  51.6 3.5 %shard_map.124 = (bf16[1,2048,384]{2,1,0:T(8,128)(2,1)}, bf16[1,2048,384]{2,1,0:T(8,128)(2,1)}) custom-call(bf16[128,2176]{1,0:T(8,128)(2,1)S(1)} %shard_map.114.a.refs_0_, bf16[128,2176]{1,0:T(8,128)(2,1)S(1)} %collective-permute-done.7.b.refs_1_, bf16[128,2176]{1,0:T(8,128)(2,1)S(1)} %collective-permute-done.9.a.refs_2_, ...), custom_call_target="tpu_custom_call" | custom-call | flops 11500000256 | tf_op jit(solution)/shard_map/pallas_call | solution.py:342
  56.0 1.6 %collective-permute-start.24 = (bf16[64,2048]{1,0:T(8,128)(2,1)S(1)}, bf16[64,2048]{1,0:T(8,128)(2,1)S(1)}, u32[]{:S(2)}, u32[]{:S(2)}) collective-permute-start(bf16[64,2048]{1,0:T(8,128)(2,1)S(1)} %slice.55), channel_id=1, source_target_pairs={{0,8},{1,9},{2,10},{3,11},{4,20},{5,21},{6,22},{7,23},{8,0},{9,1},... | collective-permute-start | bytes 786440 | tf_op jit(solution)/shard_map/ppermute | solution.py:40
  57.6 4.7 %collective-permute-start.20 = (bf16[16,2048]{1,0:T(8,128)(2,1)S(1)}, bf16[16,2048]{1,0:T(8,128)(2,1)S(1)}, u32[]{:S(2)}, u32[]{:S(2)}) collective-permute-start(bf16[16,2048]{1,0:T(8,128)(2,1)S(1)} %get-tuple-element.109), channel_id=1, source_target_pairs={{0,1},{1,2},{2,3},{3,0},{4,5},{5,6},{6,7},{7,4},{8,9},{9,10},{10,1... | collective-permute-start | bytes 196616 | tf_op jit(solution)/shard_map/ppermute | solution.py:40
  62.2 2.4 %collective-permute-start.19 = (bf16[16,2048]{1,0:T(8,128)(2,1)S(1)}, bf16[16,2048]{1,0:T(8,128)(2,1)S(1)}, u32[]{:S(2)}, u32[]{:S(2)}) collective-permute-start(bf16[16,2048]{1,0:T(8,128)(2,1)S(1)} %get-tuple-element.110), channel_id=1, source_target_pairs={{0,2},{1,3},{2,0},{3,1},{4,6},{5,7},{6,4},{7,5},{8,10},{9,11},{10,... | collective-permute-start | bytes 196616 | tf_op jit(solution)/shard_map/ppermute | solution.py:40
  64.8 2.4 %collective-permute-start.27 = (bf16[16,2048]{1,0:T(8,128)(2,1)S(1)}, bf16[16,2048]{1,0:T(8,128)(2,1)S(1)}, u32[]{:S(2)}, u32[]{:S(2)}) collective-permute-start(bf16[16,2048]{1,0:T(8,128)(2,1)S(1)} %get-tuple-element.106), channel_id=1, source_target_pairs={{0,1},{1,2},{2,3},{3,0},{4,5},{5,6},{6,7},{7,4},{8,9},{9,10},{10,1... | collective-permute-start | bytes 196616 | tf_op jit(solution)/shard_map/ppermute | solution.py:40
  67.2 2.4 %collective-permute-start.26 = (bf16[16,2048]{1,0:T(8,128)(2,1)S(1)}, bf16[16,2048]{1,0:T(8,128)(2,1)S(1)}, u32[]{:S(2)}, u32[]{:S(2)}) collective-permute-start(bf16[16,2048]{1,0:T(8,128)(2,1)S(1)} %get-tuple-element.107), channel_id=1, source_target_pairs={{0,2},{1,3},{2,0},{3,1},{4,6},{5,7},{6,4},{7,5},{8,10},{9,11},{10,... | collective-permute-start | bytes 196616 | tf_op jit(solution)/shard_map/ppermute | solution.py:40
  70.9 1.0 %collective-permute-done.27 = bf16[16,2048]{1,0:T(8,128)(2,1)S(1)} collective-permute-done((bf16[16,2048]{1,0:T(8,128)(2,1)S(1)}, bf16[16,2048]{1,0:T(8,128)(2,1)S(1)}, u32[]{:S(2)}, u32[]{:S(2)}) %collective-permute-start.27) | collective-permute-done | bytes 65568 | tf_op jit(solution)/shard_map/ppermute | solution.py:40
  71.9 2.6 %collective-permute-done.26 = bf16[16,2048]{1,0:T(8,128)(2,1)S(1)} collective-permute-done((bf16[16,2048]{1,0:T(8,128)(2,1)S(1)}, bf16[16,2048]{1,0:T(8,128)(2,1)S(1)}, u32[]{:S(2)}, u32[]{:S(2)}) %collective-permute-start.26) | collective-permute-done | bytes 65568 | tf_op jit(solution)/shard_map/ppermute | solution.py:40
  (52 shorter events, 11.4 us)
Async XLA Ops:
  1.6 8.0 %collective-permute-start = (bf16[16,2176]{1,0:T(8,128)(2,1)S(1)}, bf16[16,2176]{1,0:T(8,128)(2,1)S(1)}, u32[]{:S(2)}, u32[]{:S(2)}) collective-permute-start(bf16[16,2176]{1,0:T(8,128)(2,1)S(1)} %get-tuple-element.57.refs_0_), channel_id=1, source_target_pairs={{0,1},{1,2},{2,3},{3,0},{4,5},{5,6},{6,7},{7,4},{8,9},{9,10},{10,1... | collective-permute-start | bytes 208904 | tf_op jit(solution)/shard_map/ppermute | solution.py:40
  4.7 7.8 %collective-permute-start.1 = (bf16[16,2176]{1,0:T(8,128)(2,1)S(1)}, bf16[16,2176]{1,0:T(8,128)(2,1)S(1)}, u32[]{:S(2)}, u32[]{:S(2)}) collective-permute-start(bf16[16,2176]{1,0:T(8,128)(2,1)S(1)} %get-tuple-element.57.refs_0_), channel_id=1, source_target_pairs={{0,2},{1,3},{2,0},{3,1},{4,6},{5,7},{6,4},{7,5},{8,10},{9,11},{10,... | collective-permute-start | bytes 208904 | tf_op jit(solution)/shard_map/ppermute | solution.py:40
  7.3 5.3 %collective-permute-start.2 = (bf16[16,2176]{1,0:T(8,128)(2,1)S(1)}, bf16[16,2176]{1,0:T(8,128)(2,1)S(1)}, u32[]{:S(2)}, u32[]{:S(2)}) collective-permute-start(bf16[16,2176]{1,0:T(8,128)(2,1)S(1)} %get-tuple-element.57.refs_0_), channel_id=1, source_target_pairs={{0,3},{1,0},{2,1},{3,2},{4,7},{5,4},{6,5},{7,6},{8,11},{9,8},{10,9... | collective-permute-start | bytes 208904 | tf_op jit(solution)/shard_map/ppermute | solution.py:40
  8.6 7.8 %collective-permute-start.4 = (bf16[16,2048]{1,0:T(8,128)(2,1)S(1)}, bf16[16,2048]{1,0:T(8,128)(2,1)S(1)}, u32[]{:S(2)}, u32[]{:S(2)}) collective-permute-start(bf16[16,2048]{1,0:T(8,128)(2,1)S(1)} %get-tuple-element.63.refs_0_), channel_id=1, source_target_pairs={{0,1},{1,2},{2,3},{3,0},{4,5},{5,6},{6,7},{7,4},{8,9},{9,10},{10,1... | collective-permute-start | bytes 196616 | tf_op jit(solution)/shard_map/ppermute | solution.py:40
  9.3 8.4 %collective-permute-start.5 = (bf16[16,2048]{1,0:T(8,128)(2,1)S(1)}, bf16[16,2048]{1,0:T(8,128)(2,1)S(1)}, u32[]{:S(2)}, u32[]{:S(2)}) collective-permute-start(bf16[16,2048]{1,0:T(8,128)(2,1)S(1)} %get-tuple-element.63.refs_0_), channel_id=1, source_target_pairs={{0,2},{1,3},{2,0},{3,1},{4,6},{5,7},{6,4},{7,5},{8,10},{9,11},{10,... | collective-permute-start | bytes 196616 | tf_op jit(solution)/shard_map/ppermute | solution.py:40
  9.6 8.0 %collective-permute-start.6 = (bf16[16,2048]{1,0:T(8,128)(2,1)S(1)}, bf16[16,2048]{1,0:T(8,128)(2,1)S(1)}, u32[]{:S(2)}, u32[]{:S(2)}) collective-permute-start(bf16[16,2048]{1,0:T(8,128)(2,1)S(1)} %get-tuple-element.63.refs_0_), channel_id=1, source_target_pairs={{0,3},{1,0},{2,1},{3,2},{4,7},{5,4},{6,5},{7,6},{8,11},{9,8},{10,9... | collective-permute-start | bytes 196616 | tf_op jit(solution)/shard_map/ppermute | solution.py:40
  12.6 6.6 %collective-permute-start.3 = (bf16[64,2176]{1,0:T(8,128)(2,1)S(1)}, bf16[64,2176]{1,0:T(8,128)(2,1)S(1)}, u32[]{:S(2)}, u32[]{:S(2)}) collective-permute-start(bf16[64,2176]{1,0:T(8,128)(2,1)S(1)} %shard_map.111.refs_0_), channel_id=1, source_target_pairs={{0,8},{1,9},{2,10},{3,11},{4,20},{5,21},{6,22},{7,23},{8,0},{9,1},... | collective-permute-start | bytes 835592 | tf_op jit(solution)/shard_map/ppermute | solution.py:40
  19.3 3.0 %collective-permute-start.7 = (bf16[128,2176]{1,0:T(8,128)(2,1)S(1)}, bf16[128,2176]{1,0:T(8,128)(2,1)S(1)}, u32[]{:S(2)}, u32[]{:S(2)}) collective-permute-start(bf16[128,2176]{1,0:T(8,128)(2,1)S(1)} %shard_map.114.a.refs_0_), channel_id=1, source_target_pairs={{0,4},{1,5},{2,6},{3,7},{4,0},{5,1},{6,2},{7,3},{8,12},{9,13},{10,... | collective-permute-start | bytes 1671176 | tf_op jit(solution)/shard_map/ppermute | solution.py:40
  19.4 8.8 %collective-permute-start.10 = (bf16[64,2048]{1,0:T(8,128)(2,1)S(1)}, bf16[64,2048]{1,0:T(8,128)(2,1)S(1)}, u32[]{:S(2)}, u32[]{:S(2)}) collective-permute-start(bf16[64,2048]{1,0:T(8,128)(2,1)S(1)} %shard_map.113.refs_0_), channel_id=1, source_target_pairs={{0,8},{1,9},{2,10},{3,11},{4,20},{5,21},{6,22},{7,23},{8,0},{9,1},... | collective-permute-start | bytes 786440 | tf_op jit(solution)/shard_map/ppermute | solution.py:40
  20.8 10.5 %collective-permute-start.9 = (bf16[128,2176]{1,0:T(8,128)(2,1)S(1)}, bf16[128,2176]{1,0:T(8,128)(2,1)S(1)}, u32[]{:S(2)}, u32[]{:S(2)}) collective-permute-start(bf16[128,2176]{1,0:T(8,128)(2,1)S(1)} %shard_map.114.a.refs_0_), channel_id=1, source_target_pairs={{0,16},{1,17},{2,18},{3,19},{4,12},{5,13},{6,14},{7,15},{8,24},{9,... | collective-permute-start | bytes 1671176 | tf_op jit(solution)/shard_map/ppermute | solution.py:40
  28.1 9.7 %collective-permute-start.14 = (bf16[128,2048]{1,0:T(8,128)(2,1)S(1)}, bf16[128,2048]{1,0:T(8,128)(2,1)S(1)}, u32[]{:S(2)}, u32[]{:S(2)}) collective-permute-start(bf16[128,2048]{1,0:T(8,128)(2,1)S(1)} %shard_map.116.a), channel_id=1, source_target_pairs={{0,16},{1,17},{2,18},{3,19},{4,12},{5,13},{6,14},{7,15},{8,24},{9,... | collective-permute-start | bytes 1572872 | tf_op jit(solution)/shard_map/ppermute | solution.py:40
  30.1 17.3 %collective-permute-start.21 = (bf16[128,2048]{1,0:T(8,128)(2,1)S(1)}, bf16[128,2048]{1,0:T(8,128)(2,1)S(1)}, u32[]{:S(2)}, u32[]{:S(2)}) collective-permute-start(bf16[128,2048]{1,0:T(8,128)(2,1)S(1)} %shard_map.116.a), channel_id=1, source_target_pairs={{0,4},{1,5},{2,6},{3,7},{4,0},{5,1},{6,2},{7,3},{8,12},{9,13},{10,... | collective-permute-start | bytes 1572872 | tf_op jit(solution)/shard_map/ppermute | solution.py:40
  31.2 2.0 %collective-permute-start.11 = (bf16[128,2176]{1,0:T(8,128)(2,1)S(1)}, bf16[128,2176]{1,0:T(8,128)(2,1)S(1)}, u32[]{:S(2)}, u32[]{:S(2)}) collective-permute-start(bf16[128,2176]{1,0:T(8,128)(2,1)S(1)} %collective-permute-done.9.a.refs_2_), channel_id=1, source_target_pairs={{0,4},{1,5},{2,6},{3,7},{4,0},{5,1},{6,2},{7,3},{8,12},{9,13},{10,... | collective-permute-start | bytes 1671176 | tf_op jit(solution)/shard_map/ppermute | solution.py:40
  31.6 14.1 %collective-permute-start.8 = (bf16[128,2048]{1,0:T(8,128)(2,1)S(1)}, bf16[128,2048]{1,0:T(8,128)(2,1)S(1)}, u32[]{:S(2)}, u32[]{:S(2)}) collective-permute-start(bf16[128,2048]{1,0:T(8,128)(2,1)S(1)} %get-tuple-element.68), channel_id=1, source_target_pairs={{0,4},{1,5},{2,6},{3,7},{4,0},{5,1},{6,2},{7,3},{8,12},{9,13},{10,... | collective-permute-start | bytes 1572872 | tf_op jit(solution)/shard_map/ppermute | solution.py:40
  34.3 2.0 %collective-permute-start.12 = (bf16[128,2048]{1,0:T(8,128)(2,1)S(1)}, bf16[128,2048]{1,0:T(8,128)(2,1)S(1)}, u32[]{:S(2)}, u32[]{:S(2)}) collective-permute-start(bf16[128,2048]{1,0:T(8,128)(2,1)S(1)} %get-tuple-element.75), channel_id=1, source_target_pairs={{0,4},{1,5},{2,6},{3,7},{4,0},{5,1},{6,2},{7,3},{8,12},{9,13},{10,... | collective-permute-start | bytes 1572872 | tf_op jit(solution)/shard_map/ppermute | solution.py:40
  36.4 9.2 %collective-permute-start.13 = (bf16[128,2048]{1,0:T(8,128)(2,1)S(1)}, bf16[128,2048]{1,0:T(8,128)(2,1)S(1)}, u32[]{:S(2)}, u32[]{:S(2)}) collective-permute-start(bf16[128,2048]{1,0:T(8,128)(2,1)S(1)} %add_convert_fusion.3), channel_id=1, source_target_pairs={{0,16},{1,17},{2,18},{3,19},{4,12},{5,13},{6,14},{7,15},{8,24},{9,... | collective-permute-start | bytes 1572872 | tf_op jit(solution)/shard_map/ppermute | solution.py:40
  37.9 1.9 %collective-permute-start.15 = (bf16[128,2048]{1,0:T(8,128)(2,1)S(1)}, bf16[128,2048]{1,0:T(8,128)(2,1)S(1)}, u32[]{:S(2)}, u32[]{:S(2)}) collective-permute-start(bf16[128,2048]{1,0:T(8,128)(2,1)S(1)} %collective-permute-done.14.cot), channel_id=1, source_target_pairs={{0,4},{1,5},{2,6},{3,7},{4,0},{5,1},{6,2},{7,3},{8,12},{9,13},{10,... | collective-permute-start | bytes 1572872 | tf_op jit(solution)/shard_map/ppermute | solution.py:40
  41.5 2.0 %collective-permute-start.16 = (bf16[128,2048]{1,0:T(8,128)(2,1)S(1)}, bf16[128,2048]{1,0:T(8,128)(2,1)S(1)}, u32[]{:S(2)}, u32[]{:S(2)}) collective-permute-start(bf16[128,2048]{1,0:T(8,128)(2,1)S(1)} %get-tuple-element.86), channel_id=1, source_target_pairs={{0,4},{1,5},{2,6},{3,7},{4,0},{5,1},{6,2},{7,3},{8,12},{9,13},{10,... | collective-permute-start | bytes 1572872 | tf_op jit(solution)/shard_map/ppermute | solution.py:40
  43.7 12.1 %collective-permute-start.23 = (bf16[128,2048]{1,0:T(8,128)(2,1)S(1)}, bf16[128,2048]{1,0:T(8,128)(2,1)S(1)}, u32[]{:S(2)}, u32[]{:S(2)}) collective-permute-start(bf16[128,2048]{1,0:T(8,128)(2,1)S(1)} %add_convert_fusion.2), channel_id=1, source_target_pairs={{0,16},{1,17},{2,18},{3,19},{4,12},{5,13},{6,14},{7,15},{8,24},{9,... | collective-permute-start | bytes 1572872 | tf_op jit(solution)/shard_map/ppermute | solution.py:40
  45.9 9.1 %collective-permute-start.17 = (bf16[64,2048]{1,0:T(8,128)(2,1)S(1)}, bf16[64,2048]{1,0:T(8,128)(2,1)S(1)}, u32[]{:S(2)}, u32[]{:S(2)}) collective-permute-start(bf16[64,2048]{1,0:T(8,128)(2,1)S(1)} %slice.49), channel_id=1, source_target_pairs={{0,8},{1,9},{2,10},{3,11},{4,20},{5,21},{6,22},{7,23},{8,0},{9,1},... | collective-permute-start | bytes 786440 | tf_op jit(solution)/shard_map/ppermute | solution.py:40
  49.3 6.4 %collective-permute-start.22 = (bf16[128,2048]{1,0:T(8,128)(2,1)S(1)}, bf16[128,2048]{1,0:T(8,128)(2,1)S(1)}, u32[]{:S(2)}, u32[]{:S(2)}) collective-permute-start(bf16[128,2048]{1,0:T(8,128)(2,1)S(1)} %get-tuple-element.93), channel_id=1, source_target_pairs={{0,4},{1,5},{2,6},{3,7},{4,0},{5,1},{6,2},{7,3},{8,12},{9,13},{10,... | collective-permute-start | bytes 1572872 | tf_op jit(solution)/shard_map/ppermute | solution.py:40
  56.0 8.7 %collective-permute-start.24 = (bf16[64,2048]{1,0:T(8,128)(2,1)S(1)}, bf16[64,2048]{1,0:T(8,128)(2,1)S(1)}, u32[]{:S(2)}, u32[]{:S(2)}) collective-permute-start(bf16[64,2048]{1,0:T(8,128)(2,1)S(1)} %slice.55), channel_id=1, source_target_pairs={{0,8},{1,9},{2,10},{3,11},{4,20},{5,21},{6,22},{7,23},{8,0},{9,1},... | collective-permute-start | bytes 786440 | tf_op jit(solution)/shard_map/ppermute | solution.py:40
  57.6 12.1 %collective-permute-start.20 = (bf16[16,2048]{1,0:T(8,128)(2,1)S(1)}, bf16[16,2048]{1,0:T(8,128)(2,1)S(1)}, u32[]{:S(2)}, u32[]{:S(2)}) collective-permute-start(bf16[16,2048]{1,0:T(8,128)(2,1)S(1)} %get-tuple-element.109), channel_id=1, source_target_pairs={{0,1},{1,2},{2,3},{3,0},{4,5},{5,6},{6,7},{7,4},{8,9},{9,10},{10,1... | collective-permute-start | bytes 196616 | tf_op jit(solution)/shard_map/ppermute | solution.py:40
  62.2 7.4 %collective-permute-start.19 = (bf16[16,2048]{1,0:T(8,128)(2,1)S(1)}, bf16[16,2048]{1,0:T(8,128)(2,1)S(1)}, u32[]{:S(2)}, u32[]{:S(2)}) collective-permute-start(bf16[16,2048]{1,0:T(8,128)(2,1)S(1)} %get-tuple-element.110), channel_id=1, source_target_pairs={{0,2},{1,3},{2,0},{3,1},{4,6},{5,7},{6,4},{7,5},{8,10},{9,11},{10,... | collective-permute-start | bytes 196616 | tf_op jit(solution)/shard_map/ppermute | solution.py:40
  64.6 5.6 %collective-permute-start.18 = (bf16[16,2048]{1,0:T(8,128)(2,1)S(1)}, bf16[16,2048]{1,0:T(8,128)(2,1)S(1)}, u32[]{:S(2)}, u32[]{:S(2)}) collective-permute-start(bf16[16,2048]{1,0:T(8,128)(2,1)S(1)} %get-tuple-element.108), channel_id=1, source_target_pairs={{0,3},{1,0},{2,1},{3,2},{4,7},{5,4},{6,5},{7,6},{8,11},{9,8},{10,9... | collective-permute-start | bytes 196616 | tf_op jit(solution)/shard_map/ppermute | solution.py:40
  64.8 7.2 %collective-permute-start.27 = (bf16[16,2048]{1,0:T(8,128)(2,1)S(1)}, bf16[16,2048]{1,0:T(8,128)(2,1)S(1)}, u32[]{:S(2)}, u32[]{:S(2)}) collective-permute-start(bf16[16,2048]{1,0:T(8,128)(2,1)S(1)} %get-tuple-element.106), channel_id=1, source_target_pairs={{0,1},{1,2},{2,3},{3,0},{4,5},{5,6},{6,7},{7,4},{8,9},{9,10},{10,1... | collective-permute-start | bytes 196616 | tf_op jit(solution)/shard_map/ppermute | solution.py:40
  67.2 7.4 %collective-permute-start.26 = (bf16[16,2048]{1,0:T(8,128)(2,1)S(1)}, bf16[16,2048]{1,0:T(8,128)(2,1)S(1)}, u32[]{:S(2)}, u32[]{:S(2)}) collective-permute-start(bf16[16,2048]{1,0:T(8,128)(2,1)S(1)} %get-tuple-element.107), channel_id=1, source_target_pairs={{0,2},{1,3},{2,0},{3,1},{4,6},{5,7},{6,4},{7,5},{8,10},{9,11},{10,... | collective-permute-start | bytes 196616 | tf_op jit(solution)/shard_map/ppermute | solution.py:40
  69.6 5.6 %collective-permute-start.25 = (bf16[16,2048]{1,0:T(8,128)(2,1)S(1)}, bf16[16,2048]{1,0:T(8,128)(2,1)S(1)}, u32[]{:S(2)}, u32[]{:S(2)}) collective-permute-start(bf16[16,2048]{1,0:T(8,128)(2,1)S(1)} %get-tuple-element.105), channel_id=1, source_target_pairs={{0,3},{1,0},{2,1},{3,2},{4,7},{5,4},{6,5},{7,6},{8,11},{9,8},{10,9... | collective-permute-start | bytes 196616 | tf_op jit(solution)/shard_map/ppermute | solution.py:40

commit v3 on v2

--- a/solution.py
+++ b/solution.py
@@ -31,9 +31,8 @@
     bits = n_dp.bit_length() - 2
     core = pairs(lambda d, z: (d ^ 1, z))
     plane = [mixed(s, bits) for s in range(bits)]
-    line = [pairs(lambda d, z, j=j: (d, (z + j) % n_ex)) for j in range(1, n_ex)]
-    back = [pairs(lambda d, z, j=j: (d, (z - j) % n_ex)) for j in range(1, n_ex)]
-    return core, plane, line, back
+    line = [pairs(lambda d, z, j=j: (d, z ^ j)) for j in reversed(range(1, n_ex))]
+    return core, plane, line
 
 
 def send(x, pairs):
@@ -123,24 +122,53 @@
     )(tokens, cotangent, route.T, probs.T)
 
 
-def stage_kernel(*refs):
-    count = len(refs) // 2
-    copies = [pltpu.make_async_copy(refs[i], refs[count + i], refs[-1].at[i]) for i in range(count)]
+def stage_kernel(gate, up, down, tall, wide, sems):
+    copies = [
+        pltpu.make_async_copy(a.at[0], b, sems.at[i])
+        for i, (a, b) in enumerate(((gate, tall.at[0]), (up, tall.at[1]), (down, wide.at[2])))
+    ]
     for copy in copies:
         copy.start()
-    for copy in copies:
+    for i, copy in enumerate(copies):
         copy.wait()
-
-
-def stage(*arrays):
+        if i < 2:
+            wide[i] = jnp.transpose(tall[i])
+        else:
+            tall[i] = jnp.transpose(wide[i])
+
+
+def stage(gate, up, down):
+    _, width, hidden = gate.shape
     return pl.pallas_call(
         stage_kernel,
-        in_specs=[ANY] * len(arrays),
-        out_specs=[WHOLE] * len(arrays),
-        out_shape=[pltpu.VMEM(a.shape, a.dtype) for a in arrays],
-        scratch_shapes=[pltpu.SemaphoreType.DMA((len(arrays),))],
-        compiler_params=params(50),
-    )(*arrays)
+        in_specs=[ANY] * 3,
+        out_specs=[WHOLE] * 2,
+        out_shape=[pltpu.VMEM((3, width, hidden), BF16), pltpu.VMEM((3, hidden, width), BF16)],
+        scratch_shapes=[pltpu.SemaphoreType.DMA((3,))],
+        compiler_params=params(52),
+    )(gate, up, down)
+
+
+class Weights:
+    def __init__(self, refs):
+        self.refs = refs
+        self.staged = len(refs) == 2
+
+    def hidden(self, x):
+        if self.staged:
+            return dot(x, self.refs[0][0]), dot(x, self.refs[0][1])
+        return dot(x, self.refs[0][0]), dot(x, self.refs[1][0])
+
+    def out(self, act):
+        return dot(act, self.refs[1][2] if self.staged else self.refs[2][0])
+
+    def act_cot(self, out_cot):
+        return dot(out_cot, self.refs[0][2]) if self.staged else nt(out_cot, self.refs[2][0])
+
+    def row_cot(self, gate, up):
+        if self.staged:
+            return dot(gate, self.refs[1][0]) + dot(up, self.refs[1][1])
+        return nt(gate, self.refs[0][0]) + nt(up, self.refs[1][0])
 
 
 def join_kernel(*refs):
@@ -178,8 +206,13 @@
             out_specs=grid_specs(block, [(f, w) for f, w, _ in given], []),
         )
     call["in_specs"] = [pl.BlockSpec(memory_space=pltpu.SMEM)] * len(scalars) + call["in_specs"]
+    first = len(scalars) + len(taken)
+
+    def run(*refs):
+        kernel(*refs[:first], Weights(refs[first : first + len(weights)]), *refs[first + len(weights) :])
+
     return pl.pallas_call(
-        kernel,
+        run,
         out_shape=shaped(*[((f * n, w), t) for f, w, t in given]),
         compiler_params=params(12 if block == n else 40),
         cost_estimate=cost(length),
@@ -194,8 +227,8 @@
     return jnp.sum(jnp.where(mine, table.astype(F32), 0.0), axis=1, keepdims=True)
 
 
-def hidden_units(x, w_gate, w_up, act, gate_f, up_f):
-    gate, up = dot(x, w_gate[0]), dot(x, w_up[0])
+def hidden_units(x, weights, act, gate_f, up_f):
+    gate, up = weights.hidden(x)
     s = jax.nn.sigmoid(gate)
     gate_s = gate * s
     act_val = (gate_s * up).astype(BF16)
@@ -205,98 +238,104 @@
     return act_val
 
 
-def forward_pair_kernel(experts, expert, a, b, w_gate, w_up, w_down, kept, given, act, gate_f, up_f, weight):
-    n, width = a.shape[0], w_gate.shape[1]
+def forward_pair_kernel(experts, width, expert, a, b, weights, kept, given, act, gate_f, up_f, weight):
+    n = a.shape[0]
     x = jnp.concatenate((a[:, :width], b[:, :width]))
     p = expert_weight(experts, expert, jnp.concatenate((a[:, width:], b[:, width:])))
     weight[...] = jnp.broadcast_to(p, weight.shape)
-    act_val = hidden_units(x, w_gate, w_up, act, gate_f, up_f)
-    out = p * dot(act_val, w_down[0])
+    out = p * weights.out(hidden_units(x, weights, act, gate_f, up_f))
     kept[...] = out[:n].astype(BF16)
     given[...] = out[n:].astype(BF16)
 
 
-def forward_pair(a, b, weights, expert, experts, length=0.0):
-    width, hidden = weights[0].shape[1:]
-    given = [(1, width, BF16)] * 2 + [(2, hidden, BF16), (2, hidden, F32), (2, hidden, F32), (2, 128, F32)]
-    kernel = functools.partial(forward_pair_kernel, experts)
-    return over_rows(kernel, a.shape[0], [expert], [(1, a), (1, b)], weights, given, length)
-
-
-def forward_hidden_kernel(experts, expert, a, w_gate, w_up, act, gate_f, up_f, weight):
-    width = w_gate.shape[1]
+def forward_hidden_kernel(experts, width, expert, a, weights, act, gate_f, up_f, weight):
     weight[...] = jnp.broadcast_to(expert_weight(experts, expert, a[:, width:]), weight.shape)
-    hidden_units(a[:, :width], w_gate, w_up, act, gate_f, up_f)
-
-
-def forward_out_kernel(act, weight, w_down, out):
-    out[...] = (weight[:, :1] * dot(act[...], w_down[0])).astype(BF16)
-
-
-def forward_full_kernel(experts, expert, a, w_gate, w_up, w_down, act, gate_f, up_f, weight, out):
-    width = w_gate.shape[1]
+    hidden_units(a[:, :width], weights, act, gate_f, up_f)
+
+
+def forward_out_kernel(act, weight, weights, out):
+    out[...] = (weight[:, :1] * weights.out(act[...])).astype(BF16)
+
+
+def forward_full_kernel(experts, width, expert, a, weights, act, gate_f, up_f, weight, out):
     p = expert_weight(experts, expert, a[:, width:])
     weight[...] = jnp.broadcast_to(p, weight.shape)
-    act_val = hidden_units(a[:, :width], w_gate, w_up, act, gate_f, up_f)
-    out[...] = (p * dot(act_val, w_down[0])).astype(BF16)
-
-
-def forward_one(kernel, a, weights, expert, experts, outs, length=0.0):
-    width, hidden = weights[0].shape[1:]
-    given = [(1, hidden, BF16), (1, hidden, F32), (1, hidden, F32), (1, 128, F32)] + [(1, width, BF16)] * outs
-    return over_rows(functools.partial(kernel, experts), a.shape[0], [expert], [(1, a)], weights, given, length)
-
-
-def hidden_cots(cot, weight, gate_f, up_f, w_down, gate_cot, up_cot, out_cot):
+    act_val = hidden_units(a[:, :width], weights, act, gate_f, up_f)
+    out[...] = (p * weights.out(act_val)).astype(BF16)
+
+
+def hidden_cots(cot, weight, gate_f, up_f, weights, gate_cot, up_cot, out_cot):
     out = (cot.astype(F32) * weight[:, :1]).astype(BF16)
     out_cot[...] = out
-    act_cot = nt(out, w_down[0])
+    act_cot = weights.act_cot(out)
     gate = (act_cot * gate_f[...]).astype(BF16)
     up = (act_cot * up_f[...]).astype(BF16)
     gate_cot[...], up_cot[...] = gate, up
     return gate, up
 
 
-def row_cots(gate, up, w_gate, w_up):
-    return nt(gate, w_gate[0]) + nt(up, w_up[0])
-
-
-def backward_pair_kernel(a, b, weight, gate_f, up_f, w_gate, w_up, w_down, kept, given, gate_cot, up_cot, out_cot):
+def backward_pair_kernel(a, b, weight, gate_f, up_f, weights, kept, given, gate_cot, up_cot, out_cot):
     n = a.shape[0]
     cot = jnp.concatenate((a[...], b[...]))
-    gate, up = hidden_cots(cot, weight, gate_f, up_f, w_down, gate_cot, up_cot, out_cot)
-    part = row_cots(gate, up, w_gate, w_up)
+    part = weights.row_cot(*hidden_cots(cot, weight, gate_f, up_f, weights, gate_cot, up_cot, out_cot))
     kept[...] = part[:n].astype(BF16)
     given[...] = part[n:].astype(BF16)
 
 
-def backward_pair(a, b, weight, gate_f, up_f, weights, length=0.0):
-    n, width = a.shape
-    hidden = weights[0].shape[2]
-    taken = [(1, a), (1, b), (2, weight), (2, gate_f), (2, up_f)]
-    given = [(1, width, BF16)] * 2 + [(2, hidden, BF16)] * 2 + [(2, width, BF16)]
-    return over_rows(backward_pair_kernel, n, [], taken, weights, given, length)
-
-
-def backward_hidden_kernel(cot, weight, gate_f, up_f, w_down, gate_cot, up_cot, out_cot):
-    hidden_cots(cot[...], weight, gate_f, up_f, w_down, gate_cot, up_cot, out_cot)
-
-
-def backward_rows_kernel(gate, up, w_gate, w_up, out):
-    out[...] = row_cots(gate[...], up[...], w_gate, w_up).astype(BF16)
-
-
-def backward_full_kernel(cot, weight, gate_f, up_f, w_gate, w_up, w_down, gate_cot, up_cot, out_cot, out):
-    gate, up = hidden_cots(cot[...], weight, gate_f, up_f, w_down, gate_cot, up_cot, out_cot)
-    out[...] = row_cots(gate, up, w_gate, w_up).astype(BF16)
-
-
-def backward_one(kernel, cot, weight, gate_f, up_f, weights, outs, length=0.0):
-    n, width = cot.shape
-    hidden = gate_f.shape[1]
-    taken = [(1, cot), (1, weight), (1, gate_f), (1, up_f)]
-    given = [(1, hidden, BF16)] * 2 + [(1, width, BF16)] * (1 + outs)
-    return over_rows(kernel, n, [], taken, weights, given, length)
+def backward_hidden_kernel(cot, weight, gate_f, up_f, weights, gate_cot, up_cot, out_cot):
+    hidden_cots(cot[...], weight, gate_f, up_f, weights, gate_cot, up_cot, out_cot)
+
+
+def backward_rows_kernel(gate, up, weights, out):
+    out[...] = weights.row_cot(gate[...], up[...]).astype(BF16)
+
+
+def backward_full_kernel(cot, weight, gate_f, up_f, weights, gate_cot, up_cot, out_cot, out):
+    gate, up = hidden_cots(cot[...], weight, gate_f, up_f, weights, gate_cot, up_cot, out_cot)
+    out[...] = weights.row_cot(gate, up).astype(BF16)
+
+
+def chunk_kernel(over_left, chunks, counts, *refs):
+    outs = len(counts) - 1
+    joined = []
+    for count in counts:
+        joined.append(refs[:count])
+        refs = refs[count:]
+    results, held, sems = refs[:outs], refs[outs:-1], refs[-1]
+    split = 0 if over_left else 1
+    rest = [None if i == split else jnp.concatenate([r[...] for r in group]) for i, group in enumerate(joined)]
+    if over_left:
+        right = jnp.concatenate(rest[1:], axis=1)
+    size = held[0].shape[split] // chunks
+    copies = []
+    for i in range(chunks):
+        part = pl.ds(i * size, size)
+        piece = jnp.concatenate([r[:, part] for r in joined[split]])
+        value = tn(piece, right) if over_left else tn(rest[0], piece)
+        for j in range(outs):
+            width = value.shape[1] // outs
+            at = (part, slice(None)) if over_left else (slice(None), part)
+            held[j][at] = value[:, j * width : (j + 1) * width].astype(BF16)
+            copy = pltpu.make_async_copy(held[j].at[at], results[j].at[(0, *at)], sems.at[i, j])
+            copy.start()
+            copies.append(copy)
+    for copy in copies:
+        copy.wait()
+
+
+def gradients_by_chunks(left, rights, width, over_left, chunks=4):
+    hidden = rights[0][0].shape[1]
+    groups = [left, *rights]
+    flat = [piece for group in groups for piece in group]
+    return pl.pallas_call(
+        functools.partial(chunk_kernel, over_left, chunks, [len(g) for g in groups]),
+        in_specs=[WHOLE] * len(flat),
+        out_specs=[ANY] * len(rights),
+        out_shape=shaped(*[((1, width, hidden), BF16)] * len(rights)),
+        scratch_shapes=[pltpu.VMEM((width, hidden), BF16)] * len(rights) + [pltpu.SemaphoreType.DMA((chunks, len(rights)))],
+        compiler_params=params(16),
+        cost_estimate=cost(10.0),
+    )(*flat)
 
 
 def gradient_kernel(width, counts, *refs):
@@ -332,6 +371,10 @@
 
 def gradients(left, rights, width, steps):
     hidden = rights[0][0].shape[1]
+    if steps == 1:
+        over_left = width > hidden
+        if max(width, hidden) % (4 * 128) == 0:
+            return gradients_by_chunks(left, rights, width, over_left)
     groups = [left, *rights]
     flat = [piece for group in groups for piece in group]
     if steps == 1:
@@ -355,25 +398,41 @@
     n_dp, n_ex = lax.axis_size("dp"), lax.axis_size("expert")
     experts = n_dp * n_ex // 2
     rows, width = tokens.shape
-    core, plane, line, back = permutes(n_dp, n_ex)
+    hidden = gate_weight.shape[2]
+    core, plane, line = permutes(n_dp, n_ex)
     expert = lax.shift_right_logical(lax.axis_index(AXES).astype(jnp.int32), 1).reshape(1, 1)
     expert, tokens = lax.optimization_barrier((expert, tokens))
+    units = [(hidden, BF16), (hidden, F32), (hidden, F32), (128, F32)]
+    cots = [(hidden, BF16), (hidden, BF16), (width, BF16)]
+    wide = (1, width, BF16)
+
+    def each(factor, arrays):
+        return [(factor, *a) for a in arrays]
 
     own, cot = payload(tokens, cotangent, route, probs, experts)
-    row_lane = join(own, *[send(own, p) for p in line])
     weights = (gate_weight, up_weight, down_weight)
-    if row_lane.shape[0] * 2 <= BLOCK:
-        weights = stage(*(after(w, row_lane) for w in weights))
-    w_gate, w_up, w_down = weights
-    cot_lane = join(after(cot, w_gate), *[send(cot, p) for p in line], length=10.0)
+    staged = n_ex * rows * 2 <= BLOCK
+    if staged:
+        weights = stage(*(after(w, own) for w in weights))
+    row_lane = join(after(own, weights[0]), *[send(own, p) for p in line])
+    cot = after(cot, row_lane)
+    cot_lane = join(cot, *[send(cot, p) for p in line], length=10.0)
     for p in plane[:-2]:
         row_lane = join(row_lane, send(row_lane, p))
         cot_lane = join(cot_lane, send(cot_lane, p))
-    row_lane = join(row_lane, after(send(row_lane, plane[-2]), cot_lane))
+    row_lane = join(row_lane, send(row_lane, plane[-2]))
+    n = row_lane.shape[0]
     row_late = send(row_lane, plane[-1])
     row_other = send(row_lane, core)
-    f_early = forward_pair(row_lane, row_other, weights, expert, experts, 10.0)
-    cot_lane = join(cot_lane, after(send(cot_lane, plane[-2]), f_early[0]))
+
+    def forward(kernel, *args):
+        return functools.partial(kernel, experts, width), n, [expert], *args
+
+    f_early = over_rows(
+        *forward(forward_pair_kernel, [(1, row_lane), (1, row_other)], weights, [wide] * 2 + each(2, units))
+    )
+    kept, given, *f_early = f_early
+    cot_lane = join(cot_lane, after(send(cot_lane, plane[-2]), kept))
     cot_late = send(cot_lane, plane[-1])
     cot_other = send(cot_lane, core)
 
@@ -382,30 +441,36 @@
 
     row_late = after(row_late, cot_lane)
     row_late_other = send(row_late, core)
-    f_own = forward_one(forward_hidden_kernel, row_late, (w_gate, w_up), expert, experts, 0, 10.0)
-    f_other = forward_one(forward_full_kernel, row_late_other, weights, expert, experts, 1, 10.0)
-    o_other = send(f_other[4], core)
-    (o_own,) = over_rows(
-        forward_out_kernel, row_late.shape[0], [], [(1, f_own[0]), (1, after(f_own[3], f_other[0]))], (w_down,), [(1, width, BF16)], 10.0
+    f_own = over_rows(*forward(forward_hidden_kernel, [(1, row_late)], weights, each(1, units), 10.0))
+    *f_other, o_given = over_rows(
+        *forward(forward_full_kernel, [(1, row_late_other)], weights, each(1, units) + [wide], 10.0)
     )
+    o_other = send(o_given, core)
+    taken = [(1, f_own[0]), (1, after(f_own[3], f_other[0]))]
+    (o_own,) = over_rows(forward_out_kernel, n, [], taken, weights, [wide], 10.0)
     o_late = halve(o_own, o_other)
-    o_early_other = send(f_early[1], core)
+    o_early_other = send(given, core)
     o_back = send(o_late, plane[-1])
+
+    def with_units(cot, factor, f):
+        return [(factor, f[3]), (factor, f[1]), (factor, f[2])]
 
     cot_late = after(cot_late, o_late)
     cot_late_other = send(cot_late, core)
-    b_own = backward_one(backward_hidden_kernel, cot_late, f_own[3], f_own[1], f_own[2], (w_down,), 0, 10.0)
-    b_other = backward_one(
-        backward_full_kernel, cot_late_other, f_other[3], f_other[1], f_other[2], weights, 1, 10.0
-    )
-    g_other = send(b_other[3], core)
-    (g_own,) = over_rows(
-        backward_rows_kernel, cot_late.shape[0], [], [(1, b_own[0]), (1, after(b_own[1], b_other[0]))], (w_gate, w_up), [(1, width, BF16)], 10.0
-    )
+    taken = [(1, cot_late)] + with_units(cot_late, 1, f_own)
+    b_own = over_rows(backward_hidden_kernel, n, [], taken, weights, each(1, cots), 10.0)
+    taken = [(1, cot_late_other)] + with_units(cot_late_other, 1, f_other)
+    *b_other, g_given = over_rows(backward_full_kernel, n, [], taken, weights, each(1, cots) + [wide], 10.0)
+    g_other = send(g_given, core)
+    taken = [(1, b_own[0]), (1, after(b_own[1], b_other[0]))]
+    (g_own,) = over_rows(backward_rows_kernel, n, [], taken, weights, [wide], 10.0)
     g_late = halve(g_own, g_other)
     cot_other = after(cot_other, g_late)
-    b_early = backward_pair(cot_lane, cot_other, f_early[5], f_early[3], f_early[4], weights, 10.0)
-    g_early_other = send(b_early[1], core)
+    taken = [(1, cot_lane), (1, cot_other)] + with_units(cot_lane, 2, f_early)
+    g_kept, g_given, *b_early = over_rows(
+        backward_pair_kernel, n, [], taken, weights, [wide] * 2 + each(2, cots), 10.0
+    )
+    g_early_other = send(g_given, core)
     g_back = send(g_late, plane[-1])
     o_back = after(o_back, g_late)
 
@@ -414,18 +479,19 @@
             half = lane.shape[0] // 2
             lane = halve(lane[:half], send(lane[half:], p))
         terms = [lane[:rows]]
-        for j, p in enumerate(back, 1):
+        for j, p in enumerate(line, 1):
             terms.append(send(lane[j * rows : (j + 1) * rows], p))
         return add(*terms).astype(BF16)
 
-    mixed = finish(add(f_early[0], o_early_other, o_back).astype(BF16))
-    token_grad = finish(add(b_early[0], g_early_other, g_back).astype(BF16))
-
-    steps = max(1, row_late.shape[0] // BLOCK)
+    mixed = finish(add(kept, o_early_other, o_back).astype(BF16))
+    token_grad = finish(add(g_kept, g_early_other, g_back).astype(BF16))
+
+    steps = max(1, n // BLOCK)
     lefts = [after(row_lane, g_late), row_other, row_late, row_late_other]
-    gate_cots, up_cots, out_cots = zip(b_early[2:5], b_own[:3], b_other[:3])
+    gate_cots, up_cots, out_cots = zip(b_early, b_own, b_other)
     gate_grad, up_grad = gradients(lefts, [gate_cots, up_cots], width, steps)
-    (down_grad,) = gradients([after(f_early[2], g_late), f_own[0], f_other[0]], [out_cots], f_own[0].shape[1], steps)
+    acts = [after(f_early[0], g_late), f_own[0], f_other[0]]
+    (down_grad,) = gradients(acts, [out_cots], hidden, steps)
     return mixed, token_grad, gate_grad, up_grad, down_grad
 
 

time: 76 us -> 72.9 us (0.959)
  starting transfers between devices: 36.2 us -> 32.6 us
  waiting for transfers between devices: 17.7 us -> 20 us
  Pallas kernels: 18.8 us -> 17 us
    ppermute x28, starting transfers between devices: 36.2 us -> 32.6 us  [send(): return lax.ppermute(x, AXES, pairs)]
    ppermute x28, waiting for transfers between devices: 17.7 us -> 20 us  [send(): return lax.ppermute(x, AXES, pairs)]
    pallas_call x11, Pallas kernels: 17.7 us -> 16 us  [the longest x8 8.56 us: over_rows(): pl.pallas_call(run, out_shape=shaped(*[((f * n, w), t) for f, w, t in giv...]
  transfers between devices with their start and end apart: 28 -> 28, of which waited for: 15 -> 17; matrix products, arithmetic and copies ran while one was open for 2% -> 2% of each run, Pallas kernels for 23% -> 22%
where the time goes in v3:
time: 72.9 us; the launch traced here: 72.7 us
  starting transfers between devices  32.6 us (45%)
  waiting for transfers between devices  20 us (27%)
  Pallas kernels  17 us (23%)
  other arithmetic  2.2 us (3%)
  between operations  0.85 us (1%)
    ppermute x28, starting transfers between devices, send(): return lax.ppermute(x, AXES, pairs)  32.6 us
    ppermute x28, waiting for transfers between devices, send(): return lax.ppermute(x, AXES, pairs)  20 us
    pallas_call x8, Pallas kernels, over_rows(): pl.pallas_call(run, out_shape=shaped(*[((f * n, w), t) for f, w, t in giv...  8.56 us
    pallas_call x2, Pallas kernels, gradients_by_chunks(): pl.pallas_call(functools.partial(chunk_kernel, over_left, chunks, [len(g)...  4.57 us
    pallas_call x1, Pallas kernels, stage(): pl.pallas_call(stage_kernel, in_specs=[ANY] * 3, out_specs=[WHOLE] * 2, o...  2.86 us
  transfers between devices with their start and end apart: 28, of which 17 were waited for; matrix products, arithmetic and copies ran while one was open for 2% of the time, Pallas kernels for 22%

profile of v3, /device:TPU:0, one launch (start us, length us, event | category | flops | bytes accessed | tf_op | source)
XLA Modules:
  0.0 72.7 jit_solution(15508565338181661441)
XLA Ops:
  0.6 0.9 %shard_map.110 = (bf16[16,2176]{1,0:T(8,128)(2,1)S(1)}, bf16[16,2048]{1,0:T(8,128)(2,1)S(1)}) custom-call(bf16[16,2048]{1,0:T(8,128)(2,1)} %tokens, bf16[16,2048]{1,0:T(8,128)(2,1)} %cotangent.1, s32[8,16]{1,0:T(8,128)} %bitcast.3, f32[8,16]{1,0:T(8,128)} %bitcast.4), custom_call_target="tpu_custom_call" | custom-call | tf_op jit(solution)/shard_map/pallas_call | solution.py:111
  1.6 5.1 %collective-permute-start = (bf16[16,2176]{1,0:T(8,128)(2,1)S(1)}, bf16[16,2176]{1,0:T(8,128)(2,1)S(1)}, u32[]{:S(2)}, u32[]{:S(2)}) collective-permute-start(bf16[16,2176]{1,0:T(8,128)(2,1)S(1)} %get-tuple-element.61.refs_0_), channel_id=1, source_target_pairs={{0,3},{1,2},{2,1},{3,0},{4,7},{5,6},{6,5},{7,4},{8,11},{9,10},{10,... | collective-permute-start | bytes 208904 | tf_op jit(solution)/shard_map/ppermute | solution.py:39
  7.3 2.9 %shard_map.111 = (bf16[3,2048,384]{2,1,0:T(8,128)(2,1)S(1)}, bf16[3,384,2048]{2,1,0:T(8,128)(2,1)S(1)}) custom-call(bf16[1,2048,384]{2,1,0:T(8,128)(2,1)} %gate, bf16[1,2048,384]{2,1,0:T(8,128)(2,1)} %up, bf16[1,384,2048]{2,1,0:T(8,128)(2,1)} %down), custom_call_target="tpu_custom_call" | custom-call | tf_op jit(solution)/shard_map/pallas_call | solution.py:142
  10.2 2.4 %collective-permute-done.1.refs_2_ = bf16[16,2176]{1,0:T(8,128)(2,1)S(1)} collective-permute-done((bf16[16,2176]{1,0:T(8,128)(2,1)S(1)}, bf16[16,2176]{1,0:T(8,128)(2,1)S(1)}, u32[]{:S(2)}, u32[]{:S(2)}) %collective-permute-start.1) | collective-permute-done | bytes 69664 | tf_op jit(solution)/shard_map/ppermute | solution.py:39
  12.6 1.6 %collective-permute-start.3 = (bf16[64,2176]{1,0:T(8,128)(2,1)S(1)}, bf16[64,2176]{1,0:T(8,128)(2,1)S(1)}, u32[]{:S(2)}, u32[]{:S(2)}) collective-permute-start(bf16[64,2176]{1,0:T(8,128)(2,1)S(1)} %shard_map.112.refs_0_), channel_id=1, source_target_pairs={{0,8},{1,9},{2,10},{3,11},{4,20},{5,21},{6,22},{7,23},{8,0},{9,1},... | collective-permute-start | bytes 835592 | tf_op jit(solution)/shard_map/ppermute | solution.py:39
  14.2 2.7 %collective-permute-start.7 = (bf16[16,2048]{1,0:T(8,128)(2,1)S(1)}, bf16[16,2048]{1,0:T(8,128)(2,1)S(1)}, u32[]{:S(2)}, u32[]{:S(2)}) collective-permute-start(bf16[16,2048]{1,0:T(8,128)(2,1)S(1)} %get-tuple-element.66.refs_0_), channel_id=1, source_target_pairs={{0,3},{1,2},{2,1},{3,0},{4,7},{5,6},{6,5},{7,4},{8,11},{9,10},{10,... | collective-permute-start | bytes 196616 | tf_op jit(solution)/shard_map/ppermute | solution.py:39
  16.9 1.7 %collective-permute-start.9 = (bf16[16,2048]{1,0:T(8,128)(2,1)S(1)}, bf16[16,2048]{1,0:T(8,128)(2,1)S(1)}, u32[]{:S(2)}, u32[]{:S(2)}) collective-permute-start(bf16[16,2048]{1,0:T(8,128)(2,1)S(1)} %get-tuple-element.66.refs_0_), channel_id=1, source_target_pairs={{0,1},{1,0},{2,3},{3,2},{4,5},{5,4},{6,7},{7,6},{8,9},{9,8},{10,11... | collective-permute-start | bytes 196616 | tf_op jit(solution)/shard_map/ppermute | solution.py:39
  19.3 1.6 %collective-permute-start.6 = (bf16[128,2176]{1,0:T(8,128)(2,1)S(1)}, bf16[128,2176]{1,0:T(8,128)(2,1)S(1)}, u32[]{:S(2)}, u32[]{:S(2)}) collective-permute-start(bf16[128,2176]{1,0:T(8,128)(2,1)S(1)} %shard_map.113.refs_1_.refs_0_), channel_id=1, source_target_pairs={{0,16},{1,17},{2,18},{3,19},{4,12},{5,13},{6,14},{7,15},{8,24},{9,... | collective-permute-start | bytes 1671176 | tf_op jit(solution)/shard_map/ppermute | solution.py:39
  21.0 2.1 %collective-permute-done.8.refs_2_ = bf16[16,2048]{1,0:T(8,128)(2,1)S(1)} collective-permute-done((bf16[16,2048]{1,0:T(8,128)(2,1)S(1)}, bf16[16,2048]{1,0:T(8,128)(2,1)S(1)}, u32[]{:S(2)}, u32[]{:S(2)}) %collective-permute-start.8) | collective-permute-done | bytes 65568 | tf_op jit(solution)/shard_map/ppermute | solution.py:39
  23.9 1.9 %shard_map.114 = (bf16[128,2048]{1,0:T(8,128)(2,1)S(1)}, bf16[128,2048]{1,0:T(8,128)(2,1)S(1)}, bf16[256,384]{1,0:T(8,128)(2,1)S(1)}, f32[256,384]{1,0:T(8,128)S...) custom-call(s32[1,1]{1,0:T(1,128)} %bitcast.refs_0_, bf16[128,2176]{1,0:T(8,128)(2,1)S(1)} %shard_map.113.refs_1_.refs_0_, ...), custom_call_target="tpu_custom_call" | custom-call | tf_op jit(solution)/shard_map/pallas_call | solution.py:214
  25.9 3.7 %collective-permute-done.10.refs_1_ = bf16[64,2048]{1,0:T(8,128)(2,1)S(1)} collective-permute-done((bf16[64,2048]{1,0:T(8,128)(2,1)S(1)}, bf16[64,2048]{1,0:T(8,128)(2,1)S(1)}, u32[]{:S(2)}, u32[]{:S(2)}) %collective-permute-start.10) | collective-permute-done | bytes 262176 | tf_op jit(solution)/shard_map/ppermute | solution.py:39
  29.6 1.7 %collective-permute-start.14 = (bf16[128,2048]{1,0:T(8,128)(2,1)S(1)}, bf16[128,2048]{1,0:T(8,128)(2,1)S(1)}, u32[]{:S(2)}, u32[]{:S(2)}) collective-permute-start(bf16[128,2048]{1,0:T(8,128)(2,1)S(1)} %shard_map.116.refs_0_), channel_id=1, source_target_pairs={{0,16},{1,17},{2,18},{3,19},{4,12},{5,13},{6,14},{7,15},{8,24},{9,... | collective-permute-start | bytes 1572872 | tf_op jit(solution)/shard_map/ppermute | solution.py:39
  31.3 0.9 %collective-permute-start.21 = (bf16[128,2048]{1,0:T(8,128)(2,1)S(1)}, bf16[128,2048]{1,0:T(8,128)(2,1)S(1)}, u32[]{:S(2)}, u32[]{:S(2)}) collective-permute-start(bf16[128,2048]{1,0:T(8,128)(2,1)S(1)} %shard_map.116.refs_0_), channel_id=1, source_target_pairs={{0,4},{1,5},{2,6},{3,7},{4,0},{5,1},{6,2},{7,3},{8,12},{9,13},{10,... | collective-permute-start | bytes 1572872 | tf_op jit(solution)/shard_map/ppermute | solution.py:39
  33.4 1.1 %collective-permute-done.11.refs_1_.refs_3_ = bf16[128,2176]{1,0:T(8,128)(2,1)S(1)} collective-permute-done((bf16[128,2176]{1,0:T(8,128)(2,1)S(1)}, bf16[128,2176]{1,0:T(8,128)(2,1)S(1)}, u32[]{:S(2)}, u32[]{:S(2)}) %collective-permute-start.11) | collective-permute-done | bytes 557088 | tf_op jit(solution)/shard_map/ppermute | solution.py:39
  34.5 1.1 %shard_map.118 = (bf16[128,384]{1,0:T(8,128)(2,1)S(1)}, f32[128,384]{1,0:T(8,128)S(1)}, f32[128,384]{1,0:T(8,128)S(1)}, f32[128,128]{1,0:T(8,128)S(1)}, bf16[128,2048]{1,0:T(8,128)(2,1)S(1)}) custom-call(s32[1,1]{1,0:T(1,128)} %bitcast.refs_0_, bf16[128,2176]{1,0:T(8,128)(2,1)S(1)} %collective-permute-done.11.refs_1_.refs_3_, ...), custom_call_target="tpu_custom_call" | custom-call | flops 11500000256 | tf_op jit(solution)/shard_map/pallas_call | solution.py:214
  36.5 1.1 %collective-permute-done.12 = bf16[128,2048]{1,0:T(8,128)(2,1)S(1)} collective-permute-done((bf16[128,2048]{1,0:T(8,128)(2,1)S(1)}, bf16[128,2048]{1,0:T(8,128)(2,1)S(1)}, u32[]{:S(2)}, u32[]{:S(2)}) %collective-permute-start.12) | collective-permute-done | bytes 524320 | tf_op jit(solution)/shard_map/ppermute | solution.py:39
  39.6 1.1 %collective-permute-done.15.refs_0_ = bf16[128,2048]{1,0:T(8,128)(2,1)S(1)} collective-permute-done((bf16[128,2048]{1,0:T(8,128)(2,1)S(1)}, bf16[128,2048]{1,0:T(8,128)(2,1)S(1)}, u32[]{:S(2)}, u32[]{:S(2)}) %collective-permute-start.15) | collective-permute-done | bytes 524320 | tf_op jit(solution)/shard_map/ppermute | solution.py:39
  40.7 1.2 %shard_map.121 = (bf16[128,384]{1,0:T(8,128)(2,1)S(1)}, bf16[128,384]{1,0:T(8,128)(2,1)S(1)}, bf16[128,2048]{1,0:T(8,128)(2,1)S(1)}, bf16[128,2048]{1,0:T(8,128)(2,1)S(1)}) custom-call(bf16[128,2048]{1,0:T(8,128)(2,1)S(1)} %collective-permute-done.15.refs_0_, f32[128,128]{1,0:T(8,128)S(1)} %get-tuple-element.79.refs_1_, ...), custom_call_target="tpu_custom_call" | custom-call | flops 11500000256 | tf_op jit(solution)/shard_map/pallas_call | solution.py:214
  43.0 0.9 %collective-permute-done.16 = bf16[128,2048]{1,0:T(8,128)(2,1)S(1)} collective-permute-done((bf16[128,2048]{1,0:T(8,128)(2,1)S(1)}, bf16[128,2048]{1,0:T(8,128)(2,1)S(1)}, u32[]{:S(2)}, u32[]{:S(2)}) %collective-permute-start.16) | collective-permute-done | bytes 524320 | tf_op jit(solution)/shard_map/ppermute | solution.py:39
  44.0 1.7 %collective-permute-start.23 = (bf16[128,2048]{1,0:T(8,128)(2,1)S(1)}, bf16[128,2048]{1,0:T(8,128)(2,1)S(1)}, u32[]{:S(2)}, u32[]{:S(2)}) collective-permute-start(bf16[128,2048]{1,0:T(8,128)(2,1)S(1)} %add_convert_fusion.2), channel_id=1, source_target_pairs={{0,16},{1,17},{2,18},{3,19},{4,12},{5,13},{6,14},{7,15},{8,24},{9,... | collective-permute-start | bytes 1572872 | tf_op jit(solution)/shard_map/ppermute | solution.py:39
  45.8 1.2 %collective-permute-done.13 = bf16[128,2048]{1,0:T(8,128)(2,1)S(1)} collective-permute-done((bf16[128,2048]{1,0:T(8,128)(2,1)S(1)}, bf16[128,2048]{1,0:T(8,128)(2,1)S(1)}, u32[]{:S(2)}, u32[]{:S(2)}) %collective-permute-start.13) | collective-permute-done | bytes 524320 | tf_op jit(solution)/shard_map/ppermute | solution.py:39
  47.2 1.1 %collective-permute-start.17 = (bf16[64,2048]{1,0:T(8,128)(2,1)S(1)}, bf16[64,2048]{1,0:T(8,128)(2,1)S(1)}, u32[]{:S(2)}, u32[]{:S(2)}) collective-permute-start(bf16[64,2048]{1,0:T(8,128)(2,1)S(1)} %slice.49), channel_id=1, source_target_pairs={{0,8},{1,9},{2,10},{3,11},{4,20},{5,21},{6,22},{7,23},{8,0},{9,1},... | collective-permute-start | bytes 786440 | tf_op jit(solution)/shard_map/ppermute | solution.py:39
  48.3 2.0 %shard_map.123 = (bf16[128,2048]{1,0:T(8,128)(2,1)S(1)}, bf16[128,2048]{1,0:T(8,128)(2,1)S(1)}, bf16[256,384]{1,0:T(8,128)(2,1)S(1)}, bf16[256,384]{1,0:T(8,128)(2,1)S(1)}, bf16[256,2048]{1,0:T(8,128)(2,1)S(1)}) custom-call(bf16[128,2048]{1,0:T(8,128)(2,1)S(1)} %shard_map.116.refs_0_, bf16[128,2048]{1,0:T(8,128)(2,1)S(1)} %collective-permute-done.21.refs_1_, ...), custom_call_target="tpu_custom_call" | custom-call | flops 11500000256 | tf_op jit(solution)/shard_map/pallas_call | solution.py:214
  50.4 1.8 %shard_map.125 = bf16[1,384,2048]{2,1,0:T(8,128)(2,1)} custom-call(bf16[256,384]{1,0:T(8,128)(2,1)S(1)} %get-tuple-element.99.refs_0_, bf16[128,384]{1,0:T(8,128)(2,1)S(1)} %get-tuple-element.69.refs_0_.refs_1_, bf16[128,384]{1,0:T(8,128)(2,1)S(1)} %get-tuple-element.71.refs_2_, bf16[256,2048]{1,0:T(8,128)(2,1)S(1)} %get-tuple-element.100.refs_3_, ...), custom_call_target="tpu_custom_call" | custom-call | flops 11500000256 | tf_op jit(solution)/shard_map/pallas_call | solution.py:330
  52.2 2.8 %shard_map.124 = (bf16[1,2048,384]{2,1,0:T(8,128)(2,1)}, bf16[1,2048,384]{2,1,0:T(8,128)(2,1)}) custom-call(bf16[128,2176]{1,0:T(8,128)(2,1)S(1)} %shard_map.113.refs_1_.refs_0_, bf16[128,2176]{1,0:T(8,128)(2,1)S(1)} %collective-permute-done.4.refs_2_.refs_1_, bf16[128,2176]{1,0:T(8,128)(2,1)S(1)} %collective-permute-done.6.refs_1_.refs_2_, ...), custom_call_target="tpu_custom_call" | custom-call | flops 11500000256 | tf_op jit(solution)/shard_map/pallas_call | solution.py:330
  56.3 1.7 %collective-permute-start.24 = (bf16[64,2048]{1,0:T(8,128)(2,1)S(1)}, bf16[64,2048]{1,0:T(8,128)(2,1)S(1)}, u32[]{:S(2)}, u32[]{:S(2)}) collective-permute-start(bf16[64,2048]{1,0:T(8,128)(2,1)S(1)} %slice.55), channel_id=1, source_target_pairs={{0,8},{1,9},{2,10},{3,11},{4,20},{5,21},{6,22},{7,23},{8,0},{9,1},... | collective-permute-start | bytes 786440 | tf_op jit(solution)/shard_map/ppermute | solution.py:39
  58.7 2.2 %collective-permute-start.19 = (bf16[16,2048]{1,0:T(8,128)(2,1)S(1)}, bf16[16,2048]{1,0:T(8,128)(2,1)S(1)}, u32[]{:S(2)}, u32[]{:S(2)}) collective-permute-start(bf16[16,2048]{1,0:T(8,128)(2,1)S(1)} %get-tuple-element.108), channel_id=1, source_target_pairs={{0,2},{1,3},{2,0},{3,1},{4,6},{5,7},{6,4},{7,5},{8,10},{9,11},{10,... | collective-permute-start | bytes 196616 | tf_op jit(solution)/shard_map/ppermute | solution.py:39
  60.9 1.6 %collective-permute-start.18 = (bf16[16,2048]{1,0:T(8,128)(2,1)S(1)}, bf16[16,2048]{1,0:T(8,128)(2,1)S(1)}, u32[]{:S(2)}, u32[]{:S(2)}) collective-permute-start(bf16[16,2048]{1,0:T(8,128)(2,1)S(1)} %get-tuple-element.106), channel_id=1, source_target_pairs={{0,3},{1,2},{2,1},{3,0},{4,7},{5,6},{6,5},{7,4},{8,11},{9,10},{10,... | collective-permute-start | bytes 196616 | tf_op jit(solution)/shard_map/ppermute | solution.py:39
  63.6 2.2 %collective-permute-start.26 = (bf16[16,2048]{1,0:T(8,128)(2,1)S(1)}, bf16[16,2048]{1,0:T(8,128)(2,1)S(1)}, u32[]{:S(2)}, u32[]{:S(2)}) collective-permute-start(bf16[16,2048]{1,0:T(8,128)(2,1)S(1)} %get-tuple-element.105), channel_id=1, source_target_pairs={{0,2},{1,3},{2,0},{3,1},{4,6},{5,7},{6,4},{7,5},{8,10},{9,11},{10,... | collective-permute-start | bytes 196616 | tf_op jit(solution)/shard_map/ppermute | solution.py:39
  65.9 1.5 %collective-permute-start.25 = (bf16[16,2048]{1,0:T(8,128)(2,1)S(1)}, bf16[16,2048]{1,0:T(8,128)(2,1)S(1)}, u32[]{:S(2)}, u32[]{:S(2)}) collective-permute-start(bf16[16,2048]{1,0:T(8,128)(2,1)S(1)} %get-tuple-element.103), channel_id=1, source_target_pairs={{0,3},{1,2},{2,1},{3,0},{4,7},{5,6},{6,5},{7,4},{8,11},{9,10},{10,... | collective-permute-start | bytes 196616 | tf_op jit(solution)/shard_map/ppermute | solution.py:39
  68.4 2.5 %collective-permute-done.26 = bf16[16,2048]{1,0:T(8,128)(2,1)S(1)} collective-permute-done((bf16[16,2048]{1,0:T(8,128)(2,1)S(1)}, bf16[16,2048]{1,0:T(8,128)(2,1)S(1)}, u32[]{:S(2)}, u32[]{:S(2)}) %collective-permute-start.26) | collective-permute-done | bytes 65568 | tf_op jit(solution)/shard_map/ppermute | solution.py:39
  71.0 1.1 %collective-permute-done.25 = bf16[16,2048]{1,0:T(8,128)(2,1)S(1)} collective-permute-done((bf16[16,2048]{1,0:T(8,128)(2,1)S(1)}, bf16[16,2048]{1,0:T(8,128)(2,1)S(1)}, u32[]{:S(2)}, u32[]{:S(2)}) %collective-permute-start.25) | collective-permute-done | bytes 65568 | tf_op jit(solution)/shard_map/ppermute | solution.py:39
  (52 shorter events, 12.8 us)
Async XLA Ops:
  1.6 8.6 %collective-permute-start = (bf16[16,2176]{1,0:T(8,128)(2,1)S(1)}, bf16[16,2176]{1,0:T(8,128)(2,1)S(1)}, u32[]{:S(2)}, u32[]{:S(2)}) collective-permute-start(bf16[16,2176]{1,0:T(8,128)(2,1)S(1)} %get-tuple-element.61.refs_0_), channel_id=1, source_target_pairs={{0,3},{1,2},{2,1},{3,0},{4,7},{5,6},{6,5},{7,4},{8,11},{9,10},{10,... | collective-permute-start | bytes 208904 | tf_op jit(solution)/shard_map/ppermute | solution.py:39
  6.7 5.9 %collective-permute-start.1 = (bf16[16,2176]{1,0:T(8,128)(2,1)S(1)}, bf16[16,2176]{1,0:T(8,128)(2,1)S(1)}, u32[]{:S(2)}, u32[]{:S(2)}) collective-permute-start(bf16[16,2176]{1,0:T(8,128)(2,1)S(1)} %get-tuple-element.61.refs_0_), channel_id=1, source_target_pairs={{0,2},{1,3},{2,0},{3,1},{4,6},{5,7},{6,4},{7,5},{8,10},{9,11},{10,... | collective-permute-start | bytes 208904 | tf_op jit(solution)/shard_map/ppermute | solution.py:39
  6.7 5.9 %collective-permute-start.2 = (bf16[16,2176]{1,0:T(8,128)(2,1)S(1)}, bf16[16,2176]{1,0:T(8,128)(2,1)S(1)}, u32[]{:S(2)}, u32[]{:S(2)}) collective-permute-start(bf16[16,2176]{1,0:T(8,128)(2,1)S(1)} %get-tuple-element.61.refs_0_), channel_id=1, source_target_pairs={{0,1},{1,0},{2,3},{3,2},{4,5},{5,4},{6,7},{7,6},{8,9},{9,8},{10,11... | collective-permute-start | bytes 208904 | tf_op jit(solution)/shard_map/ppermute | solution.py:39
  12.6 6.6 %collective-permute-start.3 = (bf16[64,2176]{1,0:T(8,128)(2,1)S(1)}, bf16[64,2176]{1,0:T(8,128)(2,1)S(1)}, u32[]{:S(2)}, u32[]{:S(2)}) collective-permute-start(bf16[64,2176]{1,0:T(8,128)(2,1)S(1)} %shard_map.112.refs_0_), channel_id=1, source_target_pairs={{0,8},{1,9},{2,10},{3,11},{4,20},{5,21},{6,22},{7,23},{8,0},{9,1},... | collective-permute-start | bytes 835592 | tf_op jit(solution)/shard_map/ppermute | solution.py:39
  14.2 6.8 %collective-permute-start.7 = (bf16[16,2048]{1,0:T(8,128)(2,1)S(1)}, bf16[16,2048]{1,0:T(8,128)(2,1)S(1)}, u32[]{:S(2)}, u32[]{:S(2)}) collective-permute-start(bf16[16,2048]{1,0:T(8,128)(2,1)S(1)} %get-tuple-element.66.refs_0_), channel_id=1, source_target_pairs={{0,3},{1,2},{2,1},{3,0},{4,7},{5,6},{6,5},{7,4},{8,11},{9,10},{10,... | collective-permute-start | bytes 196616 | tf_op jit(solution)/shard_map/ppermute | solution.py:39
  16.9 6.1 %collective-permute-start.8 = (bf16[16,2048]{1,0:T(8,128)(2,1)S(1)}, bf16[16,2048]{1,0:T(8,128)(2,1)S(1)}, u32[]{:S(2)}, u32[]{:S(2)}) collective-permute-start(bf16[16,2048]{1,0:T(8,128)(2,1)S(1)} %get-tuple-element.66.refs_0_), channel_id=1, source_target_pairs={{0,2},{1,3},{2,0},{3,1},{4,6},{5,7},{6,4},{7,5},{8,10},{9,11},{10,... | collective-permute-start | bytes 196616 | tf_op jit(solution)/shard_map/ppermute | solution.py:39
  16.9 6.1 %collective-permute-start.9 = (bf16[16,2048]{1,0:T(8,128)(2,1)S(1)}, bf16[16,2048]{1,0:T(8,128)(2,1)S(1)}, u32[]{:S(2)}, u32[]{:S(2)}) collective-permute-start(bf16[16,2048]{1,0:T(8,128)(2,1)S(1)} %get-tuple-element.66.refs_0_), channel_id=1, source_target_pairs={{0,1},{1,0},{2,3},{3,2},{4,5},{5,4},{6,7},{7,6},{8,9},{9,8},{10,11... | collective-permute-start | bytes 196616 | tf_op jit(solution)/shard_map/ppermute | solution.py:39
  19.3 12.9 %collective-permute-start.6 = (bf16[128,2176]{1,0:T(8,128)(2,1)S(1)}, bf16[128,2176]{1,0:T(8,128)(2,1)S(1)}, u32[]{:S(2)}, u32[]{:S(2)}) collective-permute-start(bf16[128,2176]{1,0:T(8,128)(2,1)S(1)} %shard_map.113.refs_1_.refs_0_), channel_id=1, source_target_pairs={{0,16},{1,17},{2,18},{3,19},{4,12},{5,13},{6,14},{7,15},{8,24},{9,... | collective-permute-start | bytes 1671176 | tf_op jit(solution)/shard_map/ppermute | solution.py:39
  20.9 3.1 %collective-permute-start.4 = (bf16[128,2176]{1,0:T(8,128)(2,1)S(1)}, bf16[128,2176]{1,0:T(8,128)(2,1)S(1)}, u32[]{:S(2)}, u32[]{:S(2)}) collective-permute-start(bf16[128,2176]{1,0:T(8,128)(2,1)S(1)} %shard_map.113.refs_1_.refs_0_), channel_id=1, source_target_pairs={{0,4},{1,5},{2,6},{3,7},{4,0},{5,1},{6,2},{7,3},{8,12},{9,13},{10,... | collective-permute-start | bytes 1671176 | tf_op jit(solution)/shard_map/ppermute | solution.py:39
  23.1 6.4 %collective-permute-start.10 = (bf16[64,2048]{1,0:T(8,128)(2,1)S(1)}, bf16[64,2048]{1,0:T(8,128)(2,1)S(1)}, u32[]{:S(2)}, u32[]{:S(2)}) collective-permute-start(bf16[64,2048]{1,0:T(8,128)(2,1)S(1)} %shard_map.115.refs_0_), channel_id=1, source_target_pairs={{0,8},{1,9},{2,10},{3,11},{4,20},{5,21},{6,22},{7,23},{8,0},{9,1},... | collective-permute-start | bytes 786440 | tf_op jit(solution)/shard_map/ppermute | solution.py:39
  29.6 9.2 %collective-permute-start.14 = (bf16[128,2048]{1,0:T(8,128)(2,1)S(1)}, bf16[128,2048]{1,0:T(8,128)(2,1)S(1)}, u32[]{:S(2)}, u32[]{:S(2)}) collective-permute-start(bf16[128,2048]{1,0:T(8,128)(2,1)S(1)} %shard_map.116.refs_0_), channel_id=1, source_target_pairs={{0,16},{1,17},{2,18},{3,19},{4,12},{5,13},{6,14},{7,15},{8,24},{9,... | collective-permute-start | bytes 1572872 | tf_op jit(solution)/shard_map/ppermute | solution.py:39
  31.3 17.0 %collective-permute-start.21 = (bf16[128,2048]{1,0:T(8,128)(2,1)S(1)}, bf16[128,2048]{1,0:T(8,128)(2,1)S(1)}, u32[]{:S(2)}, u32[]{:S(2)}) collective-permute-start(bf16[128,2048]{1,0:T(8,128)(2,1)S(1)} %shard_map.116.refs_0_), channel_id=1, source_target_pairs={{0,4},{1,5},{2,6},{3,7},{4,0},{5,1},{6,2},{7,3},{8,12},{9,13},{10,... | collective-permute-start | bytes 1572872 | tf_op jit(solution)/shard_map/ppermute | solution.py:39
  32.2 2.3 %collective-permute-start.11 = (bf16[128,2176]{1,0:T(8,128)(2,1)S(1)}, bf16[128,2176]{1,0:T(8,128)(2,1)S(1)}, u32[]{:S(2)}, u32[]{:S(2)}) collective-permute-start(bf16[128,2176]{1,0:T(8,128)(2,1)S(1)} %collective-permute-done.6.refs_1_.refs_2_), channel_id=1, source_target_pairs={{0,4},{1,5},{2,6},{3,7},{4,0},{5,1},{6,2},{7,3},{8,12},{9,13},{10,... | collective-permute-start | bytes 1671176 | tf_op jit(solution)/shard_map/ppermute | solution.py:39
  32.2 14.8 %collective-permute-start.5 = (bf16[128,2048]{1,0:T(8,128)(2,1)S(1)}, bf16[128,2048]{1,0:T(8,128)(2,1)S(1)}, u32[]{:S(2)}, u32[]{:S(2)}) collective-permute-start(bf16[128,2048]{1,0:T(8,128)(2,1)S(1)} %get-tuple-element.64), channel_id=1, source_target_pairs={{0,4},{1,5},{2,6},{3,7},{4,0},{5,1},{6,2},{7,3},{8,12},{9,13},{10,... | collective-permute-start | bytes 1572872 | tf_op jit(solution)/shard_map/ppermute | solution.py:39
  35.6 2.0 %collective-permute-start.12 = (bf16[128,2048]{1,0:T(8,128)(2,1)S(1)}, bf16[128,2048]{1,0:T(8,128)(2,1)S(1)}, u32[]{:S(2)}, u32[]{:S(2)}) collective-permute-start(bf16[128,2048]{1,0:T(8,128)(2,1)S(1)} %get-tuple-element.73), channel_id=1, source_target_pairs={{0,4},{1,5},{2,6},{3,7},{4,0},{5,1},{6,2},{7,3},{8,12},{9,13},{10,... | collective-permute-start | bytes 1572872 | tf_op jit(solution)/shard_map/ppermute | solution.py:39
  37.7 9.2 %collective-permute-start.13 = (bf16[128,2048]{1,0:T(8,128)(2,1)S(1)}, bf16[128,2048]{1,0:T(8,128)(2,1)S(1)}, u32[]{:S(2)}, u32[]{:S(2)}) collective-permute-start(bf16[128,2048]{1,0:T(8,128)(2,1)S(1)} %add_convert_fusion.3), channel_id=1, source_target_pairs={{0,16},{1,17},{2,18},{3,19},{4,12},{5,13},{6,14},{7,15},{8,24},{9,... | collective-permute-start | bytes 1572872 | tf_op jit(solution)/shard_map/ppermute | solution.py:39
  38.8 1.9 %collective-permute-start.15 = (bf16[128,2048]{1,0:T(8,128)(2,1)S(1)}, bf16[128,2048]{1,0:T(8,128)(2,1)S(1)}, u32[]{:S(2)}, u32[]{:S(2)}) collective-permute-start(bf16[128,2048]{1,0:T(8,128)(2,1)S(1)} %collective-permute-done.14.refs_0_), channel_id=1, source_target_pairs={{0,4},{1,5},{2,6},{3,7},{4,0},{5,1},{6,2},{7,3},{8,12},{9,13},{10,... | collective-permute-start | bytes 1572872 | tf_op jit(solution)/shard_map/ppermute | solution.py:39
  41.9 2.0 %collective-permute-start.16 = (bf16[128,2048]{1,0:T(8,128)(2,1)S(1)}, bf16[128,2048]{1,0:T(8,128)(2,1)S(1)}, u32[]{:S(2)}, u32[]{:S(2)}) collective-permute-start(bf16[128,2048]{1,0:T(8,128)(2,1)S(1)} %get-tuple-element.84), channel_id=1, source_target_pairs={{0,4},{1,5},{2,6},{3,7},{4,0},{5,1},{6,2},{7,3},{8,12},{9,13},{10,... | collective-permute-start | bytes 1572872 | tf_op jit(solution)/shard_map/ppermute | solution.py:39
  44.0 12.1 %collective-permute-start.23 = (bf16[128,2048]{1,0:T(8,128)(2,1)S(1)}, bf16[128,2048]{1,0:T(8,128)(2,1)S(1)}, u32[]{:S(2)}, u32[]{:S(2)}) collective-permute-start(bf16[128,2048]{1,0:T(8,128)(2,1)S(1)} %add_convert_fusion.2), channel_id=1, source_target_pairs={{0,16},{1,17},{2,18},{3,19},{4,12},{5,13},{6,14},{7,15},{8,24},{9,... | collective-permute-start | bytes 1572872 | tf_op jit(solution)/shard_map/ppermute | solution.py:39
  47.2 8.1 %collective-permute-start.17 = (bf16[64,2048]{1,0:T(8,128)(2,1)S(1)}, bf16[64,2048]{1,0:T(8,128)(2,1)S(1)}, u32[]{:S(2)}, u32[]{:S(2)}) collective-permute-start(bf16[64,2048]{1,0:T(8,128)(2,1)S(1)} %slice.49), channel_id=1, source_target_pairs={{0,8},{1,9},{2,10},{3,11},{4,20},{5,21},{6,22},{7,23},{8,0},{9,1},... | collective-permute-start | bytes 786440 | tf_op jit(solution)/shard_map/ppermute | solution.py:39
  50.3 5.7 %collective-permute-start.22 = (bf16[128,2048]{1,0:T(8,128)(2,1)S(1)}, bf16[128,2048]{1,0:T(8,128)(2,1)S(1)}, u32[]{:S(2)}, u32[]{:S(2)}) collective-permute-start(bf16[128,2048]{1,0:T(8,128)(2,1)S(1)} %get-tuple-element.91), channel_id=1, source_target_pairs={{0,4},{1,5},{2,6},{3,7},{4,0},{5,1},{6,2},{7,3},{8,12},{9,13},{10,... | collective-permute-start | bytes 1572872 | tf_op jit(solution)/shard_map/ppermute | solution.py:39
  56.3 6.4 %collective-permute-start.24 = (bf16[64,2048]{1,0:T(8,128)(2,1)S(1)}, bf16[64,2048]{1,0:T(8,128)(2,1)S(1)}, u32[]{:S(2)}, u32[]{:S(2)}) collective-permute-start(bf16[64,2048]{1,0:T(8,128)(2,1)S(1)} %slice.55), channel_id=1, source_target_pairs={{0,8},{1,9},{2,10},{3,11},{4,20},{5,21},{6,22},{7,23},{8,0},{9,1},... | collective-permute-start | bytes 786440 | tf_op jit(solution)/shard_map/ppermute | solution.py:39
  58.1 7.8 %collective-permute-start.20 = (bf16[16,2048]{1,0:T(8,128)(2,1)S(1)}, bf16[16,2048]{1,0:T(8,128)(2,1)S(1)}, u32[]{:S(2)}, u32[]{:S(2)}) collective-permute-start(bf16[16,2048]{1,0:T(8,128)(2,1)S(1)} %get-tuple-element.107), channel_id=1, source_target_pairs={{0,1},{1,0},{2,3},{3,2},{4,5},{5,4},{6,7},{7,6},{8,9},{9,8},{10,11... | collective-permute-start | bytes 196616 | tf_op jit(solution)/shard_map/ppermute | solution.py:39
  58.7 8.7 %collective-permute-start.19 = (bf16[16,2048]{1,0:T(8,128)(2,1)S(1)}, bf16[16,2048]{1,0:T(8,128)(2,1)S(1)}, u32[]{:S(2)}, u32[]{:S(2)}) collective-permute-start(bf16[16,2048]{1,0:T(8,128)(2,1)S(1)} %get-tuple-element.108), channel_id=1, source_target_pairs={{0,2},{1,3},{2,0},{3,1},{4,6},{5,7},{6,4},{7,5},{8,10},{9,11},{10,... | collective-permute-start | bytes 196616 | tf_op jit(solution)/shard_map/ppermute | solution.py:39
  60.9 6.8 %collective-permute-start.18 = (bf16[16,2048]{1,0:T(8,128)(2,1)S(1)}, bf16[16,2048]{1,0:T(8,128)(2,1)S(1)}, u32[]{:S(2)}, u32[]{:S(2)}) collective-permute-start(bf16[16,2048]{1,0:T(8,128)(2,1)S(1)} %get-tuple-element.106), channel_id=1, source_target_pairs={{0,3},{1,2},{2,1},{3,0},{4,7},{5,6},{6,5},{7,4},{8,11},{9,10},{10,... | collective-permute-start | bytes 196616 | tf_op jit(solution)/shard_map/ppermute | solution.py:39
  62.9 5.5 %collective-permute-start.27 = (bf16[16,2048]{1,0:T(8,128)(2,1)S(1)}, bf16[16,2048]{1,0:T(8,128)(2,1)S(1)}, u32[]{:S(2)}, u32[]{:S(2)}) collective-permute-start(bf16[16,2048]{1,0:T(8,128)(2,1)S(1)} %get-tuple-element.104), channel_id=1, source_target_pairs={{0,1},{1,0},{2,3},{3,2},{4,5},{5,4},{6,7},{7,6},{8,9},{9,8},{10,11... | collective-permute-start | bytes 196616 | tf_op jit(solution)/shard_map/ppermute | solution.py:39
  63.6 7.3 %collective-permute-start.26 = (bf16[16,2048]{1,0:T(8,128)(2,1)S(1)}, bf16[16,2048]{1,0:T(8,128)(2,1)S(1)}, u32[]{:S(2)}, u32[]{:S(2)}) collective-permute-start(bf16[16,2048]{1,0:T(8,128)(2,1)S(1)} %get-tuple-element.105), channel_id=1, source_target_pairs={{0,2},{1,3},{2,0},{3,1},{4,6},{5,7},{6,4},{7,5},{8,10},{9,11},{10,... | collective-permute-start | bytes 196616 | tf_op jit(solution)/shard_map/ppermute | solution.py:39
  65.9 6.2 %collective-permute-start.25 = (bf16[16,2048]{1,0:T(8,128)(2,1)S(1)}, bf16[16,2048]{1,0:T(8,128)(2,1)S(1)}, u32[]{:S(2)}, u32[]{:S(2)}) collective-permute-start(bf16[16,2048]{1,0:T(8,128)(2,1)S(1)} %get-tuple-element.103), channel_id=1, source_target_pairs={{0,3},{1,2},{2,1},{3,0},{4,7},{5,6},{6,5},{7,4},{8,11},{9,10},{10,... | collective-permute-start | bytes 196616 | tf_op jit(solution)/shard_map/ppermute | solution.py:39

commit v4 on v3

--- a/solution.py
+++ b/solution.py
@@ -171,17 +171,19 @@
         return nt(gate, self.refs[0][0]) + nt(up, self.refs[1][0])
 
 
-def join_kernel(*refs):
-    at = 0
-    for ref in refs[:-1]:
-        refs[-1][at : at + ref.shape[0], :] = ref[...]
-        at += ref.shape[0]
-
-
-def join(*arrays, length=0.0):
+def join_kernel(blocks, *refs):
+    at, out = 0, refs[-1]
+    for i in range(blocks):
+        for ref in refs[:-1]:
+            size = ref.shape[0] // blocks
+            out[at : at + size, :] = ref[i * size : (i + 1) * size, :]
+            at += size
+
+
+def join(*arrays, blocks=1, length=0.0):
     rows = sum(a.shape[0] for a in arrays)
     return pl.pallas_call(
-        join_kernel,
+        functools.partial(join_kernel, blocks),
         in_specs=[WHOLE] * len(arrays),
         out_specs=WHOLE,
         out_shape=pltpu.VMEM((rows, arrays[0].shape[1]), BF16),
@@ -190,9 +192,57 @@
     )(*arrays)
 
 
+def split_sum_kernel(blocks, *refs):
+    arrays, outs = refs[:-2], refs[-2:]
+    half = outs[0].shape[0] // blocks
+    for i in range(blocks):
+        for j, out in enumerate(outs):
+            rows = pl.ds((2 * i + j) * half, half)
+            total = functools.reduce(lambda x, y: x + y, [r[rows, :].astype(F32) for r in arrays])
+            out[i * half : (i + 1) * half, :] = total.astype(BF16)
+
+
+def split_sum(blocks, *arrays):
+    rows, width = arrays[0].shape
+    return pl.pallas_call(
+        functools.partial(split_sum_kernel, blocks),
+        in_specs=[WHOLE] * len(arrays),
+        out_specs=[WHOLE] * 2,
+        out_shape=[pltpu.VMEM((rows // 2, width), BF16)] * 2,
+        compiler_params=params(4),
+        cost_estimate=cost(0.0),
+    )(*arrays)
+
+
 def grid_specs(block, arrays, whole):
     specs = [pl.BlockSpec((block * f, w), lambda i: (i, 0)) for f, w in arrays]
     return specs + [pl.BlockSpec(w.shape, lambda i: (0, 0, 0)) for w in whole]
+
+
+def last_sums_kernel(counts, *refs):
+    taken, results, held, sems = refs[: sum(counts)], refs[-5:-3], refs[-3:-1], refs[-1]
+    copies = []
+    for i, count in enumerate(counts):
+        total = functools.reduce(lambda x, y: x + y, [r[...].astype(F32) for r in taken[:count]])
+        taken = taken[count:]
+        held[i][...] = total.astype(BF16)
+        copies.append(pltpu.make_async_copy(held[i], results[i], sems.at[i]))
+        copies[i].start()
+    for copy in copies:
+        copy.wait()
+
+
+def last_sums(*groups):
+    shape = groups[0][0].shape
+    return pl.pallas_call(
+        functools.partial(last_sums_kernel, [len(g) for g in groups]),
+        in_specs=[WHOLE] * sum(len(g) for g in groups),
+        out_specs=[ANY] * len(groups),
+        out_shape=shaped(*[(shape, BF16)] * len(groups)),
+        scratch_shapes=[pltpu.VMEM(shape, BF16)] * len(groups) + [pltpu.SemaphoreType.DMA((len(groups),))],
+        compiler_params=params(4),
+        cost_estimate=cost(0.0),
+    )(*[a for g in groups for a in g])
 
 
 def over_rows(kernel, n, scalars, taken, weights, given, length=0.0):
@@ -227,23 +277,28 @@
     return jnp.sum(jnp.where(mine, table.astype(F32), 0.0), axis=1, keepdims=True)
 
 
-def hidden_units(x, weights, act, gate_f, up_f):
+def hidden_values(x, weights):
     gate, up = weights.hidden(x)
     s = jax.nn.sigmoid(gate)
     gate_s = gate * s
-    act_val = (gate_s * up).astype(BF16)
-    act[...] = act_val
-    up_f[...] = gate_s
-    gate_f[...] = up * s * (1.0 + gate * (1.0 - s))
-    return act_val
-
-
-def forward_pair_kernel(experts, width, expert, a, b, weights, kept, given, act, gate_f, up_f, weight):
+    return (gate_s * up).astype(BF16), up * s * (1.0 + gate * (1.0 - s)), gate_s
+
+
+def hidden_units(x, weights, act, gate_f, up_f):
+    values = hidden_values(x, weights)
+    act[...], gate_f[...], up_f[...] = values
+    return values[0]
+
+
+def forward_pair_kernel(experts, width, expert, a, b, weights, kept, given, *units):
     n = a.shape[0]
     x = jnp.concatenate((a[:, :width], b[:, :width]))
     p = expert_weight(experts, expert, jnp.concatenate((a[:, width:], b[:, width:])))
-    weight[...] = jnp.broadcast_to(p, weight.shape)
-    out = p * weights.out(hidden_units(x, weights, act, gate_f, up_f))
+    values = hidden_values(x, weights)
+    out = p * weights.out(values[0])
+    for i, value in enumerate((*values, jnp.broadcast_to(p, (2 * n, 128)))):
+        units[i][...] = value[:n]
+        units[i + 4][...] = value[n:]
     kept[...] = out[:n].astype(BF16)
     given[...] = out[n:].astype(BF16)
 
@@ -272,14 +327,6 @@
     up = (act_cot * up_f[...]).astype(BF16)
     gate_cot[...], up_cot[...] = gate, up
     return gate, up
-
-
-def backward_pair_kernel(a, b, weight, gate_f, up_f, weights, kept, given, gate_cot, up_cot, out_cot):
-    n = a.shape[0]
-    cot = jnp.concatenate((a[...], b[...]))
-    part = weights.row_cot(*hidden_cots(cot, weight, gate_f, up_f, weights, gate_cot, up_cot, out_cot))
-    kept[...] = part[:n].astype(BF16)
-    given[...] = part[n:].astype(BF16)
 
 
 def backward_hidden_kernel(cot, weight, gate_f, up_f, weights, gate_cot, up_cot, out_cot):
@@ -414,13 +461,13 @@
     staged = n_ex * rows * 2 <= BLOCK
     if staged:
         weights = stage(*(after(w, own) for w in weights))
-    row_lane = join(after(own, weights[0]), *[send(own, p) for p in line])
+    for p in plane[:-1]:
+        cot = join(cot, send(cot, p))
+    row_lane = join(after(own, weights[0], cot), *[send(own, p) for p in line])
     cot = after(cot, row_lane)
     cot_lane = join(cot, *[send(cot, p) for p in line], length=10.0)
-    for p in plane[:-2]:
-        row_lane = join(row_lane, send(row_lane, p))
-        cot_lane = join(cot_lane, send(cot_lane, p))
-    row_lane = join(row_lane, send(row_lane, plane[-2]))
+    for p in plane[:-1]:
+        row_lane = join(row_lane, send(row_lane, p), blocks=n_ex)
     n = row_lane.shape[0]
     row_late = send(row_lane, plane[-1])
     row_other = send(row_lane, core)
@@ -429,15 +476,19 @@
         return functools.partial(kernel, experts, width), n, [expert], *args
 
     f_early = over_rows(
-        *forward(forward_pair_kernel, [(1, row_lane), (1, row_other)], weights, [wide] * 2 + each(2, units))
+        *forward(forward_pair_kernel, [(1, row_lane), (1, row_other)], weights, [wide] * 2 + each(1, units * 2))
     )
     kept, given, *f_early = f_early
-    cot_lane = join(cot_lane, after(send(cot_lane, plane[-2]), kept))
+    f_early = (f_early[:4], f_early[4:])
+    cot_lane = after(cot_lane, kept)
     cot_late = send(cot_lane, plane[-1])
     cot_other = send(cot_lane, core)
 
     def halve(kept, received):
         return add(kept, received).astype(BF16)
+
+    def with_units(f):
+        return [(1, f[3]), (1, f[1]), (1, f[2])]
 
     row_late = after(row_late, cot_lane)
     row_late_other = send(row_late, core)
@@ -448,50 +499,52 @@
     o_other = send(o_given, core)
     taken = [(1, f_own[0]), (1, after(f_own[3], f_other[0]))]
     (o_own,) = over_rows(forward_out_kernel, n, [], taken, weights, [wide], 10.0)
-    o_late = halve(o_own, o_other)
+    taken = [(1, after(cot_lane, f_other[0]))] + with_units(f_early[0])
+    *b_early, g_kept = over_rows(backward_full_kernel, n, [], taken, weights, each(1, cots) + [wide], 10.0)
+    o_late = halve(o_own, after(o_other, g_kept))
     o_early_other = send(given, core)
     o_back = send(o_late, plane[-1])
 
-    def with_units(cot, factor, f):
-        return [(factor, f[3]), (factor, f[1]), (factor, f[2])]
-
     cot_late = after(cot_late, o_late)
     cot_late_other = send(cot_late, core)
-    taken = [(1, cot_late)] + with_units(cot_late, 1, f_own)
+    taken = [(1, cot_late)] + with_units(f_own)
     b_own = over_rows(backward_hidden_kernel, n, [], taken, weights, each(1, cots), 10.0)
-    taken = [(1, cot_late_other)] + with_units(cot_late_other, 1, f_other)
+    taken = [(1, after(cot_other, b_own[0]))] + with_units(f_early[1])
+    *b_early_other, g_early = over_rows(backward_full_kernel, n, [], taken, weights, each(1, cots) + [wide], 10.0)
+    taken = [(1, after(cot_late_other, g_early))] + with_units(f_other)
     *b_other, g_given = over_rows(backward_full_kernel, n, [], taken, weights, each(1, cots) + [wide], 10.0)
     g_other = send(g_given, core)
     taken = [(1, b_own[0]), (1, after(b_own[1], b_other[0]))]
     (g_own,) = over_rows(backward_rows_kernel, n, [], taken, weights, [wide], 10.0)
     g_late = halve(g_own, g_other)
-    cot_other = after(cot_other, g_late)
-    taken = [(1, cot_lane), (1, cot_other)] + with_units(cot_lane, 2, f_early)
-    g_kept, g_given, *b_early = over_rows(
-        backward_pair_kernel, n, [], taken, weights, [wide] * 2 + each(2, cots), 10.0
-    )
-    g_early_other = send(g_given, core)
+    g_early_other = send(g_early, core)
     g_back = send(g_late, plane[-1])
     o_back = after(o_back, g_late)
 
-    def finish(lane):
-        for p in reversed(plane[:-1]):
-            half = lane.shape[0] // 2
-            lane = halve(lane[:half], send(lane[half:], p))
-        terms = [lane[:rows]]
-        for j, p in enumerate(line, 1):
-            terms.append(send(lane[j * rows : (j + 1) * rows], p))
-        return add(*terms).astype(BF16)
-
-    mixed = finish(add(kept, o_early_other, o_back).astype(BF16))
-    token_grad = finish(add(g_kept, g_early_other, g_back).astype(BF16))
+    def line_sends(lane):
+        rows = lane.shape[0] // n_ex
+        return [lane[:rows]] + [send(lane[j * rows : (j + 1) * rows], p) for j, p in enumerate(line, 1)]
 
     steps = max(1, n // BLOCK)
-    lefts = [after(row_lane, g_late), row_other, row_late, row_late_other]
-    gate_cots, up_cots, out_cots = zip(b_early, b_own, b_other)
+    gate_cots, up_cots, out_cots = zip(b_early, b_early_other, b_own, b_other)
+
+    parts = (g_kept, g_early_other, g_back)
+    for p in reversed(plane[:-1]):
+        g_lane, g_sent = split_sum(n_ex, *parts)
+        parts = (g_lane, send(g_sent, p))
+    lefts = [after(row_lane, g_sent), row_other, row_late, row_late_other]
     gate_grad, up_grad = gradients(lefts, [gate_cots, up_cots], width, steps)
-    acts = [after(f_early[0], g_late), f_own[0], f_other[0]]
+    acts = [after(f_early[0][0], g_sent), f_early[1][0], f_own[0], f_other[0]]
     (down_grad,) = gradients(acts, [out_cots], hidden, steps)
+    g_lane = add(parts[0], after(parts[1], gate_grad, down_grad)).astype(BF16)
+    g_terms = line_sends(g_lane)
+    o_terms = line_sends(add(kept, o_early_other, o_back).astype(BF16))
+    parts = (join(after(o_terms[0], g_lane), length=20.0), *o_terms[1:])
+    for p in reversed(plane[:-1]):
+        lane = add(*parts).astype(BF16)
+        half = lane.shape[0] // 2
+        parts = (lane[:half], send(lane[half:], p))
+    mixed, token_grad = last_sums(parts, g_terms)
     return mixed, token_grad, gate_grad, up_grad, down_grad
 
 

time: 72.9 us -> 70.3 us (0.964)
  other arithmetic: 2.2 us -> 0.66 us
  Pallas kernels: 17 us -> 18.5 us
  starting transfers between devices: 32.6 us -> 31.2 us
  waiting for transfers between devices: 20 us -> 18.7 us
    convert_element_type x4 -> x3, other arithmetic: 1.81 us -> 0.38 us  [the longest x1 0.24 us: body(): o_terms = line_sends(add(kept, o_early_other, o_back).astype(BF16))]
    ppermute x28, starting transfers between devices: 32.6 us -> 31.2 us  [send(): return lax.ppermute(x, AXES, pairs)]
    ppermute x28, waiting for transfers between devices: 20 us -> 18.7 us  [send(): return lax.ppermute(x, AXES, pairs)]
    pallas_call x4 -> x7, Pallas kernels: 0.11 us -> 1 us  [the longest x1 0.7 us: last_sums(): pl.pallas_call(functools.partial(last_sums_kernel, [len(g) for g in group...]
    pallas_call x8 -> x9, Pallas kernels: 8.56 us -> 8.94 us  [over_rows(): pl.pallas_call(run, out_shape=shaped(*[((f * n, w), t) for f, w, t in giv...]
  transfers between devices with their start and end apart: 28 -> 28, of which waited for: 17 -> 13; matrix products, arithmetic and copies ran while one was open for 2% -> 1% of each run, Pallas kernels for 22% -> 24%
where the time goes in v4:
time: 70.3 us; the launch traced here: 70.2 us
  starting transfers between devices  31.2 us (44%)
  waiting for transfers between devices  18.7 us (27%)
  Pallas kernels  18.5 us (26%)
  between operations  1.05 us (1%)
    ppermute x28, starting transfers between devices, send(): return lax.ppermute(x, AXES, pairs)  31.2 us
    ppermute x28, waiting for transfers between devices, send(): return lax.ppermute(x, AXES, pairs)  18.7 us
    pallas_call x9, Pallas kernels, over_rows(): pl.pallas_call(run, out_shape=shaped(*[((f * n, w), t) for f, w, t in giv...  8.94 us
    pallas_call x2, Pallas kernels, gradients_by_chunks(): pl.pallas_call(functools.partial(chunk_kernel, over_left, chunks, [len(g)...  4.8 us
    pallas_call x1, Pallas kernels, stage(): pl.pallas_call(stage_kernel, in_specs=[ANY] * 3, out_specs=[WHOLE] * 2, o...  2.86 us
  transfers between devices with their start and end apart: 28, of which 13 were waited for; matrix products, arithmetic and copies ran while one was open for 1% of the time, Pallas kernels for 24%

profile of v4, /device:TPU:0, one launch (start us, length us, event | category | flops | bytes accessed | tf_op | source)
XLA Modules:
  0.0 70.2 jit_solution(17553813969336618742)
XLA Ops:
  1.6 3.1 %collective-permute-start.3 = (bf16[16,2176]{1,0:T(8,128)(2,1)S(1)}, bf16[16,2176]{1,0:T(8,128)(2,1)S(1)}, u32[]{:S(2)}, u32[]{:S(2)}) collective-permute-start(bf16[16,2176]{1,0:T(8,128)(2,1)S(1)} %get-tuple-element.78.refs_0_), channel_id=1, source_target_pairs={{0,1},{1,0},{2,3},{3,2},{4,5},{5,4},{6,7},{7,6},{8,9},{9,8},{10,11... | collective-permute-start | bytes 208904 | tf_op jit(solution)/shard_map/ppermute | solution.py:39
  4.7 2.6 %collective-permute-start.2 = (bf16[16,2176]{1,0:T(8,128)(2,1)S(1)}, bf16[16,2176]{1,0:T(8,128)(2,1)S(1)}, u32[]{:S(2)}, u32[]{:S(2)}) collective-permute-start(bf16[16,2176]{1,0:T(8,128)(2,1)S(1)} %get-tuple-element.78.refs_0_), channel_id=1, source_target_pairs={{0,2},{1,3},{2,0},{3,1},{4,6},{5,7},{6,4},{7,5},{8,10},{9,11},{10,... | collective-permute-start | bytes 208904 | tf_op jit(solution)/shard_map/ppermute | solution.py:39
  7.3 1.7 %collective-permute-start = (bf16[16,2048]{1,0:T(8,128)(2,1)S(1)}, bf16[16,2048]{1,0:T(8,128)(2,1)S(1)}, u32[]{:S(2)}, u32[]{:S(2)}) collective-permute-start(bf16[16,2048]{1,0:T(8,128)(2,1)S(1)} %get-tuple-element.77.refs_0_), channel_id=1, source_target_pairs={{0,8},{1,9},{2,10},{3,11},{4,20},{5,21},{6,22},{7,23},{8,0},{9,1},... | collective-permute-start | bytes 196616 | tf_op jit(solution)/shard_map/ppermute | solution.py:39
  9.0 2.9 %shard_map.111 = (bf16[3,2048,384]{2,1,0:T(8,128)(2,1)S(1)}, bf16[3,384,2048]{2,1,0:T(8,128)(2,1)S(1)}) custom-call(bf16[1,2048,384]{2,1,0:T(8,128)(2,1)} %gate, bf16[1,2048,384]{2,1,0:T(8,128)(2,1)} %up, bf16[1,384,2048]{2,1,0:T(8,128)(2,1)} %down), custom_call_target="tpu_custom_call" | custom-call | tf_op jit(solution)/shard_map/pallas_call | solution.py:142
  12.2 1.3 %collective-permute-done.1.refs_1_ = bf16[16,2176]{1,0:T(8,128)(2,1)S(1)} collective-permute-done((bf16[16,2176]{1,0:T(8,128)(2,1)S(1)}, bf16[16,2176]{1,0:T(8,128)(2,1)S(1)}, u32[]{:S(2)}, u32[]{:S(2)}) %collective-permute-start.1) | collective-permute-done | bytes 69664 | tf_op jit(solution)/shard_map/ppermute | solution.py:39
  13.5 1.6 %collective-permute-start.4 = (bf16[64,2176]{1,0:T(8,128)(2,1)S(1)}, bf16[64,2176]{1,0:T(8,128)(2,1)S(1)}, u32[]{:S(2)}, u32[]{:S(2)}) collective-permute-start(bf16[64,2176]{1,0:T(8,128)(2,1)S(1)} %shard_map.113.refs_0_), channel_id=1, source_target_pairs={{0,8},{1,9},{2,10},{3,11},{4,20},{5,21},{6,22},{7,23},{8,0},{9,1},... | collective-permute-start | bytes 835592 | tf_op jit(solution)/shard_map/ppermute | solution.py:39
  15.8 1.7 %collective-permute-start.9 = (bf16[32,2048]{1,0:T(8,128)(2,1)S(1)}, bf16[32,2048]{1,0:T(8,128)(2,1)S(1)}, u32[]{:S(2)}, u32[]{:S(2)}) collective-permute-start(bf16[32,2048]{1,0:T(8,128)(2,1)S(1)} %shard_map.112.refs_0_), channel_id=1, source_target_pairs={{0,2},{1,3},{2,0},{3,1},{4,6},{5,7},{6,4},{7,5},{8,10},{9,11},{10,... | collective-permute-start | bytes 393224 | tf_op jit(solution)/shard_map/ppermute | solution.py:39
  17.6 1.9 %collective-permute-start.8 = (bf16[32,2048]{1,0:T(8,128)(2,1)S(1)}, bf16[32,2048]{1,0:T(8,128)(2,1)S(1)}, u32[]{:S(2)}, u32[]{:S(2)}) collective-permute-start(bf16[32,2048]{1,0:T(8,128)(2,1)S(1)} %shard_map.112.refs_0_), channel_id=1, source_target_pairs={{0,3},{1,2},{2,1},{3,0},{4,7},{5,6},{6,5},{7,4},{8,11},{9,10},{10,... | collective-permute-start | bytes 393224 | tf_op jit(solution)/shard_map/ppermute | solution.py:39
  20.2 1.6 %collective-permute-start.7 = (bf16[128,2176]{1,0:T(8,128)(2,1)S(1)}, bf16[128,2176]{1,0:T(8,128)(2,1)S(1)}, u32[]{:S(2)}, u32[]{:S(2)}) collective-permute-start(bf16[128,2176]{1,0:T(8,128)(2,1)S(1)} %shard_map.114.refs_1_.refs_0_), channel_id=1, source_target_pairs={{0,16},{1,17},{2,18},{3,19},{4,12},{5,13},{6,14},{7,15},{8,24},{9,... | collective-permute-start | bytes 1671176 | tf_op jit(solution)/shard_map/ppermute | solution.py:39
  21.8 5.3 %collective-permute-done.9.refs_2_ = bf16[32,2048]{1,0:T(8,128)(2,1)S(1)} collective-permute-done((bf16[32,2048]{1,0:T(8,128)(2,1)S(1)}, bf16[32,2048]{1,0:T(8,128)(2,1)S(1)}, u32[]{:S(2)}, u32[]{:S(2)}) %collective-permute-start.9) | collective-permute-done | bytes 131104 | tf_op jit(solution)/shard_map/ppermute | solution.py:39
  27.2 1.9 %shard_map.115 = (bf16[128,2048]{1,0:T(8,128)(2,1)S(1)}, bf16[128,2048]{1,0:T(8,128)(2,1)S(1)}, bf16[128,384]{1,0:T(8,128)(2,1)S(1)}, f32[128,384]{1,0:T(8,128)S...) custom-call(s32[1,1]{1,0:T(1,128)} %bitcast.refs_0_, ...), custom_call_target="tpu_custom_call" | custom-call | tf_op jit(solution)/shard_map/pallas_call | solution.py:264
  29.8 1.1 %collective-permute-start.6 = (bf16[128,2048]{1,0:T(8,128)(2,1)S(1)}, bf16[128,2048]{1,0:T(8,128)(2,1)S(1)}, u32[]{:S(2)}, u32[]{:S(2)}) collective-permute-start(bf16[128,2048]{1,0:T(8,128)(2,1)S(1)} %get-tuple-element.81), channel_id=1, source_target_pairs={{0,4},{1,5},{2,6},{3,7},{4,0},{5,1},{6,2},{7,3},{8,12},{9,13},{10,... | collective-permute-start | bytes 1572872 | tf_op jit(solution)/shard_map/ppermute | solution.py:39
  31.6 1.6 %collective-permute-done.11.refs_1_.refs_3_ = bf16[128,2176]{1,0:T(8,128)(2,1)S(1)} collective-permute-done((bf16[128,2176]{1,0:T(8,128)(2,1)S(1)}, bf16[128,2176]{1,0:T(8,128)(2,1)S(1)}, u32[]{:S(2)}, u32[]{:S(2)}) %collective-permute-start.11) | collective-permute-done | bytes 557088 | tf_op jit(solution)/shard_map/ppermute | solution.py:39
  33.2 1.1 %shard_map.118 = (bf16[128,384]{1,0:T(8,128)(2,1)S(1)}, f32[128,384]{1,0:T(8,128)S(1)}, f32[128,384]{1,0:T(8,128)S(1)}, f32[128,128]{1,0:T(8,128)S(1)}, bf16[128,2048]{1,0:T(8,128)(2,1)S(1)}) custom-call(s32[1,1]{1,0:T(1,128)} %bitcast.refs_0_, bf16[128,2176]{1,0:T(8,128)(2,1)S(1)} %collective-permute-done.11.refs_1_.refs_3_, ...), custom_call_target="tpu_custom_call" | custom-call | flops 11500000256 | tf_op jit(solution)/shard_map/pallas_call | solution.py:264
  35.2 1.2 %shard_map.120 = (bf16[128,384]{1,0:T(8,128)(2,1)S(1)}, bf16[128,384]{1,0:T(8,128)(2,1)S(1)}, bf16[128,2048]{1,0:T(8,128)(2,1)S(1)}, bf16[128,2048]{1,0:T(8,128)(2,1)S(1)}) custom-call(bf16[128,2048]{1,0:T(8,128)(2,1)S(1)} %shard_map.116.refs_0_, f32[128,128]{1,0:T(8,128)S(1)} %get-tuple-element.91.refs_1_, f32[128,384]{1,0:T(8,128)S(1)} %get-tuple-element.92.refs_2_, ...), custom_call_target="tpu_custom_call" | custom-call | flops 11500000256 | tf_op jit(solution)/shard_map/pallas_call | solution.py:264
  37.3 1.1 %collective-permute-done.14.refs_0_ = bf16[128,2048]{1,0:T(8,128)(2,1)S(1)} collective-permute-done((bf16[128,2048]{1,0:T(8,128)(2,1)S(1)}, bf16[128,2048]{1,0:T(8,128)(2,1)S(1)}, u32[]{:S(2)}, u32[]{:S(2)}) %collective-permute-start.14) | collective-permute-done | bytes 524320 | tf_op jit(solution)/shard_map/ppermute | solution.py:39
  38.9 1.2 %shard_map.122 = (bf16[128,384]{1,0:T(8,128)(2,1)S(1)}, bf16[128,384]{1,0:T(8,128)(2,1)S(1)}, bf16[128,2048]{1,0:T(8,128)(2,1)S(1)}, bf16[128,2048]{1,0:T(8,128)(2,1)S(1)}) custom-call(bf16[128,2048]{1,0:T(8,128)(2,1)S(1)} %collective-permute-done.16.refs_0_, f32[128,128]{1,0:T(8,128)S(1)} %get-tuple-element.102.refs_1_, ...), custom_call_target="tpu_custom_call" | custom-call | flops 11500000256 | tf_op jit(solution)/shard_map/pallas_call | solution.py:264
  40.7 1.2 %shard_map.123 = (bf16[128,384]{1,0:T(8,128)(2,1)S(1)}, bf16[128,384]{1,0:T(8,128)(2,1)S(1)}, bf16[128,2048]{1,0:T(8,128)(2,1)S(1)}, bf16[128,2048]{1,0:T(8,128)(2,1)S(1)}) custom-call(bf16[128,2048]{1,0:T(8,128)(2,1)S(1)} %collective-permute-done.15.refs_0_, f32[128,128]{1,0:T(8,128)S(1)} %get-tuple-element.107.refs_1_, ...), custom_call_target="tpu_custom_call" | custom-call | flops 11500000256 | tf_op jit(solution)/shard_map/pallas_call | solution.py:264
  42.7 1.2 %collective-permute-done.17 = bf16[128,2048]{1,0:T(8,128)(2,1)S(1)} collective-permute-done((bf16[128,2048]{1,0:T(8,128)(2,1)S(1)}, bf16[128,2048]{1,0:T(8,128)(2,1)S(1)}, u32[]{:S(2)}, u32[]{:S(2)}) %collective-permute-start.17) | collective-permute-done | bytes 524320 | tf_op jit(solution)/shard_map/ppermute | solution.py:39
  44.6 1.2 %collective-permute-done.13 = bf16[128,2048]{1,0:T(8,128)(2,1)S(1)} collective-permute-done((bf16[128,2048]{1,0:T(8,128)(2,1)S(1)}, bf16[128,2048]{1,0:T(8,128)(2,1)S(1)}, u32[]{:S(2)}, u32[]{:S(2)}) %collective-permute-start.13) | collective-permute-done | bytes 524320 | tf_op jit(solution)/shard_map/ppermute | solution.py:39
  46.1 2.0 %collective-permute-start.23 = (bf16[32,2048]{1,0:T(8,128)(2,1)S(1)}, bf16[32,2048]{1,0:T(8,128)(2,1)S(1)}, u32[]{:S(2)}, u32[]{:S(2)}) collective-permute-start(bf16[32,2048]{1,0:T(8,128)(2,1)S(1)} %get-tuple-element.136), channel_id=1, source_target_pairs={{0,1},{1,0},{2,3},{3,2},{4,5},{5,4},{6,7},{7,6},{8,9},{9,8},{10,11... | collective-permute-start | bytes 393224 | tf_op jit(solution)/shard_map/ppermute | solution.py:39
  49.1 1.4 %collective-permute-start.21 = (bf16[32,2048]{1,0:T(8,128)(2,1)S(1)}, bf16[32,2048]{1,0:T(8,128)(2,1)S(1)}, u32[]{:S(2)}, u32[]{:S(2)}) collective-permute-start(bf16[32,2048]{1,0:T(8,128)(2,1)S(1)} %get-tuple-element.138), channel_id=1, source_target_pairs={{0,3},{1,2},{2,1},{3,0},{4,7},{5,6},{6,5},{7,4},{8,11},{9,10},{10,... | collective-permute-start | bytes 393224 | tf_op jit(solution)/shard_map/ppermute | solution.py:39
  50.6 2.7 %collective-permute-done.19.refs_2_ = bf16[128,2048]{1,0:T(8,128)(2,1)S(1)} collective-permute-done((bf16[128,2048]{1,0:T(8,128)(2,1)S(1)}, bf16[128,2048]{1,0:T(8,128)(2,1)S(1)}, u32[]{:S(2)}, u32[]{:S(2)}) %collective-permute-start.19) | collective-permute-done | bytes 524320 | tf_op jit(solution)/shard_map/ppermute | solution.py:39
  53.5 1.6 %collective-permute-start.20 = (bf16[64,2048]{1,0:T(8,128)(2,1)S(1)}, bf16[64,2048]{1,0:T(8,128)(2,1)S(1)}, u32[]{:S(2)}, u32[]{:S(2)}) collective-permute-start(bf16[64,2048]{1,0:T(8,128)(2,1)S(1)} %get-tuple-element.115), channel_id=1, source_target_pairs={{0,8},{1,9},{2,10},{3,11},{4,20},{5,21},{6,22},{7,23},{8,0},{9,1},... | collective-permute-start | bytes 786440 | tf_op jit(solution)/shard_map/ppermute | solution.py:39
  55.0 2.0 %shard_map.127 = bf16[1,384,2048]{2,1,0:T(8,128)(2,1)} custom-call(bf16[128,384]{1,0:T(8,128)(2,1)S(1)} %get-tuple-element.124.refs_0_, bf16[128,384]{1,0:T(8,128)(2,1)S(1)} %get-tuple-element.125.refs_1_, bf16[128,384]{1,0:T(8,128)(2,1)S(1)} %get-tuple-element.85.refs_0_.refs_2_, bf16[128,384]{1,0:T(8,128)(2,1)S(1)} %get-tuple-element.87.refs_3_, ...), custom_call_target="tpu_custom_call" | custom-call | flops 11500000256 | tf_op jit(solution)/shard_map/pallas_call | solution.py:377
  57.0 2.8 %shard_map.126 = (bf16[1,2048,384]{2,1,0:T(8,128)(2,1)}, bf16[1,2048,384]{2,1,0:T(8,128)(2,1)}) custom-call(bf16[128,2176]{1,0:T(8,128)(2,1)S(1)} %shard_map.114.refs_1_.refs_0_, bf16[128,2176]{1,0:T(8,128)(2,1)S(1)} %collective-permute-done.5.refs_2_.refs_1_, bf16[128,2176]{1,0:T(8,128)(2,1)S(1)} %collective-permute-done.7.refs_1_.refs_2_, ...), custom_call_target="tpu_custom_call" | custom-call | flops 11500000256 | tf_op jit(solution)/shard_map/pallas_call | solution.py:377
  60.0 2.0 %collective-permute-start.27 = (bf16[16,2048]{1,0:T(8,128)(2,1)S(1)}, bf16[16,2048]{1,0:T(8,128)(2,1)S(1)}, u32[]{:S(2)}, u32[]{:S(2)}) collective-permute-start(bf16[16,2048]{1,0:T(8,128)(2,1)S(1)} %get-tuple-element.139), channel_id=1, source_target_pairs={{0,1},{1,0},{2,3},{3,2},{4,5},{5,4},{6,7},{7,6},{8,9},{9,8},{10,11... | collective-permute-start | bytes 196616 | tf_op jit(solution)/shard_map/ppermute | solution.py:39
  62.0 1.0 %collective-permute-start.26 = (bf16[16,2048]{1,0:T(8,128)(2,1)S(1)}, bf16[16,2048]{1,0:T(8,128)(2,1)S(1)}, u32[]{:S(2)}, u32[]{:S(2)}) collective-permute-start(bf16[16,2048]{1,0:T(8,128)(2,1)S(1)} %get-tuple-element.140), channel_id=1, source_target_pairs={{0,2},{1,3},{2,0},{3,1},{4,6},{5,7},{6,4},{7,5},{8,10},{9,11},{10,... | collective-permute-start | bytes 196616 | tf_op jit(solution)/shard_map/ppermute | solution.py:39
  63.1 1.5 %collective-permute-start.25 = (bf16[16,2048]{1,0:T(8,128)(2,1)S(1)}, bf16[16,2048]{1,0:T(8,128)(2,1)S(1)}, u32[]{:S(2)}, u32[]{:S(2)}) collective-permute-start(bf16[16,2048]{1,0:T(8,128)(2,1)S(1)} %get-tuple-element.141), channel_id=1, source_target_pairs={{0,3},{1,2},{2,1},{3,0},{4,7},{5,6},{6,5},{7,4},{8,11},{9,10},{10,... | collective-permute-start | bytes 196616 | tf_op jit(solution)/shard_map/ppermute | solution.py:39
  64.6 1.6 %collective-permute-start.24 = (bf16[16,2048]{1,0:T(8,128)(2,1)S(1)}, bf16[16,2048]{1,0:T(8,128)(2,1)S(1)}, u32[]{:S(2)}, u32[]{:S(2)}) collective-permute-start(bf16[16,2048]{1,0:T(8,128)(2,1)S(1)} %get-tuple-element.143), channel_id=1, source_target_pairs={{0,8},{1,9},{2,10},{3,11},{4,20},{5,21},{6,22},{7,23},{8,0},{9,1},... | collective-permute-start | bytes 196616 | tf_op jit(solution)/shard_map/ppermute | solution.py:39
  66.2 1.8 %collective-permute-done.26.refs_4_ = bf16[16,2048]{1,0:T(8,128)(2,1)S(1)} collective-permute-done((bf16[16,2048]{1,0:T(8,128)(2,1)S(1)}, bf16[16,2048]{1,0:T(8,128)(2,1)S(1)}, u32[]{:S(2)}, u32[]{:S(2)}) %collective-permute-start.26) | collective-permute-done | bytes 65568 | tf_op jit(solution)/shard_map/ppermute | solution.py:39
  68.0 1.3 %collective-permute-done.25.refs_3_ = bf16[16,2048]{1,0:T(8,128)(2,1)S(1)} collective-permute-done((bf16[16,2048]{1,0:T(8,128)(2,1)S(1)}, bf16[16,2048]{1,0:T(8,128)(2,1)S(1)}, u32[]{:S(2)}, u32[]{:S(2)}) %collective-permute-start.25) | collective-permute-done | bytes 65568 | tf_op jit(solution)/shard_map/ppermute | solution.py:39
  (52 shorter events, 11.2 us)
Async XLA Ops:
  1.6 10.3 %collective-permute-start.3 = (bf16[16,2176]{1,0:T(8,128)(2,1)S(1)}, bf16[16,2176]{1,0:T(8,128)(2,1)S(1)}, u32[]{:S(2)}, u32[]{:S(2)}) collective-permute-start(bf16[16,2176]{1,0:T(8,128)(2,1)S(1)} %get-tuple-element.78.refs_0_), channel_id=1, source_target_pairs={{0,1},{1,0},{2,3},{3,2},{4,5},{5,4},{6,7},{7,6},{8,9},{9,8},{10,11... | collective-permute-start | bytes 208904 | tf_op jit(solution)/shard_map/ppermute | solution.py:39
  4.7 7.5 %collective-permute-start.2 = (bf16[16,2176]{1,0:T(8,128)(2,1)S(1)}, bf16[16,2176]{1,0:T(8,128)(2,1)S(1)}, u32[]{:S(2)}, u32[]{:S(2)}) collective-permute-start(bf16[16,2176]{1,0:T(8,128)(2,1)S(1)} %get-tuple-element.78.refs_0_), channel_id=1, source_target_pairs={{0,2},{1,3},{2,0},{3,1},{4,6},{5,7},{6,4},{7,5},{8,10},{9,11},{10,... | collective-permute-start | bytes 208904 | tf_op jit(solution)/shard_map/ppermute | solution.py:39
  7.3 6.2 %collective-permute-start.1 = (bf16[16,2176]{1,0:T(8,128)(2,1)S(1)}, bf16[16,2176]{1,0:T(8,128)(2,1)S(1)}, u32[]{:S(2)}, u32[]{:S(2)}) collective-permute-start(bf16[16,2176]{1,0:T(8,128)(2,1)S(1)} %get-tuple-element.78.refs_0_), channel_id=1, source_target_pairs={{0,3},{1,2},{2,1},{3,0},{4,7},{5,6},{6,5},{7,4},{8,11},{9,10},{10,... | collective-permute-start | bytes 208904 | tf_op jit(solution)/shard_map/ppermute | solution.py:39
  7.3 4.6 %collective-permute-start = (bf16[16,2048]{1,0:T(8,128)(2,1)S(1)}, bf16[16,2048]{1,0:T(8,128)(2,1)S(1)}, u32[]{:S(2)}, u32[]{:S(2)}) collective-permute-start(bf16[16,2048]{1,0:T(8,128)(2,1)S(1)} %get-tuple-element.77.refs_0_), channel_id=1, source_target_pairs={{0,8},{1,9},{2,10},{3,11},{4,20},{5,21},{6,22},{7,23},{8,0},{9,1},... | collective-permute-start | bytes 196616 | tf_op jit(solution)/shard_map/ppermute | solution.py:39
  13.5 6.7 %collective-permute-start.4 = (bf16[64,2176]{1,0:T(8,128)(2,1)S(1)}, bf16[64,2176]{1,0:T(8,128)(2,1)S(1)}, u32[]{:S(2)}, u32[]{:S(2)}) collective-permute-start(bf16[64,2176]{1,0:T(8,128)(2,1)S(1)} %shard_map.113.refs_0_), channel_id=1, source_target_pairs={{0,8},{1,9},{2,10},{3,11},{4,20},{5,21},{6,22},{7,23},{8,0},{9,1},... | collective-permute-start | bytes 835592 | tf_op jit(solution)/shard_map/ppermute | solution.py:39
  15.1 6.8 %collective-permute-start.10 = (bf16[32,2048]{1,0:T(8,128)(2,1)S(1)}, bf16[32,2048]{1,0:T(8,128)(2,1)S(1)}, u32[]{:S(2)}, u32[]{:S(2)}) collective-permute-start(bf16[32,2048]{1,0:T(8,128)(2,1)S(1)} %shard_map.112.refs_0_), channel_id=1, source_target_pairs={{0,1},{1,0},{2,3},{3,2},{4,5},{5,4},{6,7},{7,6},{8,9},{9,8},{10,11... | collective-permute-start | bytes 393224 | tf_op jit(solution)/shard_map/ppermute | solution.py:39
  15.8 11.3 %collective-permute-start.9 = (bf16[32,2048]{1,0:T(8,128)(2,1)S(1)}, bf16[32,2048]{1,0:T(8,128)(2,1)S(1)}, u32[]{:S(2)}, u32[]{:S(2)}) collective-permute-start(bf16[32,2048]{1,0:T(8,128)(2,1)S(1)} %shard_map.112.refs_0_), channel_id=1, source_target_pairs={{0,2},{1,3},{2,0},{3,1},{4,6},{5,7},{6,4},{7,5},{8,10},{9,11},{10,... | collective-permute-start | bytes 393224 | tf_op jit(solution)/shard_map/ppermute | solution.py:39
  17.6 9.5 %collective-permute-start.8 = (bf16[32,2048]{1,0:T(8,128)(2,1)S(1)}, bf16[32,2048]{1,0:T(8,128)(2,1)S(1)}, u32[]{:S(2)}, u32[]{:S(2)}) collective-permute-start(bf16[32,2048]{1,0:T(8,128)(2,1)S(1)} %shard_map.112.refs_0_), channel_id=1, source_target_pairs={{0,3},{1,2},{2,1},{3,0},{4,7},{5,6},{6,5},{7,4},{8,11},{9,10},{10,... | collective-permute-start | bytes 393224 | tf_op jit(solution)/shard_map/ppermute | solution.py:39
  20.2 9.6 %collective-permute-start.7 = (bf16[128,2176]{1,0:T(8,128)(2,1)S(1)}, bf16[128,2176]{1,0:T(8,128)(2,1)S(1)}, u32[]{:S(2)}, u32[]{:S(2)}) collective-permute-start(bf16[128,2176]{1,0:T(8,128)(2,1)S(1)} %shard_map.114.refs_1_.refs_0_), channel_id=1, source_target_pairs={{0,16},{1,17},{2,18},{3,19},{4,12},{5,13},{6,14},{7,15},{8,24},{9,... | collective-permute-start | bytes 1671176 | tf_op jit(solution)/shard_map/ppermute | solution.py:39
  21.8 5.3 %collective-permute-start.5 = (bf16[128,2176]{1,0:T(8,128)(2,1)S(1)}, bf16[128,2176]{1,0:T(8,128)(2,1)S(1)}, u32[]{:S(2)}, u32[]{:S(2)}) collective-permute-start(bf16[128,2176]{1,0:T(8,128)(2,1)S(1)} %shard_map.114.refs_1_.refs_0_), channel_id=1, source_target_pairs={{0,4},{1,5},{2,6},{3,7},{4,0},{5,1},{6,2},{7,3},{8,12},{9,13},{10,... | collective-permute-start | bytes 1671176 | tf_op jit(solution)/shard_map/ppermute | solution.py:39
  29.1 9.9 %collective-permute-start.16 = (bf16[128,2048]{1,0:T(8,128)(2,1)S(1)}, bf16[128,2048]{1,0:T(8,128)(2,1)S(1)}, u32[]{:S(2)}, u32[]{:S(2)}) collective-permute-start(bf16[128,2048]{1,0:T(8,128)(2,1)S(1)} %shard_map.116.refs_0_), channel_id=1, source_target_pairs={{0,4},{1,5},{2,6},{3,7},{4,0},{5,1},{6,2},{7,3},{8,12},{9,13},{10,... | collective-permute-start | bytes 1572872 | tf_op jit(solution)/shard_map/ppermute | solution.py:39
  29.2 9.2 %collective-permute-start.14 = (bf16[128,2048]{1,0:T(8,128)(2,1)S(1)}, bf16[128,2048]{1,0:T(8,128)(2,1)S(1)}, u32[]{:S(2)}, u32[]{:S(2)}) collective-permute-start(bf16[128,2048]{1,0:T(8,128)(2,1)S(1)} %shard_map.116.refs_0_), channel_id=1, source_target_pairs={{0,16},{1,17},{2,18},{3,19},{4,12},{5,13},{6,14},{7,15},{8,24},{9,... | collective-permute-start | bytes 1572872 | tf_op jit(solution)/shard_map/ppermute | solution.py:39
  29.8 16.0 %collective-permute-start.6 = (bf16[128,2048]{1,0:T(8,128)(2,1)S(1)}, bf16[128,2048]{1,0:T(8,128)(2,1)S(1)}, u32[]{:S(2)}, u32[]{:S(2)}) collective-permute-start(bf16[128,2048]{1,0:T(8,128)(2,1)S(1)} %get-tuple-element.81), channel_id=1, source_target_pairs={{0,4},{1,5},{2,6},{3,7},{4,0},{5,1},{6,2},{7,3},{8,12},{9,13},{10,... | collective-permute-start | bytes 1572872 | tf_op jit(solution)/shard_map/ppermute | solution.py:39
  30.9 2.3 %collective-permute-start.11 = (bf16[128,2176]{1,0:T(8,128)(2,1)S(1)}, bf16[128,2176]{1,0:T(8,128)(2,1)S(1)}, u32[]{:S(2)}, u32[]{:S(2)}) collective-permute-start(bf16[128,2176]{1,0:T(8,128)(2,1)S(1)} %collective-permute-done.7.refs_1_.refs_2_), channel_id=1, source_target_pairs={{0,4},{1,5},{2,6},{3,7},{4,0},{5,1},{6,2},{7,3},{8,12},{9,13},{10,... | collective-permute-start | bytes 1671176 | tf_op jit(solution)/shard_map/ppermute | solution.py:39
  34.3 2.1 %collective-permute-start.12 = (bf16[128,2048]{1,0:T(8,128)(2,1)S(1)}, bf16[128,2048]{1,0:T(8,128)(2,1)S(1)}, u32[]{:S(2)}, u32[]{:S(2)}) collective-permute-start(bf16[128,2048]{1,0:T(8,128)(2,1)S(1)} %get-tuple-element.89), channel_id=1, source_target_pairs={{0,4},{1,5},{2,6},{3,7},{4,0},{5,1},{6,2},{7,3},{8,12},{9,13},{10,... | collective-permute-start | bytes 1572872 | tf_op jit(solution)/shard_map/ppermute | solution.py:39
  36.5 9.2 %collective-permute-start.13 = (bf16[128,2048]{1,0:T(8,128)(2,1)S(1)}, bf16[128,2048]{1,0:T(8,128)(2,1)S(1)}, u32[]{:S(2)}, u32[]{:S(2)}) collective-permute-start(bf16[128,2048]{1,0:T(8,128)(2,1)S(1)} %add_convert_fusion.2), channel_id=1, source_target_pairs={{0,16},{1,17},{2,18},{3,19},{4,12},{5,13},{6,14},{7,15},{8,24},{9,... | collective-permute-start | bytes 1572872 | tf_op jit(solution)/shard_map/ppermute | solution.py:39
  38.4 2.3 %collective-permute-start.15 = (bf16[128,2048]{1,0:T(8,128)(2,1)S(1)}, bf16[128,2048]{1,0:T(8,128)(2,1)S(1)}, u32[]{:S(2)}, u32[]{:S(2)}) collective-permute-start(bf16[128,2048]{1,0:T(8,128)(2,1)S(1)} %collective-permute-done.14.refs_0_), channel_id=1, source_target_pairs={{0,4},{1,5},{2,6},{3,7},{4,0},{5,1},{6,2},{7,3},{8,12},{9,13},{10,... | collective-permute-start | bytes 1572872 | tf_op jit(solution)/shard_map/ppermute | solution.py:39
  40.1 10.4 %collective-permute-start.18 = (bf16[128,2048]{1,0:T(8,128)(2,1)S(1)}, bf16[128,2048]{1,0:T(8,128)(2,1)S(1)}, u32[]{:S(2)}, u32[]{:S(2)}) collective-permute-start(bf16[128,2048]{1,0:T(8,128)(2,1)S(1)} %get-tuple-element.105), channel_id=1, source_target_pairs={{0,4},{1,5},{2,6},{3,7},{4,0},{5,1},{6,2},{7,3},{8,12},{9,13},{10,... | collective-permute-start | bytes 1572872 | tf_op jit(solution)/shard_map/ppermute | solution.py:39
  41.9 2.0 %collective-permute-start.17 = (bf16[128,2048]{1,0:T(8,128)(2,1)S(1)}, bf16[128,2048]{1,0:T(8,128)(2,1)S(1)}, u32[]{:S(2)}, u32[]{:S(2)}) collective-permute-start(bf16[128,2048]{1,0:T(8,128)(2,1)S(1)} %get-tuple-element.112), channel_id=1, source_target_pairs={{0,4},{1,5},{2,6},{3,7},{4,0},{5,1},{6,2},{7,3},{8,12},{9,13},{10,... | collective-permute-start | bytes 1572872 | tf_op jit(solution)/shard_map/ppermute | solution.py:39
  44.0 9.2 %collective-permute-start.19 = (bf16[128,2048]{1,0:T(8,128)(2,1)S(1)}, bf16[128,2048]{1,0:T(8,128)(2,1)S(1)}, u32[]{:S(2)}, u32[]{:S(2)}) collective-permute-start(bf16[128,2048]{1,0:T(8,128)(2,1)S(1)} %add_convert_fusion.1), channel_id=1, source_target_pairs={{0,16},{1,17},{2,18},{3,19},{4,12},{5,13},{6,14},{7,15},{8,24},{9,... | collective-permute-start | bytes 1572872 | tf_op jit(solution)/shard_map/ppermute | solution.py:39
  46.1 17.0 %collective-permute-start.23 = (bf16[32,2048]{1,0:T(8,128)(2,1)S(1)}, bf16[32,2048]{1,0:T(8,128)(2,1)S(1)}, u32[]{:S(2)}, u32[]{:S(2)}) collective-permute-start(bf16[32,2048]{1,0:T(8,128)(2,1)S(1)} %get-tuple-element.136), channel_id=1, source_target_pairs={{0,1},{1,0},{2,3},{3,2},{4,5},{5,4},{6,7},{7,6},{8,9},{9,8},{10,11... | collective-permute-start | bytes 393224 | tf_op jit(solution)/shard_map/ppermute | solution.py:39
  48.1 16.4 %collective-permute-start.22 = (bf16[32,2048]{1,0:T(8,128)(2,1)S(1)}, bf16[32,2048]{1,0:T(8,128)(2,1)S(1)}, u32[]{:S(2)}, u32[]{:S(2)}) collective-permute-start(bf16[32,2048]{1,0:T(8,128)(2,1)S(1)} %get-tuple-element.137), channel_id=1, source_target_pairs={{0,2},{1,3},{2,0},{3,1},{4,6},{5,7},{6,4},{7,5},{8,10},{9,11},{10,... | collective-permute-start | bytes 393224 | tf_op jit(solution)/shard_map/ppermute | solution.py:39
  49.1 15.4 %collective-permute-start.21 = (bf16[32,2048]{1,0:T(8,128)(2,1)S(1)}, bf16[32,2048]{1,0:T(8,128)(2,1)S(1)}, u32[]{:S(2)}, u32[]{:S(2)}) collective-permute-start(bf16[32,2048]{1,0:T(8,128)(2,1)S(1)} %get-tuple-element.138), channel_id=1, source_target_pairs={{0,3},{1,2},{2,1},{3,0},{4,7},{5,6},{6,5},{7,4},{8,11},{9,10},{10,... | collective-permute-start | bytes 393224 | tf_op jit(solution)/shard_map/ppermute | solution.py:39
  53.5 6.4 %collective-permute-start.20 = (bf16[64,2048]{1,0:T(8,128)(2,1)S(1)}, bf16[64,2048]{1,0:T(8,128)(2,1)S(1)}, u32[]{:S(2)}, u32[]{:S(2)}) collective-permute-start(bf16[64,2048]{1,0:T(8,128)(2,1)S(1)} %get-tuple-element.115), channel_id=1, source_target_pairs={{0,8},{1,9},{2,10},{3,11},{4,20},{5,21},{6,22},{7,23},{8,0},{9,1},... | collective-permute-start | bytes 786440 | tf_op jit(solution)/shard_map/ppermute | solution.py:39
  60.0 6.2 %collective-permute-start.27 = (bf16[16,2048]{1,0:T(8,128)(2,1)S(1)}, bf16[16,2048]{1,0:T(8,128)(2,1)S(1)}, u32[]{:S(2)}, u32[]{:S(2)}) collective-permute-start(bf16[16,2048]{1,0:T(8,128)(2,1)S(1)} %get-tuple-element.139), channel_id=1, source_target_pairs={{0,1},{1,0},{2,3},{3,2},{4,5},{5,4},{6,7},{7,6},{8,9},{9,8},{10,11... | collective-permute-start | bytes 196616 | tf_op jit(solution)/shard_map/ppermute | solution.py:39
  62.0 6.0 %collective-permute-start.26 = (bf16[16,2048]{1,0:T(8,128)(2,1)S(1)}, bf16[16,2048]{1,0:T(8,128)(2,1)S(1)}, u32[]{:S(2)}, u32[]{:S(2)}) collective-permute-start(bf16[16,2048]{1,0:T(8,128)(2,1)S(1)} %get-tuple-element.140), channel_id=1, source_target_pairs={{0,2},{1,3},{2,0},{3,1},{4,6},{5,7},{6,4},{7,5},{8,10},{9,11},{10,... | collective-permute-start | bytes 196616 | tf_op jit(solution)/shard_map/ppermute | solution.py:39
  63.1 6.2 %collective-permute-start.25 = (bf16[16,2048]{1,0:T(8,128)(2,1)S(1)}, bf16[16,2048]{1,0:T(8,128)(2,1)S(1)}, u32[]{:S(2)}, u32[]{:S(2)}) collective-permute-start(bf16[16,2048]{1,0:T(8,128)(2,1)S(1)} %get-tuple-element.141), channel_id=1, source_target_pairs={{0,3},{1,2},{2,1},{3,0},{4,7},{5,6},{6,5},{7,4},{8,11},{9,10},{10,... | collective-permute-start | bytes 196616 | tf_op jit(solution)/shard_map/ppermute | solution.py:39
  64.6 4.7 %collective-permute-start.24 = (bf16[16,2048]{1,0:T(8,128)(2,1)S(1)}, bf16[16,2048]{1,0:T(8,128)(2,1)S(1)}, u32[]{:S(2)}, u32[]{:S(2)}) collective-permute-start(bf16[16,2048]{1,0:T(8,128)(2,1)S(1)} %get-tuple-element.143), channel_id=1, source_target_pairs={{0,8},{1,9},{2,10},{3,11},{4,20},{5,21},{6,22},{7,23},{8,0},{9,1},... | collective-permute-start | bytes 196616 | tf_op jit(solution)/shard_map/ppermute | solution.py:39

commit v5 on v4

--- a/solution.py
+++ b/solution.py
@@ -171,19 +171,20 @@
         return nt(gate, self.refs[0][0]) + nt(up, self.refs[1][0])
 
 
-def join_kernel(blocks, *refs):
+def join_kernel(blocks, flip, *refs):
     at, out = 0, refs[-1]
+    arrays = (refs[0], *refs[-2:0:-1]) if flip else refs[:-1]
     for i in range(blocks):
-        for ref in refs[:-1]:
+        for ref in arrays:
             size = ref.shape[0] // blocks
             out[at : at + size, :] = ref[i * size : (i + 1) * size, :]
             at += size
 
 
-def join(*arrays, blocks=1, length=0.0):
+def join(*arrays, blocks=1, flip=False, length=0.0):
     rows = sum(a.shape[0] for a in arrays)
     return pl.pallas_call(
-        functools.partial(join_kernel, blocks),
+        functools.partial(join_kernel, blocks, flip),
         in_specs=[WHOLE] * len(arrays),
         out_specs=WHOLE,
         out_shape=pltpu.VMEM((rows, arrays[0].shape[1]), BF16),
@@ -288,19 +289,6 @@
     values = hidden_values(x, weights)
     act[...], gate_f[...], up_f[...] = values
     return values[0]
-
-
-def forward_pair_kernel(experts, width, expert, a, b, weights, kept, given, *units):
-    n = a.shape[0]
-    x = jnp.concatenate((a[:, :width], b[:, :width]))
-    p = expert_weight(experts, expert, jnp.concatenate((a[:, width:], b[:, width:])))
-    values = hidden_values(x, weights)
-    out = p * weights.out(values[0])
-    for i, value in enumerate((*values, jnp.broadcast_to(p, (2 * n, 128)))):
-        units[i][...] = value[:n]
-        units[i + 4][...] = value[n:]
-    kept[...] = out[:n].astype(BF16)
-    given[...] = out[n:].astype(BF16)
 
 
 def forward_hidden_kernel(experts, width, expert, a, weights, act, gate_f, up_f, weight):
@@ -463,7 +451,7 @@
         weights = stage(*(after(w, own) for w in weights))
     for p in plane[:-1]:
         cot = join(cot, send(cot, p))
-    row_lane = join(after(own, weights[0], cot), *[send(own, p) for p in line])
+    row_lane = join(after(own, weights[0], cot), *[send(own, p) for p in line[::-1]], flip=True)
     cot = after(cot, row_lane)
     cot_lane = join(cot, *[send(cot, p) for p in line], length=10.0)
     for p in plane[:-1]:
@@ -475,12 +463,6 @@
     def forward(kernel, *args):
         return functools.partial(kernel, experts, width), n, [expert], *args
 
-    f_early = over_rows(
-        *forward(forward_pair_kernel, [(1, row_lane), (1, row_other)], weights, [wide] * 2 + each(1, units * 2))
-    )
-    kept, given, *f_early = f_early
-    f_early = (f_early[:4], f_early[4:])
-    cot_lane = after(cot_lane, kept)
     cot_late = send(cot_lane, plane[-1])
     cot_other = send(cot_lane, core)
 
@@ -493,15 +475,15 @@
     row_late = after(row_late, cot_lane)
     row_late_other = send(row_late, core)
     f_own = over_rows(*forward(forward_hidden_kernel, [(1, row_late)], weights, each(1, units), 10.0))
-    *f_other, o_given = over_rows(
-        *forward(forward_full_kernel, [(1, row_late_other)], weights, each(1, units) + [wide], 10.0)
-    )
+    full = weights, each(1, units) + [wide], 10.0
+    *f_early_own, kept = over_rows(*forward(forward_full_kernel, [(1, after(row_lane, f_own[0]))], *full))
+    row_late_other_in = after(row_late_other, kept)
+    *f_other, o_given = over_rows(*forward(forward_full_kernel, [(1, row_late_other_in)], *full))
     o_other = send(o_given, core)
-    taken = [(1, f_own[0]), (1, after(f_own[3], f_other[0]))]
-    (o_own,) = over_rows(forward_out_kernel, n, [], taken, weights, [wide], 10.0)
-    taken = [(1, after(cot_lane, f_other[0]))] + with_units(f_early[0])
-    *b_early, g_kept = over_rows(backward_full_kernel, n, [], taken, weights, each(1, cots) + [wide], 10.0)
-    o_late = halve(o_own, after(o_other, g_kept))
+    *f_early_other, given = over_rows(*forward(forward_full_kernel, [(1, after(row_other, f_other[0]))], *full))
+    taken = [(1, f_own[0]), (1, after(f_own[3], given))]
+    (o_own,) = over_rows(forward_out_kernel, n, [], taken, weights, [wide])
+    o_late = halve(o_own, o_other)
     o_early_other = send(given, core)
     o_back = send(o_late, plane[-1])
 
@@ -509,15 +491,18 @@
     cot_late_other = send(cot_late, core)
     taken = [(1, cot_late)] + with_units(f_own)
     b_own = over_rows(backward_hidden_kernel, n, [], taken, weights, each(1, cots), 10.0)
-    taken = [(1, after(cot_other, b_own[0]))] + with_units(f_early[1])
-    *b_early_other, g_early = over_rows(backward_full_kernel, n, [], taken, weights, each(1, cots) + [wide], 10.0)
-    taken = [(1, after(cot_late_other, g_early))] + with_units(f_other)
-    *b_other, g_given = over_rows(backward_full_kernel, n, [], taken, weights, each(1, cots) + [wide], 10.0)
+    full = weights, each(1, cots) + [wide], 10.0
+    taken = [(1, after(cot_lane, b_own[0]))] + with_units(f_early_own)
+    *b_early, g_kept = over_rows(backward_full_kernel, n, [], taken, *full)
+    taken = [(1, after(cot_late_other, g_kept))] + with_units(f_other)
+    *b_other, g_given = over_rows(backward_full_kernel, n, [], taken, *full)
     g_other = send(g_given, core)
-    taken = [(1, b_own[0]), (1, after(b_own[1], b_other[0]))]
-    (g_own,) = over_rows(backward_rows_kernel, n, [], taken, weights, [wide], 10.0)
+    taken = [(1, after(cot_other, b_other[0]))] + with_units(f_early_other)
+    *b_early_other, g_early = over_rows(backward_full_kernel, n, [], taken, *full)
+    taken = [(1, b_own[0]), (1, after(b_own[1], g_early))]
+    (g_own,) = over_rows(backward_rows_kernel, n, [], taken, weights, [wide])
     g_late = halve(g_own, g_other)
-    g_early_other = send(g_early, core)
+    g_early_other = send(after(g_early, g_late), core)
     g_back = send(g_late, plane[-1])
     o_back = after(o_back, g_late)
 
@@ -528,13 +513,14 @@
     steps = max(1, n // BLOCK)
     gate_cots, up_cots, out_cots = zip(b_early, b_early_other, b_own, b_other)
 
+    g_sent = g_late
     parts = (g_kept, g_early_other, g_back)
     for p in reversed(plane[:-1]):
         g_lane, g_sent = split_sum(n_ex, *parts)
         parts = (g_lane, send(g_sent, p))
     lefts = [after(row_lane, g_sent), row_other, row_late, row_late_other]
     gate_grad, up_grad = gradients(lefts, [gate_cots, up_cots], width, steps)
-    acts = [after(f_early[0][0], g_sent), f_early[1][0], f_own[0], f_other[0]]
+    acts = [after(f_early_own[0], g_sent), f_early_other[0], f_own[0], f_other[0]]
     (down_grad,) = gradients(acts, [out_cots], hidden, steps)
     g_lane = add(parts[0], after(parts[1], gate_grad, down_grad)).astype(BF16)
     g_terms = line_sends(g_lane)

time: 70.3 us -> 68.4 us (0.973)
  waiting for transfers between devices: 18.7 us -> 15.4 us
  starting transfers between devices: 31.2 us -> 32.3 us
    ppermute x28, waiting for transfers between devices: 18.7 us -> 15.4 us  [send(): return lax.ppermute(x, AXES, pairs)]
    ppermute x28, starting transfers between devices: 31.2 us -> 32.3 us  [send(): return lax.ppermute(x, AXES, pairs)]
    pallas_call x9 -> x10, Pallas kernels: 8.94 us -> 9.21 us  [over_rows(): pl.pallas_call(run, out_shape=shaped(*[((f * n, w), t) for f, w, t in giv...]
  transfers between devices with their start and end apart: 28 -> 28, of which waited for: 13 -> 11; matrix products, arithmetic and copies ran while one was open for 1% -> 1% of each run, Pallas kernels for 24% -> 25%
where the time goes in v5:
time: 68.4 us; the launch traced here: 68.2 us
  starting transfers between devices  32.3 us (47%)
  Pallas kernels  18.8 us (27%)
  waiting for transfers between devices  15.4 us (23%)
  between operations  1.07 us (2%)
    ppermute x28, starting transfers between devices, send(): return lax.ppermute(x, AXES, pairs)  32.3 us
    ppermute x28, waiting for transfers between devices, send(): return lax.ppermute(x, AXES, pairs)  15.4 us
    pallas_call x10, Pallas kernels, over_rows(): pl.pallas_call(run, out_shape=shaped(*[((f * n, w), t) for f, w, t in giv...  9.21 us
    pallas_call x2, Pallas kernels, gradients_by_chunks(): pl.pallas_call(functools.partial(chunk_kernel, over_left, chunks, [len(g)...  4.57 us
    pallas_call x1, Pallas kernels, stage(): pl.pallas_call(stage_kernel, in_specs=[ANY] * 3, out_specs=[WHOLE] * 2, o...  2.86 us
  transfers between devices with their start and end apart: 28, of which 11 were waited for; matrix products, arithmetic and copies ran while one was open for 1% of the time, Pallas kernels for 25%

profile of v5, /device:TPU:0, one launch (start us, length us, event | category | flops | bytes accessed | tf_op | source)
XLA Modules:
  0.0 68.2 jit_solution(2647527639223271327)
XLA Ops:
  0.6 0.9 %shard_map.110 = (bf16[16,2176]{1,0:T(8,128)(2,1)S(1)}, bf16[16,2048]{1,0:T(8,128)(2,1)S(1)}) custom-call(bf16[16,2048]{1,0:T(8,128)(2,1)} %tokens, bf16[16,2048]{1,0:T(8,128)(2,1)} %cotangent.1, s32[8,16]{1,0:T(8,128)} %bitcast.3, f32[8,16]{1,0:T(8,128)} %bitcast.4), custom_call_target="tpu_custom_call" | custom-call | tf_op jit(solution)/shard_map/pallas_call | solution.py:111
  1.6 5.1 %collective-permute-start.3 = (bf16[16,2176]{1,0:T(8,128)(2,1)S(1)}, bf16[16,2176]{1,0:T(8,128)(2,1)S(1)}, u32[]{:S(2)}, u32[]{:S(2)}) collective-permute-start(bf16[16,2176]{1,0:T(8,128)(2,1)S(1)} %get-tuple-element.80.refs_0_), channel_id=1, source_target_pairs={{0,3},{1,2},{2,1},{3,0},{4,7},{5,6},{6,5},{7,4},{8,11},{9,10},{10,... | collective-permute-start | bytes 208904 | tf_op jit(solution)/shard_map/ppermute | solution.py:39
  7.3 1.6 %collective-permute-start = (bf16[16,2048]{1,0:T(8,128)(2,1)S(1)}, bf16[16,2048]{1,0:T(8,128)(2,1)S(1)}, u32[]{:S(2)}, u32[]{:S(2)}) collective-permute-start(bf16[16,2048]{1,0:T(8,128)(2,1)S(1)} %get-tuple-element.79.refs_0_), channel_id=1, source_target_pairs={{0,8},{1,9},{2,10},{3,11},{4,20},{5,21},{6,22},{7,23},{8,0},{9,1},... | collective-permute-start | bytes 196616 | tf_op jit(solution)/shard_map/ppermute | solution.py:39
  9.0 2.9 %shard_map.111 = (bf16[3,2048,384]{2,1,0:T(8,128)(2,1)S(1)}, bf16[3,384,2048]{2,1,0:T(8,128)(2,1)S(1)}) custom-call(bf16[1,2048,384]{2,1,0:T(8,128)(2,1)} %gate, bf16[1,2048,384]{2,1,0:T(8,128)(2,1)} %up, bf16[1,384,2048]{2,1,0:T(8,128)(2,1)} %down), custom_call_target="tpu_custom_call" | custom-call | tf_op jit(solution)/shard_map/pallas_call | solution.py:142
  12.6 1.6 %collective-permute-start.4 = (bf16[64,2176]{1,0:T(8,128)(2,1)S(1)}, bf16[64,2176]{1,0:T(8,128)(2,1)S(1)}, u32[]{:S(2)}, u32[]{:S(2)}) collective-permute-start(bf16[64,2176]{1,0:T(8,128)(2,1)S(1)} %shard_map.113.refs_0_), channel_id=1, source_target_pairs={{0,8},{1,9},{2,10},{3,11},{4,20},{5,21},{6,22},{7,23},{8,0},{9,1},... | collective-permute-start | bytes 835592 | tf_op jit(solution)/shard_map/ppermute | solution.py:39
  14.2 1.0 %collective-permute-start.8 = (bf16[32,2048]{1,0:T(8,128)(2,1)S(1)}, bf16[32,2048]{1,0:T(8,128)(2,1)S(1)}, u32[]{:S(2)}, u32[]{:S(2)}) collective-permute-start(bf16[32,2048]{1,0:T(8,128)(2,1)S(1)} %shard_map.112.refs_0_), channel_id=1, source_target_pairs={{0,1},{1,0},{2,3},{3,2},{4,5},{5,4},{6,7},{7,6},{8,9},{9,8},{10,11... | collective-permute-start | bytes 393224 | tf_op jit(solution)/shard_map/ppermute | solution.py:39
  15.2 2.3 %collective-permute-start.7 = (bf16[32,2048]{1,0:T(8,128)(2,1)S(1)}, bf16[32,2048]{1,0:T(8,128)(2,1)S(1)}, u32[]{:S(2)}, u32[]{:S(2)}) collective-permute-start(bf16[32,2048]{1,0:T(8,128)(2,1)S(1)} %shard_map.112.refs_0_), channel_id=1, source_target_pairs={{0,2},{1,3},{2,0},{3,1},{4,6},{5,7},{6,4},{7,5},{8,10},{9,11},{10,... | collective-permute-start | bytes 393224 | tf_op jit(solution)/shard_map/ppermute | solution.py:39
  17.6 1.0 %collective-permute-start.6 = (bf16[32,2048]{1,0:T(8,128)(2,1)S(1)}, bf16[32,2048]{1,0:T(8,128)(2,1)S(1)}, u32[]{:S(2)}, u32[]{:S(2)}) collective-permute-start(bf16[32,2048]{1,0:T(8,128)(2,1)S(1)} %shard_map.112.refs_0_), channel_id=1, source_target_pairs={{0,3},{1,2},{2,1},{3,0},{4,7},{5,6},{6,5},{7,4},{8,11},{9,10},{10,... | collective-permute-start | bytes 393224 | tf_op jit(solution)/shard_map/ppermute | solution.py:39
  19.3 1.6 %collective-permute-start.5 = (bf16[128,2176]{1,0:T(8,128)(2,1)S(1)}, bf16[128,2176]{1,0:T(8,128)(2,1)S(1)}, u32[]{:S(2)}, u32[]{:S(2)}) collective-permute-start(bf16[128,2176]{1,0:T(8,128)(2,1)S(1)} %shard_map.114.refs_1_.refs_0_), channel_id=1, source_target_pairs={{0,16},{1,17},{2,18},{3,19},{4,12},{5,13},{6,14},{7,15},{8,24},{9,... | collective-permute-start | bytes 1671176 | tf_op jit(solution)/shard_map/ppermute | solution.py:39
  20.9 6.2 %collective-permute-done.7.refs_2_ = bf16[32,2048]{1,0:T(8,128)(2,1)S(1)} collective-permute-done((bf16[32,2048]{1,0:T(8,128)(2,1)S(1)}, bf16[32,2048]{1,0:T(8,128)(2,1)S(1)}, u32[]{:S(2)}, u32[]{:S(2)}) %collective-permute-start.7) | collective-permute-done | bytes 131104 | tf_op jit(solution)/shard_map/ppermute | solution.py:39
  27.8 1.1 %collective-permute-start.9 = (bf16[128,2176]{1,0:T(8,128)(2,1)S(1)}, bf16[128,2176]{1,0:T(8,128)(2,1)S(1)}, u32[]{:S(2)}, u32[]{:S(2)}) collective-permute-start(bf16[128,2176]{1,0:T(8,128)(2,1)S(1)} %shard_map.114.refs_1_.refs_0_), channel_id=1, source_target_pairs={{0,4},{1,5},{2,6},{3,7},{4,0},{5,1},{6,2},{7,3},{8,12},{9,13},{10,... | collective-permute-start | bytes 1671176 | tf_op jit(solution)/shard_map/ppermute | solution.py:39
  29.6 1.1 %shard_map.117 = (bf16[128,384]{1,0:T(8,128)(2,1)S(1)}, f32[128,384]{1,0:T(8,128)S(1)}, f32[128,384]{1,0:T(8,128)S(1)}, f32[128,128]{1,0:T(8,128)S(1)}, bf16[128,2048]{1,0:T(8,128)(2,1)S(1)}) custom-call(s32[1,1]{1,0:T(1,128)} %bitcast.refs_0_, bf16[128,2176]{1,0:T(8,128)(2,1)S(1)} %shard_map.114.refs_1_.refs_0_, ...), custom_call_target="tpu_custom_call" | custom-call | flops 11500000256 | tf_op jit(solution)/shard_map/pallas_call | solution.py:265
  31.3 1.1 %shard_map.118 = (bf16[128,384]{1,0:T(8,128)(2,1)S(1)}, f32[128,384]{1,0:T(8,128)S(1)}, f32[128,384]{1,0:T(8,128)S(1)}, f32[128,128]{1,0:T(8,128)S(1)}, bf16[128,2048]{1,0:T(8,128)(2,1)S(1)}) custom-call(s32[1,1]{1,0:T(1,128)} %bitcast.refs_0_, bf16[128,2176]{1,0:T(8,128)(2,1)S(1)} %collective-permute-done.10.refs_1_.refs_3_, ...), custom_call_target="tpu_custom_call" | custom-call | flops 11500000256 | tf_op jit(solution)/shard_map/pallas_call | solution.py:265
  32.8 1.1 %shard_map.119 = (bf16[128,384]{1,0:T(8,128)(2,1)S(1)}, f32[128,384]{1,0:T(8,128)S(1)}, f32[128,384]{1,0:T(8,128)S(1)}, f32[128,128]{1,0:T(8,128)S(1)}, bf16[128,2048]{1,0:T(8,128)(2,1)S(1)}) custom-call(s32[1,1]{1,0:T(1,128)} %bitcast.refs_0_, bf16[128,2176]{1,0:T(8,128)(2,1)S(1)} %collective-permute-done.9.refs_1_, ...), custom_call_target="tpu_custom_call" | custom-call | flops 11500000256 | tf_op jit(solution)/shard_map/pallas_call | solution.py:265
  34.7 1.2 %collective-permute-start.13 = (bf16[128,2048]{1,0:T(8,128)(2,1)S(1)}, bf16[128,2048]{1,0:T(8,128)(2,1)S(1)}, u32[]{:S(2)}, u32[]{:S(2)}) collective-permute-start(bf16[128,2048]{1,0:T(8,128)(2,1)S(1)} %add_convert_fusion.2), channel_id=1, source_target_pairs={{0,16},{1,17},{2,18},{3,19},{4,12},{5,13},{6,14},{7,15},{8,24},{9,... | collective-permute-start | bytes 1572872 | tf_op jit(solution)/shard_map/ppermute | solution.py:39
  37.0 1.2 %shard_map.122 = (bf16[128,384]{1,0:T(8,128)(2,1)S(1)}, bf16[128,384]{1,0:T(8,128)(2,1)S(1)}, bf16[128,2048]{1,0:T(8,128)(2,1)S(1)}, bf16[128,2048]{1,0:T(8,128)(2,1)S(1)}) custom-call(bf16[128,2048]{1,0:T(8,128)(2,1)S(1)} %shard_map.115.refs_0_, f32[128,128]{1,0:T(8,128)S(1)} %get-tuple-element.100.refs_1_, f32[128,384]{1,0:T(8,128)S(1)} %get-tuple-element.101.refs_2_, ...), custom_call_target="tpu_custom_call" | custom-call | flops 11500000256 | tf_op jit(solution)/shard_map/pallas_call | solution.py:265
  38.4 1.2 %shard_map.123 = (bf16[128,384]{1,0:T(8,128)(2,1)S(1)}, bf16[128,384]{1,0:T(8,128)(2,1)S(1)}, bf16[128,2048]{1,0:T(8,128)(2,1)S(1)}, bf16[128,2048]{1,0:T(8,128)(2,1)S(1)}) custom-call(bf16[128,2048]{1,0:T(8,128)(2,1)S(1)} %collective-permute-done.16.refs_0_, f32[128,128]{1,0:T(8,128)S(1)} %get-tuple-element.105.refs_1_, ...), custom_call_target="tpu_custom_call" | custom-call | flops 11500000256 | tf_op jit(solution)/shard_map/pallas_call | solution.py:265
  40.0 1.2 %shard_map.124 = (bf16[128,384]{1,0:T(8,128)(2,1)S(1)}, bf16[128,384]{1,0:T(8,128)(2,1)S(1)}, bf16[128,2048]{1,0:T(8,128)(2,1)S(1)}, bf16[128,2048]{1,0:T(8,128)(2,1)S(1)}) custom-call(bf16[128,2048]{1,0:T(8,128)(2,1)S(1)} %collective-permute-done.15.refs_0_, f32[128,128]{1,0:T(8,128)S(1)} %get-tuple-element.110.refs_1_, ...), custom_call_target="tpu_custom_call" | custom-call | flops 11500000256 | tf_op jit(solution)/shard_map/pallas_call | solution.py:265
  42.0 0.8 %collective-permute-start.19 = (bf16[128,2048]{1,0:T(8,128)(2,1)S(1)}, bf16[128,2048]{1,0:T(8,128)(2,1)S(1)}, u32[]{:S(2)}, u32[]{:S(2)}) collective-permute-start(bf16[128,2048]{1,0:T(8,128)(2,1)S(1)} %add_convert_fusion.1), channel_id=1, source_target_pairs={{0,16},{1,17},{2,18},{3,19},{4,12},{5,13},{6,14},{7,15},{8,24},{9,... | collective-permute-start | bytes 1572872 | tf_op jit(solution)/shard_map/ppermute | solution.py:39
  44.3 2.1 %collective-permute-start.23 = (bf16[32,2048]{1,0:T(8,128)(2,1)S(1)}, bf16[32,2048]{1,0:T(8,128)(2,1)S(1)}, u32[]{:S(2)}, u32[]{:S(2)}) collective-permute-start(bf16[32,2048]{1,0:T(8,128)(2,1)S(1)} %get-tuple-element.140), channel_id=1, source_target_pairs={{0,1},{1,0},{2,3},{3,2},{4,5},{5,4},{6,7},{7,6},{8,9},{9,8},{10,11... | collective-permute-start | bytes 393224 | tf_op jit(solution)/shard_map/ppermute | solution.py:39
  46.4 1.0 %collective-permute-start.22 = (bf16[32,2048]{1,0:T(8,128)(2,1)S(1)}, bf16[32,2048]{1,0:T(8,128)(2,1)S(1)}, u32[]{:S(2)}, u32[]{:S(2)}) collective-permute-start(bf16[32,2048]{1,0:T(8,128)(2,1)S(1)} %get-tuple-element.141), channel_id=1, source_target_pairs={{0,2},{1,3},{2,0},{3,1},{4,6},{5,7},{6,4},{7,5},{8,10},{9,11},{10,... | collective-permute-start | bytes 393224 | tf_op jit(solution)/shard_map/ppermute | solution.py:39
  47.4 1.4 %collective-permute-start.21 = (bf16[32,2048]{1,0:T(8,128)(2,1)S(1)}, bf16[32,2048]{1,0:T(8,128)(2,1)S(1)}, u32[]{:S(2)}, u32[]{:S(2)}) collective-permute-start(bf16[32,2048]{1,0:T(8,128)(2,1)S(1)} %get-tuple-element.142), channel_id=1, source_target_pairs={{0,3},{1,2},{2,1},{3,0},{4,7},{5,6},{6,5},{7,4},{8,11},{9,10},{10,... | collective-permute-start | bytes 393224 | tf_op jit(solution)/shard_map/ppermute | solution.py:39
  48.8 2.4 %collective-permute-done.19.refs_2_ = bf16[128,2048]{1,0:T(8,128)(2,1)S(1)} collective-permute-done((bf16[128,2048]{1,0:T(8,128)(2,1)S(1)}, bf16[128,2048]{1,0:T(8,128)(2,1)S(1)}, u32[]{:S(2)}, u32[]{:S(2)}) %collective-permute-start.19) | collective-permute-done | bytes 524320 | tf_op jit(solution)/shard_map/ppermute | solution.py:39
  51.6 1.5 %collective-permute-start.20 = (bf16[64,2048]{1,0:T(8,128)(2,1)S(1)}, bf16[64,2048]{1,0:T(8,128)(2,1)S(1)}, u32[]{:S(2)}, u32[]{:S(2)}) collective-permute-start(bf16[64,2048]{1,0:T(8,128)(2,1)S(1)} %get-tuple-element.119), channel_id=1, source_target_pairs={{0,8},{1,9},{2,10},{3,11},{4,20},{5,21},{6,22},{7,23},{8,0},{9,1},... | collective-permute-start | bytes 786440 | tf_op jit(solution)/shard_map/ppermute | solution.py:39
  53.1 1.8 %shard_map.128 = bf16[1,384,2048]{2,1,0:T(8,128)(2,1)} custom-call(bf16[128,384]{1,0:T(8,128)(2,1)S(1)} %get-tuple-element.128.refs_0_, bf16[128,384]{1,0:T(8,128)(2,1)S(1)} %get-tuple-element.129.refs_1_, bf16[128,384]{1,0:T(8,128)(2,1)S(1)} %get-tuple-element.84.refs_0_.refs_2_, bf16[128,384]{1,0:T(8,128)(2,1)S(1)} %get-tuple-element.88.refs_3_, ...), custom_call_target="tpu_custom_call" | custom-call | flops 11500000256 | tf_op jit(solution)/shard_map/pallas_call | solution.py:365
  54.9 2.8 %shard_map.127 = (bf16[1,2048,384]{2,1,0:T(8,128)(2,1)}, bf16[1,2048,384]{2,1,0:T(8,128)(2,1)}) custom-call(bf16[128,2176]{1,0:T(8,128)(2,1)S(1)} %shard_map.114.refs_1_.refs_0_, bf16[128,2176]{1,0:T(8,128)(2,1)S(1)} %collective-permute-done.9.refs_1_, bf16[128,2176]{1,0:T(8,128)(2,1)S(1)} %collective-permute-done.5.refs_1_.refs_2_, ...), custom_call_target="tpu_custom_call" | custom-call | flops 11500000256 | tf_op jit(solution)/shard_map/pallas_call | solution.py:365
  58.2 2.0 %collective-permute-start.27 = (bf16[16,2048]{1,0:T(8,128)(2,1)S(1)}, bf16[16,2048]{1,0:T(8,128)(2,1)S(1)}, u32[]{:S(2)}, u32[]{:S(2)}) collective-permute-start(bf16[16,2048]{1,0:T(8,128)(2,1)S(1)} %get-tuple-element.143), channel_id=1, source_target_pairs={{0,1},{1,0},{2,3},{3,2},{4,5},{5,4},{6,7},{7,6},{8,9},{9,8},{10,11... | collective-permute-start | bytes 196616 | tf_op jit(solution)/shard_map/ppermute | solution.py:39
  60.2 0.9 %collective-permute-start.26 = (bf16[16,2048]{1,0:T(8,128)(2,1)S(1)}, bf16[16,2048]{1,0:T(8,128)(2,1)S(1)}, u32[]{:S(2)}, u32[]{:S(2)}) collective-permute-start(bf16[16,2048]{1,0:T(8,128)(2,1)S(1)} %get-tuple-element.144), channel_id=1, source_target_pairs={{0,2},{1,3},{2,0},{3,1},{4,6},{5,7},{6,4},{7,5},{8,10},{9,11},{10,... | collective-permute-start | bytes 196616 | tf_op jit(solution)/shard_map/ppermute | solution.py:39
  61.1 1.6 %collective-permute-start.25 = (bf16[16,2048]{1,0:T(8,128)(2,1)S(1)}, bf16[16,2048]{1,0:T(8,128)(2,1)S(1)}, u32[]{:S(2)}, u32[]{:S(2)}) collective-permute-start(bf16[16,2048]{1,0:T(8,128)(2,1)S(1)} %get-tuple-element.145), channel_id=1, source_target_pairs={{0,3},{1,2},{2,1},{3,0},{4,7},{5,6},{6,5},{7,4},{8,11},{9,10},{10,... | collective-permute-start | bytes 196616 | tf_op jit(solution)/shard_map/ppermute | solution.py:39
  62.8 1.5 %collective-permute-start.24 = (bf16[16,2048]{1,0:T(8,128)(2,1)S(1)}, bf16[16,2048]{1,0:T(8,128)(2,1)S(1)}, u32[]{:S(2)}, u32[]{:S(2)}) collective-permute-start(bf16[16,2048]{1,0:T(8,128)(2,1)S(1)} %get-tuple-element.147), channel_id=1, source_target_pairs={{0,8},{1,9},{2,10},{3,11},{4,20},{5,21},{6,22},{7,23},{8,0},{9,1},... | collective-permute-start | bytes 196616 | tf_op jit(solution)/shard_map/ppermute | solution.py:39
  64.4 1.6 %collective-permute-done.26.refs_4_ = bf16[16,2048]{1,0:T(8,128)(2,1)S(1)} collective-permute-done((bf16[16,2048]{1,0:T(8,128)(2,1)S(1)}, bf16[16,2048]{1,0:T(8,128)(2,1)S(1)}, u32[]{:S(2)}, u32[]{:S(2)}) %collective-permute-start.26) | collective-permute-done | bytes 65568 | tf_op jit(solution)/shard_map/ppermute | solution.py:39
  66.0 1.4 %collective-permute-done.25.refs_3_ = bf16[16,2048]{1,0:T(8,128)(2,1)S(1)} collective-permute-done((bf16[16,2048]{1,0:T(8,128)(2,1)S(1)}, bf16[16,2048]{1,0:T(8,128)(2,1)S(1)}, u32[]{:S(2)}, u32[]{:S(2)}) %collective-permute-start.25) | collective-permute-done | bytes 65568 | tf_op jit(solution)/shard_map/ppermute | solution.py:39
  (53 shorter events, 10.9 us)
Async XLA Ops:
  1.6 10.3 %collective-permute-start.3 = (bf16[16,2176]{1,0:T(8,128)(2,1)S(1)}, bf16[16,2176]{1,0:T(8,128)(2,1)S(1)}, u32[]{:S(2)}, u32[]{:S(2)}) collective-permute-start(bf16[16,2176]{1,0:T(8,128)(2,1)S(1)} %get-tuple-element.80.refs_0_), channel_id=1, source_target_pairs={{0,3},{1,2},{2,1},{3,0},{4,7},{5,6},{6,5},{7,4},{8,11},{9,10},{10,... | collective-permute-start | bytes 208904 | tf_op jit(solution)/shard_map/ppermute | solution.py:39
  6.7 5.9 %collective-permute-start.2 = (bf16[16,2176]{1,0:T(8,128)(2,1)S(1)}, bf16[16,2176]{1,0:T(8,128)(2,1)S(1)}, u32[]{:S(2)}, u32[]{:S(2)}) collective-permute-start(bf16[16,2176]{1,0:T(8,128)(2,1)S(1)} %get-tuple-element.80.refs_0_), channel_id=1, source_target_pairs={{0,2},{1,3},{2,0},{3,1},{4,6},{5,7},{6,4},{7,5},{8,10},{9,11},{10,... | collective-permute-start | bytes 208904 | tf_op jit(solution)/shard_map/ppermute | solution.py:39
  6.7 5.9 %collective-permute-start.1 = (bf16[16,2176]{1,0:T(8,128)(2,1)S(1)}, bf16[16,2176]{1,0:T(8,128)(2,1)S(1)}, u32[]{:S(2)}, u32[]{:S(2)}) collective-permute-start(bf16[16,2176]{1,0:T(8,128)(2,1)S(1)} %get-tuple-element.80.refs_0_), channel_id=1, source_target_pairs={{0,1},{1,0},{2,3},{3,2},{4,5},{5,4},{6,7},{7,6},{8,9},{9,8},{10,11... | collective-permute-start | bytes 208904 | tf_op jit(solution)/shard_map/ppermute | solution.py:39
  7.3 4.5 %collective-permute-start = (bf16[16,2048]{1,0:T(8,128)(2,1)S(1)}, bf16[16,2048]{1,0:T(8,128)(2,1)S(1)}, u32[]{:S(2)}, u32[]{:S(2)}) collective-permute-start(bf16[16,2048]{1,0:T(8,128)(2,1)S(1)} %get-tuple-element.79.refs_0_), channel_id=1, source_target_pairs={{0,8},{1,9},{2,10},{3,11},{4,20},{5,21},{6,22},{7,23},{8,0},{9,1},... | collective-permute-start | bytes 196616 | tf_op jit(solution)/shard_map/ppermute | solution.py:39
  12.6 6.6 %collective-permute-start.4 = (bf16[64,2176]{1,0:T(8,128)(2,1)S(1)}, bf16[64,2176]{1,0:T(8,128)(2,1)S(1)}, u32[]{:S(2)}, u32[]{:S(2)}) collective-permute-start(bf16[64,2176]{1,0:T(8,128)(2,1)S(1)} %shard_map.113.refs_0_), channel_id=1, source_target_pairs={{0,8},{1,9},{2,10},{3,11},{4,20},{5,21},{6,22},{7,23},{8,0},{9,1},... | collective-permute-start | bytes 835592 | tf_op jit(solution)/shard_map/ppermute | solution.py:39
  14.2 6.7 %collective-permute-start.8 = (bf16[32,2048]{1,0:T(8,128)(2,1)S(1)}, bf16[32,2048]{1,0:T(8,128)(2,1)S(1)}, u32[]{:S(2)}, u32[]{:S(2)}) collective-permute-start(bf16[32,2048]{1,0:T(8,128)(2,1)S(1)} %shard_map.112.refs_0_), channel_id=1, source_target_pairs={{0,1},{1,0},{2,3},{3,2},{4,5},{5,4},{6,7},{7,6},{8,9},{9,8},{10,11... | collective-permute-start | bytes 393224 | tf_op jit(solution)/shard_map/ppermute | solution.py:39
  15.2 11.9 %collective-permute-start.7 = (bf16[32,2048]{1,0:T(8,128)(2,1)S(1)}, bf16[32,2048]{1,0:T(8,128)(2,1)S(1)}, u32[]{:S(2)}, u32[]{:S(2)}) collective-permute-start(bf16[32,2048]{1,0:T(8,128)(2,1)S(1)} %shard_map.112.refs_0_), channel_id=1, source_target_pairs={{0,2},{1,3},{2,0},{3,1},{4,6},{5,7},{6,4},{7,5},{8,10},{9,11},{10,... | collective-permute-start | bytes 393224 | tf_op jit(solution)/shard_map/ppermute | solution.py:39
  17.6 9.6 %collective-permute-start.6 = (bf16[32,2048]{1,0:T(8,128)(2,1)S(1)}, bf16[32,2048]{1,0:T(8,128)(2,1)S(1)}, u32[]{:S(2)}, u32[]{:S(2)}) collective-permute-start(bf16[32,2048]{1,0:T(8,128)(2,1)S(1)} %shard_map.112.refs_0_), channel_id=1, source_target_pairs={{0,3},{1,2},{2,1},{3,0},{4,7},{5,6},{6,5},{7,4},{8,11},{9,10},{10,... | collective-permute-start | bytes 393224 | tf_op jit(solution)/shard_map/ppermute | solution.py:39
  19.3 9.6 %collective-permute-start.5 = (bf16[128,2176]{1,0:T(8,128)(2,1)S(1)}, bf16[128,2176]{1,0:T(8,128)(2,1)S(1)}, u32[]{:S(2)}, u32[]{:S(2)}) collective-permute-start(bf16[128,2176]{1,0:T(8,128)(2,1)S(1)} %shard_map.114.refs_1_.refs_0_), channel_id=1, source_target_pairs={{0,16},{1,17},{2,18},{3,19},{4,12},{5,13},{6,14},{7,15},{8,24},{9,... | collective-permute-start | bytes 1671176 | tf_op jit(solution)/shard_map/ppermute | solution.py:39
  27.2 12.4 %collective-permute-start.15 = (bf16[128,2048]{1,0:T(8,128)(2,1)S(1)}, bf16[128,2048]{1,0:T(8,128)(2,1)S(1)}, u32[]{:S(2)}, u32[]{:S(2)}) collective-permute-start(bf16[128,2048]{1,0:T(8,128)(2,1)S(1)} %shard_map.115.refs_0_), channel_id=1, source_target_pairs={{0,4},{1,5},{2,6},{3,7},{4,0},{5,1},{6,2},{7,3},{8,12},{9,13},{10,... | collective-permute-start | bytes 1572872 | tf_op jit(solution)/shard_map/ppermute | solution.py:39
  27.2 9.2 %collective-permute-start.14 = (bf16[128,2048]{1,0:T(8,128)(2,1)S(1)}, bf16[128,2048]{1,0:T(8,128)(2,1)S(1)}, u32[]{:S(2)}, u32[]{:S(2)}) collective-permute-start(bf16[128,2048]{1,0:T(8,128)(2,1)S(1)} %shard_map.115.refs_0_), channel_id=1, source_target_pairs={{0,16},{1,17},{2,18},{3,19},{4,12},{5,13},{6,14},{7,15},{8,24},{9,... | collective-permute-start | bytes 1572872 | tf_op jit(solution)/shard_map/ppermute | solution.py:39
  27.8 4.6 %collective-permute-start.9 = (bf16[128,2176]{1,0:T(8,128)(2,1)S(1)}, bf16[128,2176]{1,0:T(8,128)(2,1)S(1)}, u32[]{:S(2)}, u32[]{:S(2)}) collective-permute-start(bf16[128,2176]{1,0:T(8,128)(2,1)S(1)} %shard_map.114.refs_1_.refs_0_), channel_id=1, source_target_pairs={{0,4},{1,5},{2,6},{3,7},{4,0},{5,1},{6,2},{7,3},{8,12},{9,13},{10,... | collective-permute-start | bytes 1671176 | tf_op jit(solution)/shard_map/ppermute | solution.py:39
  28.9 2.4 %collective-permute-start.10 = (bf16[128,2176]{1,0:T(8,128)(2,1)S(1)}, bf16[128,2176]{1,0:T(8,128)(2,1)S(1)}, u32[]{:S(2)}, u32[]{:S(2)}) collective-permute-start(bf16[128,2176]{1,0:T(8,128)(2,1)S(1)} %collective-permute-done.5.refs_1_.refs_2_), channel_id=1, source_target_pairs={{0,4},{1,5},{2,6},{3,7},{4,0},{5,1},{6,2},{7,3},{8,12},{9,13},{10,... | collective-permute-start | bytes 1671176 | tf_op jit(solution)/shard_map/ppermute | solution.py:39
  32.4 2.2 %collective-permute-start.12 = (bf16[128,2048]{1,0:T(8,128)(2,1)S(1)}, bf16[128,2048]{1,0:T(8,128)(2,1)S(1)}, u32[]{:S(2)}, u32[]{:S(2)}) collective-permute-start(bf16[128,2048]{1,0:T(8,128)(2,1)S(1)} %get-tuple-element.93), channel_id=1, source_target_pairs={{0,4},{1,5},{2,6},{3,7},{4,0},{5,1},{6,2},{7,3},{8,12},{9,13},{10,... | collective-permute-start | bytes 1572872 | tf_op jit(solution)/shard_map/ppermute | solution.py:39
  33.9 10.1 %collective-permute-start.11 = (bf16[128,2048]{1,0:T(8,128)(2,1)S(1)}, bf16[128,2048]{1,0:T(8,128)(2,1)S(1)}, u32[]{:S(2)}, u32[]{:S(2)}) collective-permute-start(bf16[128,2048]{1,0:T(8,128)(2,1)S(1)} %get-tuple-element.90), channel_id=1, source_target_pairs={{0,4},{1,5},{2,6},{3,7},{4,0},{5,1},{6,2},{7,3},{8,12},{9,13},{10,... | collective-permute-start | bytes 1572872 | tf_op jit(solution)/shard_map/ppermute | solution.py:39
  34.7 9.2 %collective-permute-start.13 = (bf16[128,2048]{1,0:T(8,128)(2,1)S(1)}, bf16[128,2048]{1,0:T(8,128)(2,1)S(1)}, u32[]{:S(2)}, u32[]{:S(2)}) collective-permute-start(bf16[128,2048]{1,0:T(8,128)(2,1)S(1)} %add_convert_fusion.2), channel_id=1, source_target_pairs={{0,16},{1,17},{2,18},{3,19},{4,12},{5,13},{6,14},{7,15},{8,24},{9,... | collective-permute-start | bytes 1572872 | tf_op jit(solution)/shard_map/ppermute | solution.py:39
  36.5 1.9 %collective-permute-start.16 = (bf16[128,2048]{1,0:T(8,128)(2,1)S(1)}, bf16[128,2048]{1,0:T(8,128)(2,1)S(1)}, u32[]{:S(2)}, u32[]{:S(2)}) collective-permute-start(bf16[128,2048]{1,0:T(8,128)(2,1)S(1)} %collective-permute-done.14.refs_0_), channel_id=1, source_target_pairs={{0,4},{1,5},{2,6},{3,7},{4,0},{5,1},{6,2},{7,3},{8,12},{9,13},{10,... | collective-permute-start | bytes 1572872 | tf_op jit(solution)/shard_map/ppermute | solution.py:39
  39.6 2.3 %collective-permute-start.17 = (bf16[128,2048]{1,0:T(8,128)(2,1)S(1)}, bf16[128,2048]{1,0:T(8,128)(2,1)S(1)}, u32[]{:S(2)}, u32[]{:S(2)}) collective-permute-start(bf16[128,2048]{1,0:T(8,128)(2,1)S(1)} %get-tuple-element.115), channel_id=1, source_target_pairs={{0,4},{1,5},{2,6},{3,7},{4,0},{5,1},{6,2},{7,3},{8,12},{9,13},{10,... | collective-permute-start | bytes 1572872 | tf_op jit(solution)/shard_map/ppermute | solution.py:39
  42.0 9.2 %collective-permute-start.19 = (bf16[128,2048]{1,0:T(8,128)(2,1)S(1)}, bf16[128,2048]{1,0:T(8,128)(2,1)S(1)}, u32[]{:S(2)}, u32[]{:S(2)}) collective-permute-start(bf16[128,2048]{1,0:T(8,128)(2,1)S(1)} %add_convert_fusion.1), channel_id=1, source_target_pairs={{0,16},{1,17},{2,18},{3,19},{4,12},{5,13},{6,14},{7,15},{8,24},{9,... | collective-permute-start | bytes 1572872 | tf_op jit(solution)/shard_map/ppermute | solution.py:39
  42.8 6.0 %collective-permute-start.18 = (bf16[128,2048]{1,0:T(8,128)(2,1)S(1)}, bf16[128,2048]{1,0:T(8,128)(2,1)S(1)}, u32[]{:S(2)}, u32[]{:S(2)}) collective-permute-start(bf16[128,2048]{1,0:T(8,128)(2,1)S(1)} %get-tuple-element.117), channel_id=1, source_target_pairs={{0,4},{1,5},{2,6},{3,7},{4,0},{5,1},{6,2},{7,3},{8,12},{9,13},{10,... | collective-permute-start | bytes 1572872 | tf_op jit(solution)/shard_map/ppermute | solution.py:39
  44.3 16.8 %collective-permute-start.23 = (bf16[32,2048]{1,0:T(8,128)(2,1)S(1)}, bf16[32,2048]{1,0:T(8,128)(2,1)S(1)}, u32[]{:S(2)}, u32[]{:S(2)}) collective-permute-start(bf16[32,2048]{1,0:T(8,128)(2,1)S(1)} %get-tuple-element.140), channel_id=1, source_target_pairs={{0,1},{1,0},{2,3},{3,2},{4,5},{5,4},{6,7},{7,6},{8,9},{9,8},{10,11... | collective-permute-start | bytes 393224 | tf_op jit(solution)/shard_map/ppermute | solution.py:39
  46.4 16.4 %collective-permute-start.22 = (bf16[32,2048]{1,0:T(8,128)(2,1)S(1)}, bf16[32,2048]{1,0:T(8,128)(2,1)S(1)}, u32[]{:S(2)}, u32[]{:S(2)}) collective-permute-start(bf16[32,2048]{1,0:T(8,128)(2,1)S(1)} %get-tuple-element.141), channel_id=1, source_target_pairs={{0,2},{1,3},{2,0},{3,1},{4,6},{5,7},{6,4},{7,5},{8,10},{9,11},{10,... | collective-permute-start | bytes 393224 | tf_op jit(solution)/shard_map/ppermute | solution.py:39
  47.4 15.3 %collective-permute-start.21 = (bf16[32,2048]{1,0:T(8,128)(2,1)S(1)}, bf16[32,2048]{1,0:T(8,128)(2,1)S(1)}, u32[]{:S(2)}, u32[]{:S(2)}) collective-permute-start(bf16[32,2048]{1,0:T(8,128)(2,1)S(1)} %get-tuple-element.142), channel_id=1, source_target_pairs={{0,3},{1,2},{2,1},{3,0},{4,7},{5,6},{6,5},{7,4},{8,11},{9,10},{10,... | collective-permute-start | bytes 393224 | tf_op jit(solution)/shard_map/ppermute | solution.py:39
  51.6 6.4 %collective-permute-start.20 = (bf16[64,2048]{1,0:T(8,128)(2,1)S(1)}, bf16[64,2048]{1,0:T(8,128)(2,1)S(1)}, u32[]{:S(2)}, u32[]{:S(2)}) collective-permute-start(bf16[64,2048]{1,0:T(8,128)(2,1)S(1)} %get-tuple-element.119), channel_id=1, source_target_pairs={{0,8},{1,9},{2,10},{3,11},{4,20},{5,21},{6,22},{7,23},{8,0},{9,1},... | collective-permute-start | bytes 786440 | tf_op jit(solution)/shard_map/ppermute | solution.py:39
  58.2 6.2 %collective-permute-start.27 = (bf16[16,2048]{1,0:T(8,128)(2,1)S(1)}, bf16[16,2048]{1,0:T(8,128)(2,1)S(1)}, u32[]{:S(2)}, u32[]{:S(2)}) collective-permute-start(bf16[16,2048]{1,0:T(8,128)(2,1)S(1)} %get-tuple-element.143), channel_id=1, source_target_pairs={{0,1},{1,0},{2,3},{3,2},{4,5},{5,4},{6,7},{7,6},{8,9},{9,8},{10,11... | collective-permute-start | bytes 196616 | tf_op jit(solution)/shard_map/ppermute | solution.py:39
  60.2 5.8 %collective-permute-start.26 = (bf16[16,2048]{1,0:T(8,128)(2,1)S(1)}, bf16[16,2048]{1,0:T(8,128)(2,1)S(1)}, u32[]{:S(2)}, u32[]{:S(2)}) collective-permute-start(bf16[16,2048]{1,0:T(8,128)(2,1)S(1)} %get-tuple-element.144), channel_id=1, source_target_pairs={{0,2},{1,3},{2,0},{3,1},{4,6},{5,7},{6,4},{7,5},{8,10},{9,11},{10,... | collective-permute-start | bytes 196616 | tf_op jit(solution)/shard_map/ppermute | solution.py:39
  61.1 6.2 %collective-permute-start.25 = (bf16[16,2048]{1,0:T(8,128)(2,1)S(1)}, bf16[16,2048]{1,0:T(8,128)(2,1)S(1)}, u32[]{:S(2)}, u32[]{:S(2)}) collective-permute-start(bf16[16,2048]{1,0:T(8,128)(2,1)S(1)} %get-tuple-element.145), channel_id=1, source_target_pairs={{0,3},{1,2},{2,1},{3,0},{4,7},{5,6},{6,5},{7,4},{8,11},{9,10},{10,... | collective-permute-start | bytes 196616 | tf_op jit(solution)/shard_map/ppermute | solution.py:39
  62.8 4.5 %collective-permute-start.24 = (bf16[16,2048]{1,0:T(8,128)(2,1)S(1)}, bf16[16,2048]{1,0:T(8,128)(2,1)S(1)}, u32[]{:S(2)}, u32[]{:S(2)}) collective-permute-start(bf16[16,2048]{1,0:T(8,128)(2,1)S(1)} %get-tuple-element.147), channel_id=1, source_target_pairs={{0,8},{1,9},{2,10},{3,11},{4,20},{5,21},{6,22},{7,23},{8,0},{9,1},... | collective-permute-start | bytes 196616 | tf_op jit(solution)/shard_map/ppermute | solution.py:39

commit v6 on v5

--- a/solution.py
+++ b/solution.py
@@ -220,6 +220,21 @@
     return specs + [pl.BlockSpec(w.shape, lambda i: (0, 0, 0)) for w in whole]
 
 
+def sum_kernel(*refs):
+    refs[-1][...] = functools.reduce(lambda x, y: x + y, [r[...].astype(F32) for r in refs[:-1]]).astype(BF16)
+
+
+def summed(*arrays, length=0.0):
+    return pl.pallas_call(
+        sum_kernel,
+        in_specs=[WHOLE] * len(arrays),
+        out_specs=WHOLE,
+        out_shape=pltpu.VMEM(arrays[0].shape, BF16),
+        compiler_params=params(4),
+        cost_estimate=cost(length),
+    )(*arrays)
+
+
 def last_sums_kernel(counts, *refs):
     taken, results, held, sems = refs[: sum(counts)], refs[-5:-3], refs[-3:-1], refs[-1]
     copies = []
@@ -297,14 +312,14 @@
 
 
 def forward_out_kernel(act, weight, weights, out):
-    out[...] = (weight[:, :1] * weights.out(act[...])).astype(BF16)
+    out[...] = (weight[:, :1] * weights.out(act[...])).astype(out.dtype)
 
 
 def forward_full_kernel(experts, width, expert, a, weights, act, gate_f, up_f, weight, out):
     p = expert_weight(experts, expert, a[:, width:])
     weight[...] = jnp.broadcast_to(p, weight.shape)
     act_val = hidden_units(a[:, :width], weights, act, gate_f, up_f)
-    out[...] = (p * weights.out(act_val)).astype(BF16)
+    out[...] = (p * weights.out(act_val)).astype(out.dtype)
 
 
 def hidden_cots(cot, weight, gate_f, up_f, weights, gate_cot, up_cot, out_cot):
@@ -322,12 +337,12 @@
 
 
 def backward_rows_kernel(gate, up, weights, out):
-    out[...] = weights.row_cot(gate[...], up[...]).astype(BF16)
+    out[...] = weights.row_cot(gate[...], up[...]).astype(out.dtype)
 
 
 def backward_full_kernel(cot, weight, gate_f, up_f, weights, gate_cot, up_cot, out_cot, out):
     gate, up = hidden_cots(cot[...], weight, gate_f, up_f, weights, gate_cot, up_cot, out_cot)
-    out[...] = weights.row_cot(gate, up).astype(BF16)
+    out[...] = weights.row_cot(gate, up).astype(out.dtype)
 
 
 def chunk_kernel(over_left, chunks, counts, *refs):
@@ -439,7 +454,7 @@
     expert, tokens = lax.optimization_barrier((expert, tokens))
     units = [(hidden, BF16), (hidden, F32), (hidden, F32), (128, F32)]
     cots = [(hidden, BF16), (hidden, BF16), (width, BF16)]
-    wide = (1, width, BF16)
+    wide, wide_kept = (1, width, BF16), (1, width, F32)
 
     def each(factor, arrays):
         return [(factor, *a) for a in arrays]
@@ -476,13 +491,15 @@
     row_late_other = send(row_late, core)
     f_own = over_rows(*forward(forward_hidden_kernel, [(1, row_late)], weights, each(1, units), 10.0))
     full = weights, each(1, units) + [wide], 10.0
-    *f_early_own, kept = over_rows(*forward(forward_full_kernel, [(1, after(row_lane, f_own[0]))], *full))
+    *f_early_own, kept = over_rows(
+        *forward(forward_full_kernel, [(1, after(row_lane, f_own[0]))], weights, each(1, units) + [wide_kept], 10.0)
+    )
     row_late_other_in = after(row_late_other, kept)
     *f_other, o_given = over_rows(*forward(forward_full_kernel, [(1, row_late_other_in)], *full))
     o_other = send(o_given, core)
     *f_early_other, given = over_rows(*forward(forward_full_kernel, [(1, after(row_other, f_other[0]))], *full))
     taken = [(1, f_own[0]), (1, after(f_own[3], given))]
-    (o_own,) = over_rows(forward_out_kernel, n, [], taken, weights, [wide])
+    (o_own,) = over_rows(forward_out_kernel, n, [], taken, weights, [wide_kept])
     o_late = halve(o_own, o_other)
     o_early_other = send(given, core)
     o_back = send(o_late, plane[-1])
@@ -493,14 +510,16 @@
     b_own = over_rows(backward_hidden_kernel, n, [], taken, weights, each(1, cots), 10.0)
     full = weights, each(1, cots) + [wide], 10.0
     taken = [(1, after(cot_lane, b_own[0]))] + with_units(f_early_own)
-    *b_early, g_kept = over_rows(backward_full_kernel, n, [], taken, *full)
+    *b_early, g_kept = over_rows(
+        backward_full_kernel, n, [], taken, weights, each(1, cots) + [wide_kept], 10.0
+    )
     taken = [(1, after(cot_late_other, g_kept))] + with_units(f_other)
     *b_other, g_given = over_rows(backward_full_kernel, n, [], taken, *full)
     g_other = send(g_given, core)
     taken = [(1, after(cot_other, b_other[0]))] + with_units(f_early_other)
     *b_early_other, g_early = over_rows(backward_full_kernel, n, [], taken, *full)
     taken = [(1, b_own[0]), (1, after(b_own[1], g_early))]
-    (g_own,) = over_rows(backward_rows_kernel, n, [], taken, weights, [wide])
+    (g_own,) = over_rows(backward_rows_kernel, n, [], taken, weights, [wide_kept])
     g_late = halve(g_own, g_other)
     g_early_other = send(after(g_early, g_late), core)
     g_back = send(g_late, plane[-1])
@@ -525,12 +544,12 @@
     g_lane = add(parts[0], after(parts[1], gate_grad, down_grad)).astype(BF16)
     g_terms = line_sends(g_lane)
     o_terms = line_sends(add(kept, o_early_other, o_back).astype(BF16))
-    parts = (join(after(o_terms[0], g_lane), length=20.0), *o_terms[1:])
+    parts = (join(after(o_terms[0], g_lane), length=20.0), *o_terms[:0:-1])
     for p in reversed(plane[:-1]):
         lane = add(*parts).astype(BF16)
         half = lane.shape[0] // 2
         parts = (lane[:half], send(lane[half:], p))
-    mixed, token_grad = last_sums(parts, g_terms)
+    mixed, token_grad = last_sums(parts, [summed(*g_terms[:1], *g_terms[:0:-1], length=10.0)])
     return mixed, token_grad, gate_grad, up_grad, down_grad
 
 

time: 68.4 us -> 67.9 us (level)
  starting transfers between devices: 32.3 us -> 31.4 us
    ppermute x28, starting transfers between devices: 32.3 us -> 31.4 us  [send(): return lax.ppermute(x, AXES, pairs)]
  transfers between devices with their start and end apart: 28 -> 28, of which waited for: 11 -> 13; matrix products, arithmetic and copies ran while one was open for 1% -> 1% of each run, Pallas kernels for 25% -> 25%
where the time goes in v6:
time: 67.9 us; the launch traced here: 67.7 us
  starting transfers between devices  31.4 us (46%)
  Pallas kernels  18.8 us (28%)
  waiting for transfers between devices  15.8 us (23%)
  between operations  1.07 us (2%)
    ppermute x28, starting transfers between devices, send(): return lax.ppermute(x, AXES, pairs)  31.4 us
    ppermute x28, waiting for transfers between devices, send(): return lax.ppermute(x, AXES, pairs)  15.8 us
    pallas_call x10, Pallas kernels, over_rows(): pl.pallas_call(run, out_shape=shaped(*[((f * n, w), t) for f, w, t in giv...  9.22 us
    pallas_call x2, Pallas kernels, gradients_by_chunks(): pl.pallas_call(functools.partial(chunk_kernel, over_left, chunks, [len(g)...  4.76 us
    pallas_call x1, Pallas kernels, stage(): pl.pallas_call(stage_kernel, in_specs=[ANY] * 3, out_specs=[WHOLE] * 2, o...  2.86 us
  transfers between devices with their start and end apart: 28, of which 13 were waited for; matrix products, arithmetic and copies ran while one was open for 1% of the time, Pallas kernels for 25%

profile of v6, /device:TPU:0, one launch (start us, length us, event | category | flops | bytes accessed | tf_op | source)
XLA Modules:
  0.0 67.7 jit_solution(16655768229341026864)
XLA Ops:
  0.6 0.9 %shard_map.110 = (bf16[16,2176]{1,0:T(8,128)(2,1)S(1)}, bf16[16,2048]{1,0:T(8,128)(2,1)S(1)}) custom-call(bf16[16,2048]{1,0:T(8,128)(2,1)} %tokens, bf16[16,2048]{1,0:T(8,128)(2,1)} %cotangent.1, s32[8,16]{1,0:T(8,128)} %bitcast.3, f32[8,16]{1,0:T(8,128)} %bitcast.4), custom_call_target="tpu_custom_call" | custom-call | tf_op jit(solution)/shard_map/pallas_call | solution.py:111
  1.6 5.1 %collective-permute-start.3 = (bf16[16,2176]{1,0:T(8,128)(2,1)S(1)}, bf16[16,2176]{1,0:T(8,128)(2,1)S(1)}, u32[]{:S(2)}, u32[]{:S(2)}) collective-permute-start(bf16[16,2176]{1,0:T(8,128)(2,1)S(1)} %get-tuple-element.80.refs_0_), channel_id=1, source_target_pairs={{0,3},{1,2},{2,1},{3,0},{4,7},{5,6},{6,5},{7,4},{8,11},{9,10},{10,... | collective-permute-start | bytes 208904 | tf_op jit(solution)/shard_map/ppermute | solution.py:39
  7.3 1.6 %collective-permute-start = (bf16[16,2048]{1,0:T(8,128)(2,1)S(1)}, bf16[16,2048]{1,0:T(8,128)(2,1)S(1)}, u32[]{:S(2)}, u32[]{:S(2)}) collective-permute-start(bf16[16,2048]{1,0:T(8,128)(2,1)S(1)} %get-tuple-element.79.refs_0_), channel_id=1, source_target_pairs={{0,8},{1,9},{2,10},{3,11},{4,20},{5,21},{6,22},{7,23},{8,0},{9,1},... | collective-permute-start | bytes 196616 | tf_op jit(solution)/shard_map/ppermute | solution.py:39
  9.0 2.9 %shard_map.111 = (bf16[3,2048,384]{2,1,0:T(8,128)(2,1)S(1)}, bf16[3,384,2048]{2,1,0:T(8,128)(2,1)S(1)}) custom-call(bf16[1,2048,384]{2,1,0:T(8,128)(2,1)} %gate, bf16[1,2048,384]{2,1,0:T(8,128)(2,1)} %up, bf16[1,384,2048]{2,1,0:T(8,128)(2,1)} %down), custom_call_target="tpu_custom_call" | custom-call | tf_op jit(solution)/shard_map/pallas_call | solution.py:142
  12.6 1.6 %collective-permute-start.4 = (bf16[64,2176]{1,0:T(8,128)(2,1)S(1)}, bf16[64,2176]{1,0:T(8,128)(2,1)S(1)}, u32[]{:S(2)}, u32[]{:S(2)}) collective-permute-start(bf16[64,2176]{1,0:T(8,128)(2,1)S(1)} %shard_map.113.refs_0_), channel_id=1, source_target_pairs={{0,8},{1,9},{2,10},{3,11},{4,20},{5,21},{6,22},{7,23},{8,0},{9,1},... | collective-permute-start | bytes 835592 | tf_op jit(solution)/shard_map/ppermute | solution.py:39
  14.2 1.0 %collective-permute-start.8 = (bf16[32,2048]{1,0:T(8,128)(2,1)S(1)}, bf16[32,2048]{1,0:T(8,128)(2,1)S(1)}, u32[]{:S(2)}, u32[]{:S(2)}) collective-permute-start(bf16[32,2048]{1,0:T(8,128)(2,1)S(1)} %shard_map.112.refs_0_), channel_id=1, source_target_pairs={{0,1},{1,0},{2,3},{3,2},{4,5},{5,4},{6,7},{7,6},{8,9},{9,8},{10,11... | collective-permute-start | bytes 393224 | tf_op jit(solution)/shard_map/ppermute | solution.py:39
  15.2 2.3 %collective-permute-start.7 = (bf16[32,2048]{1,0:T(8,128)(2,1)S(1)}, bf16[32,2048]{1,0:T(8,128)(2,1)S(1)}, u32[]{:S(2)}, u32[]{:S(2)}) collective-permute-start(bf16[32,2048]{1,0:T(8,128)(2,1)S(1)} %shard_map.112.refs_0_), channel_id=1, source_target_pairs={{0,2},{1,3},{2,0},{3,1},{4,6},{5,7},{6,4},{7,5},{8,10},{9,11},{10,... | collective-permute-start | bytes 393224 | tf_op jit(solution)/shard_map/ppermute | solution.py:39
  17.6 1.0 %collective-permute-start.6 = (bf16[32,2048]{1,0:T(8,128)(2,1)S(1)}, bf16[32,2048]{1,0:T(8,128)(2,1)S(1)}, u32[]{:S(2)}, u32[]{:S(2)}) collective-permute-start(bf16[32,2048]{1,0:T(8,128)(2,1)S(1)} %shard_map.112.refs_0_), channel_id=1, source_target_pairs={{0,3},{1,2},{2,1},{3,0},{4,7},{5,6},{6,5},{7,4},{8,11},{9,10},{10,... | collective-permute-start | bytes 393224 | tf_op jit(solution)/shard_map/ppermute | solution.py:39
  19.3 1.6 %collective-permute-start.5 = (bf16[128,2176]{1,0:T(8,128)(2,1)S(1)}, bf16[128,2176]{1,0:T(8,128)(2,1)S(1)}, u32[]{:S(2)}, u32[]{:S(2)}) collective-permute-start(bf16[128,2176]{1,0:T(8,128)(2,1)S(1)} %shard_map.114.refs_1_.refs_0_), channel_id=1, source_target_pairs={{0,16},{1,17},{2,18},{3,19},{4,12},{5,13},{6,14},{7,15},{8,24},{9,... | collective-permute-start | bytes 1671176 | tf_op jit(solution)/shard_map/ppermute | solution.py:39
  20.9 6.2 %collective-permute-done.7.refs_2_ = bf16[32,2048]{1,0:T(8,128)(2,1)S(1)} collective-permute-done((bf16[32,2048]{1,0:T(8,128)(2,1)S(1)}, bf16[32,2048]{1,0:T(8,128)(2,1)S(1)}, u32[]{:S(2)}, u32[]{:S(2)}) %collective-permute-start.7) | collective-permute-done | bytes 131104 | tf_op jit(solution)/shard_map/ppermute | solution.py:39
  27.8 1.1 %collective-permute-start.9 = (bf16[128,2176]{1,0:T(8,128)(2,1)S(1)}, bf16[128,2176]{1,0:T(8,128)(2,1)S(1)}, u32[]{:S(2)}, u32[]{:S(2)}) collective-permute-start(bf16[128,2176]{1,0:T(8,128)(2,1)S(1)} %shard_map.114.refs_1_.refs_0_), channel_id=1, source_target_pairs={{0,4},{1,5},{2,6},{3,7},{4,0},{5,1},{6,2},{7,3},{8,12},{9,13},{10,... | collective-permute-start | bytes 1671176 | tf_op jit(solution)/shard_map/ppermute | solution.py:39
  29.6 1.1 %shard_map.117 = (bf16[128,384]{1,0:T(8,128)(2,1)S(1)}, f32[128,384]{1,0:T(8,128)S(1)}, f32[128,384]{1,0:T(8,128)S(1)}, f32[128,128]{1,0:T(8,128)S(1)}, f32[128,2048]{1,0:T(8,128)S(1)}) custom-call(s32[1,1]{1,0:T(1,128)} %bitcast.refs_0_, bf16[128,2176]{1,0:T(8,128)(2,1)S(1)} %shard_map.114.refs_1_.refs_0_, ...), custom_call_target="tpu_custom_call" | custom-call | flops 11500000256 | tf_op jit(solution)/shard_map/pallas_call | solution.py:280
  31.3 1.1 %shard_map.118 = (bf16[128,384]{1,0:T(8,128)(2,1)S(1)}, f32[128,384]{1,0:T(8,128)S(1)}, f32[128,384]{1,0:T(8,128)S(1)}, f32[128,128]{1,0:T(8,128)S(1)}, bf16[128,2048]{1,0:T(8,128)(2,1)S(1)}) custom-call(s32[1,1]{1,0:T(1,128)} %bitcast.refs_0_, bf16[128,2176]{1,0:T(8,128)(2,1)S(1)} %collective-permute-done.10.refs_1_.refs_3_, ...), custom_call_target="tpu_custom_call" | custom-call | flops 11500000256 | tf_op jit(solution)/shard_map/pallas_call | solution.py:280
  32.8 1.1 %shard_map.119 = (bf16[128,384]{1,0:T(8,128)(2,1)S(1)}, f32[128,384]{1,0:T(8,128)S(1)}, f32[128,384]{1,0:T(8,128)S(1)}, f32[128,128]{1,0:T(8,128)S(1)}, bf16[128,2048]{1,0:T(8,128)(2,1)S(1)}) custom-call(s32[1,1]{1,0:T(1,128)} %bitcast.refs_0_, bf16[128,2176]{1,0:T(8,128)(2,1)S(1)} %collective-permute-done.9.refs_1_, ...), custom_call_target="tpu_custom_call" | custom-call | flops 11500000256 | tf_op jit(solution)/shard_map/pallas_call | solution.py:280
  34.7 1.2 %collective-permute-start.13 = (bf16[128,2048]{1,0:T(8,128)(2,1)S(1)}, bf16[128,2048]{1,0:T(8,128)(2,1)S(1)}, u32[]{:S(2)}, u32[]{:S(2)}) collective-permute-start(bf16[128,2048]{1,0:T(8,128)(2,1)S(1)} %add_convert_fusion.2), channel_id=1, source_target_pairs={{0,16},{1,17},{2,18},{3,19},{4,12},{5,13},{6,14},{7,15},{8,24},{9,... | collective-permute-start | bytes 1572872 | tf_op jit(solution)/shard_map/ppermute | solution.py:39
  37.0 1.2 %shard_map.122 = (bf16[128,384]{1,0:T(8,128)(2,1)S(1)}, bf16[128,384]{1,0:T(8,128)(2,1)S(1)}, bf16[128,2048]{1,0:T(8,128)(2,1)S(1)}, f32[128,2048]{1,0:T(8,128)S(1)}) custom-call(bf16[128,2048]{1,0:T(8,128)(2,1)S(1)} %shard_map.115.refs_0_, f32[128,128]{1,0:T(8,128)S(1)} %get-tuple-element.100.refs_1_, f32[128,384]{1,0:T(8,128)S(1)} %get-tuple-element.101.refs_2_, ...), custom_call_target="tpu_custom_call" | custom-call | flops 11500000256 | tf_op jit(solution)/shard_map/pallas_call | solution.py:280
  38.4 1.2 %shard_map.123 = (bf16[128,384]{1,0:T(8,128)(2,1)S(1)}, bf16[128,384]{1,0:T(8,128)(2,1)S(1)}, bf16[128,2048]{1,0:T(8,128)(2,1)S(1)}, bf16[128,2048]{1,0:T(8,128)(2,1)S(1)}) custom-call(bf16[128,2048]{1,0:T(8,128)(2,1)S(1)} %collective-permute-done.16.refs_0_, f32[128,128]{1,0:T(8,128)S(1)} %get-tuple-element.105.refs_1_, ...), custom_call_target="tpu_custom_call" | custom-call | flops 11500000256 | tf_op jit(solution)/shard_map/pallas_call | solution.py:280
  40.0 1.2 %shard_map.124 = (bf16[128,384]{1,0:T(8,128)(2,1)S(1)}, bf16[128,384]{1,0:T(8,128)(2,1)S(1)}, bf16[128,2048]{1,0:T(8,128)(2,1)S(1)}, bf16[128,2048]{1,0:T(8,128)(2,1)S(1)}) custom-call(bf16[128,2048]{1,0:T(8,128)(2,1)S(1)} %collective-permute-done.15.refs_0_, f32[128,128]{1,0:T(8,128)S(1)} %get-tuple-element.110.refs_1_, ...), custom_call_target="tpu_custom_call" | custom-call | flops 11500000256 | tf_op jit(solution)/shard_map/pallas_call | solution.py:280
  42.0 0.8 %collective-permute-start.19 = (bf16[128,2048]{1,0:T(8,128)(2,1)S(1)}, bf16[128,2048]{1,0:T(8,128)(2,1)S(1)}, u32[]{:S(2)}, u32[]{:S(2)}) collective-permute-start(bf16[128,2048]{1,0:T(8,128)(2,1)S(1)} %add_convert_fusion.1), channel_id=1, source_target_pairs={{0,16},{1,17},{2,18},{3,19},{4,12},{5,13},{6,14},{7,15},{8,24},{9,... | collective-permute-start | bytes 1572872 | tf_op jit(solution)/shard_map/ppermute | solution.py:39
  42.7 1.2 %collective-permute-done.13 = bf16[128,2048]{1,0:T(8,128)(2,1)S(1)} collective-permute-done((bf16[128,2048]{1,0:T(8,128)(2,1)S(1)}, bf16[128,2048]{1,0:T(8,128)(2,1)S(1)}, u32[]{:S(2)}, u32[]{:S(2)}) %collective-permute-start.13) | collective-permute-done | bytes 524320 | tf_op jit(solution)/shard_map/ppermute | solution.py:39
  44.2 2.5 %collective-permute-start.23 = (bf16[32,2048]{1,0:T(8,128)(2,1)S(1)}, bf16[32,2048]{1,0:T(8,128)(2,1)S(1)}, u32[]{:S(2)}, u32[]{:S(2)}) collective-permute-start(bf16[32,2048]{1,0:T(8,128)(2,1)S(1)} %get-tuple-element.140), channel_id=1, source_target_pairs={{0,3},{1,2},{2,1},{3,0},{4,7},{5,6},{6,5},{7,4},{8,11},{9,10},{10,... | collective-permute-start | bytes 393224 | tf_op jit(solution)/shard_map/ppermute | solution.py:39
  46.8 1.0 %collective-permute-start.22 = (bf16[32,2048]{1,0:T(8,128)(2,1)S(1)}, bf16[32,2048]{1,0:T(8,128)(2,1)S(1)}, u32[]{:S(2)}, u32[]{:S(2)}) collective-permute-start(bf16[32,2048]{1,0:T(8,128)(2,1)S(1)} %get-tuple-element.141), channel_id=1, source_target_pairs={{0,2},{1,3},{2,0},{3,1},{4,6},{5,7},{6,4},{7,5},{8,10},{9,11},{10,... | collective-permute-start | bytes 393224 | tf_op jit(solution)/shard_map/ppermute | solution.py:39
  47.7 0.9 %collective-permute-start.21 = (bf16[32,2048]{1,0:T(8,128)(2,1)S(1)}, bf16[32,2048]{1,0:T(8,128)(2,1)S(1)}, u32[]{:S(2)}, u32[]{:S(2)}) collective-permute-start(bf16[32,2048]{1,0:T(8,128)(2,1)S(1)} %get-tuple-element.142), channel_id=1, source_target_pairs={{0,1},{1,0},{2,3},{3,2},{4,5},{5,4},{6,7},{7,6},{8,9},{9,8},{10,11... | collective-permute-start | bytes 393224 | tf_op jit(solution)/shard_map/ppermute | solution.py:39
  48.7 2.6 %collective-permute-done.19.refs_2_ = bf16[128,2048]{1,0:T(8,128)(2,1)S(1)} collective-permute-done((bf16[128,2048]{1,0:T(8,128)(2,1)S(1)}, bf16[128,2048]{1,0:T(8,128)(2,1)S(1)}, u32[]{:S(2)}, u32[]{:S(2)}) %collective-permute-start.19) | collective-permute-done | bytes 524320 | tf_op jit(solution)/shard_map/ppermute | solution.py:39
  51.4 1.5 %collective-permute-start.20 = (bf16[64,2048]{1,0:T(8,128)(2,1)S(1)}, bf16[64,2048]{1,0:T(8,128)(2,1)S(1)}, u32[]{:S(2)}, u32[]{:S(2)}) collective-permute-start(bf16[64,2048]{1,0:T(8,128)(2,1)S(1)} %get-tuple-element.119), channel_id=1, source_target_pairs={{0,8},{1,9},{2,10},{3,11},{4,20},{5,21},{6,22},{7,23},{8,0},{9,1},... | collective-permute-start | bytes 786440 | tf_op jit(solution)/shard_map/ppermute | solution.py:39
  52.9 2.0 %shard_map.128 = bf16[1,384,2048]{2,1,0:T(8,128)(2,1)} custom-call(bf16[128,384]{1,0:T(8,128)(2,1)S(1)} %get-tuple-element.128.refs_0_, bf16[128,384]{1,0:T(8,128)(2,1)S(1)} %get-tuple-element.129.refs_1_, bf16[128,384]{1,0:T(8,128)(2,1)S(1)} %get-tuple-element.84.refs_0_.refs_2_, bf16[128,384]{1,0:T(8,128)(2,1)S(1)} %get-tuple-element.88.refs_3_, ...), custom_call_target="tpu_custom_call" | custom-call | flops 11500000256 | tf_op jit(solution)/shard_map/pallas_call | solution.py:380
  54.9 2.8 %shard_map.127 = (bf16[1,2048,384]{2,1,0:T(8,128)(2,1)}, bf16[1,2048,384]{2,1,0:T(8,128)(2,1)}) custom-call(bf16[128,2176]{1,0:T(8,128)(2,1)S(1)} %shard_map.114.refs_1_.refs_0_, bf16[128,2176]{1,0:T(8,128)(2,1)S(1)} %collective-permute-done.9.refs_1_, bf16[128,2176]{1,0:T(8,128)(2,1)S(1)} %collective-permute-done.5.refs_1_.refs_2_, ...), custom_call_target="tpu_custom_call" | custom-call | flops 11500000256 | tf_op jit(solution)/shard_map/pallas_call | solution.py:380
  57.9 2.4 %collective-permute-start.27 = (bf16[16,2048]{1,0:T(8,128)(2,1)S(1)}, bf16[16,2048]{1,0:T(8,128)(2,1)S(1)}, u32[]{:S(2)}, u32[]{:S(2)}) collective-permute-start(bf16[16,2048]{1,0:T(8,128)(2,1)S(1)} %get-tuple-element.143), channel_id=1, source_target_pairs={{0,3},{1,2},{2,1},{3,0},{4,7},{5,6},{6,5},{7,4},{8,11},{9,10},{10,... | collective-permute-start | bytes 196616 | tf_op jit(solution)/shard_map/ppermute | solution.py:39
  60.3 1.1 %collective-permute-start.26 = (bf16[16,2048]{1,0:T(8,128)(2,1)S(1)}, bf16[16,2048]{1,0:T(8,128)(2,1)S(1)}, u32[]{:S(2)}, u32[]{:S(2)}) collective-permute-start(bf16[16,2048]{1,0:T(8,128)(2,1)S(1)} %get-tuple-element.144), channel_id=1, source_target_pairs={{0,2},{1,3},{2,0},{3,1},{4,6},{5,7},{6,4},{7,5},{8,10},{9,11},{10,... | collective-permute-start | bytes 196616 | tf_op jit(solution)/shard_map/ppermute | solution.py:39
  61.4 1.0 %collective-permute-start.25 = (bf16[16,2048]{1,0:T(8,128)(2,1)S(1)}, bf16[16,2048]{1,0:T(8,128)(2,1)S(1)}, u32[]{:S(2)}, u32[]{:S(2)}) collective-permute-start(bf16[16,2048]{1,0:T(8,128)(2,1)S(1)} %get-tuple-element.145), channel_id=1, source_target_pairs={{0,1},{1,0},{2,3},{3,2},{4,5},{5,4},{6,7},{7,6},{8,9},{9,8},{10,11... | collective-permute-start | bytes 196616 | tf_op jit(solution)/shard_map/ppermute | solution.py:39
  62.5 1.5 %collective-permute-start.24 = (bf16[16,2048]{1,0:T(8,128)(2,1)S(1)}, bf16[16,2048]{1,0:T(8,128)(2,1)S(1)}, u32[]{:S(2)}, u32[]{:S(2)}) collective-permute-start(bf16[16,2048]{1,0:T(8,128)(2,1)S(1)} %get-tuple-element.147), channel_id=1, source_target_pairs={{0,8},{1,9},{2,10},{3,11},{4,20},{5,21},{6,22},{7,23},{8,0},{9,1},... | collective-permute-start | bytes 196616 | tf_op jit(solution)/shard_map/ppermute | solution.py:39
  64.7 1.6 %collective-permute-done.26.refs_2_ = bf16[16,2048]{1,0:T(8,128)(2,1)S(1)} collective-permute-done((bf16[16,2048]{1,0:T(8,128)(2,1)S(1)}, bf16[16,2048]{1,0:T(8,128)(2,1)S(1)}, u32[]{:S(2)}, u32[]{:S(2)}) %collective-permute-start.26) | collective-permute-done | bytes 65568 | tf_op jit(solution)/shard_map/ppermute | solution.py:39
  (54 shorter events, 10.5 us)
Async XLA Ops:
  1.6 10.3 %collective-permute-start.3 = (bf16[16,2176]{1,0:T(8,128)(2,1)S(1)}, bf16[16,2176]{1,0:T(8,128)(2,1)S(1)}, u32[]{:S(2)}, u32[]{:S(2)}) collective-permute-start(bf16[16,2176]{1,0:T(8,128)(2,1)S(1)} %get-tuple-element.80.refs_0_), channel_id=1, source_target_pairs={{0,3},{1,2},{2,1},{3,0},{4,7},{5,6},{6,5},{7,4},{8,11},{9,10},{10,... | collective-permute-start | bytes 208904 | tf_op jit(solution)/shard_map/ppermute | solution.py:39
  6.7 5.9 %collective-permute-start.2 = (bf16[16,2176]{1,0:T(8,128)(2,1)S(1)}, bf16[16,2176]{1,0:T(8,128)(2,1)S(1)}, u32[]{:S(2)}, u32[]{:S(2)}) collective-permute-start(bf16[16,2176]{1,0:T(8,128)(2,1)S(1)} %get-tuple-element.80.refs_0_), channel_id=1, source_target_pairs={{0,2},{1,3},{2,0},{3,1},{4,6},{5,7},{6,4},{7,5},{8,10},{9,11},{10,... | collective-permute-start | bytes 208904 | tf_op jit(solution)/shard_map/ppermute | solution.py:39
  6.7 5.9 %collective-permute-start.1 = (bf16[16,2176]{1,0:T(8,128)(2,1)S(1)}, bf16[16,2176]{1,0:T(8,128)(2,1)S(1)}, u32[]{:S(2)}, u32[]{:S(2)}) collective-permute-start(bf16[16,2176]{1,0:T(8,128)(2,1)S(1)} %get-tuple-element.80.refs_0_), channel_id=1, source_target_pairs={{0,1},{1,0},{2,3},{3,2},{4,5},{5,4},{6,7},{7,6},{8,9},{9,8},{10,11... | collective-permute-start | bytes 208904 | tf_op jit(solution)/shard_map/ppermute | solution.py:39
  7.3 4.5 %collective-permute-start = (bf16[16,2048]{1,0:T(8,128)(2,1)S(1)}, bf16[16,2048]{1,0:T(8,128)(2,1)S(1)}, u32[]{:S(2)}, u32[]{:S(2)}) collective-permute-start(bf16[16,2048]{1,0:T(8,128)(2,1)S(1)} %get-tuple-element.79.refs_0_), channel_id=1, source_target_pairs={{0,8},{1,9},{2,10},{3,11},{4,20},{5,21},{6,22},{7,23},{8,0},{9,1},... | collective-permute-start | bytes 196616 | tf_op jit(solution)/shard_map/ppermute | solution.py:39
  12.6 6.6 %collective-permute-start.4 = (bf16[64,2176]{1,0:T(8,128)(2,1)S(1)}, bf16[64,2176]{1,0:T(8,128)(2,1)S(1)}, u32[]{:S(2)}, u32[]{:S(2)}) collective-permute-start(bf16[64,2176]{1,0:T(8,128)(2,1)S(1)} %shard_map.113.refs_0_), channel_id=1, source_target_pairs={{0,8},{1,9},{2,10},{3,11},{4,20},{5,21},{6,22},{7,23},{8,0},{9,1},... | collective-permute-start | bytes 835592 | tf_op jit(solution)/shard_map/ppermute | solution.py:39
  14.2 6.7 %collective-permute-start.8 = (bf16[32,2048]{1,0:T(8,128)(2,1)S(1)}, bf16[32,2048]{1,0:T(8,128)(2,1)S(1)}, u32[]{:S(2)}, u32[]{:S(2)}) collective-permute-start(bf16[32,2048]{1,0:T(8,128)(2,1)S(1)} %shard_map.112.refs_0_), channel_id=1, source_target_pairs={{0,1},{1,0},{2,3},{3,2},{4,5},{5,4},{6,7},{7,6},{8,9},{9,8},{10,11... | collective-permute-start | bytes 393224 | tf_op jit(solution)/shard_map/ppermute | solution.py:39
  15.2 11.9 %collective-permute-start.7 = (bf16[32,2048]{1,0:T(8,128)(2,1)S(1)}, bf16[32,2048]{1,0:T(8,128)(2,1)S(1)}, u32[]{:S(2)}, u32[]{:S(2)}) collective-permute-start(bf16[32,2048]{1,0:T(8,128)(2,1)S(1)} %shard_map.112.refs_0_), channel_id=1, source_target_pairs={{0,2},{1,3},{2,0},{3,1},{4,6},{5,7},{6,4},{7,5},{8,10},{9,11},{10,... | collective-permute-start | bytes 393224 | tf_op jit(solution)/shard_map/ppermute | solution.py:39
  17.6 9.6 %collective-permute-start.6 = (bf16[32,2048]{1,0:T(8,128)(2,1)S(1)}, bf16[32,2048]{1,0:T(8,128)(2,1)S(1)}, u32[]{:S(2)}, u32[]{:S(2)}) collective-permute-start(bf16[32,2048]{1,0:T(8,128)(2,1)S(1)} %shard_map.112.refs_0_), channel_id=1, source_target_pairs={{0,3},{1,2},{2,1},{3,0},{4,7},{5,6},{6,5},{7,4},{8,11},{9,10},{10,... | collective-permute-start | bytes 393224 | tf_op jit(solution)/shard_map/ppermute | solution.py:39
  19.3 9.6 %collective-permute-start.5 = (bf16[128,2176]{1,0:T(8,128)(2,1)S(1)}, bf16[128,2176]{1,0:T(8,128)(2,1)S(1)}, u32[]{:S(2)}, u32[]{:S(2)}) collective-permute-start(bf16[128,2176]{1,0:T(8,128)(2,1)S(1)} %shard_map.114.refs_1_.refs_0_), channel_id=1, source_target_pairs={{0,16},{1,17},{2,18},{3,19},{4,12},{5,13},{6,14},{7,15},{8,24},{9,... | collective-permute-start | bytes 1671176 | tf_op jit(solution)/shard_map/ppermute | solution.py:39
  27.2 12.4 %collective-permute-start.15 = (bf16[128,2048]{1,0:T(8,128)(2,1)S(1)}, bf16[128,2048]{1,0:T(8,128)(2,1)S(1)}, u32[]{:S(2)}, u32[]{:S(2)}) collective-permute-start(bf16[128,2048]{1,0:T(8,128)(2,1)S(1)} %shard_map.115.refs_0_), channel_id=1, source_target_pairs={{0,4},{1,5},{2,6},{3,7},{4,0},{5,1},{6,2},{7,3},{8,12},{9,13},{10,... | collective-permute-start | bytes 1572872 | tf_op jit(solution)/shard_map/ppermute | solution.py:39
  27.2 9.2 %collective-permute-start.14 = (bf16[128,2048]{1,0:T(8,128)(2,1)S(1)}, bf16[128,2048]{1,0:T(8,128)(2,1)S(1)}, u32[]{:S(2)}, u32[]{:S(2)}) collective-permute-start(bf16[128,2048]{1,0:T(8,128)(2,1)S(1)} %shard_map.115.refs_0_), channel_id=1, source_target_pairs={{0,16},{1,17},{2,18},{3,19},{4,12},{5,13},{6,14},{7,15},{8,24},{9,... | collective-permute-start | bytes 1572872 | tf_op jit(solution)/shard_map/ppermute | solution.py:39
  27.8 4.6 %collective-permute-start.9 = (bf16[128,2176]{1,0:T(8,128)(2,1)S(1)}, bf16[128,2176]{1,0:T(8,128)(2,1)S(1)}, u32[]{:S(2)}, u32[]{:S(2)}) collective-permute-start(bf16[128,2176]{1,0:T(8,128)(2,1)S(1)} %shard_map.114.refs_1_.refs_0_), channel_id=1, source_target_pairs={{0,4},{1,5},{2,6},{3,7},{4,0},{5,1},{6,2},{7,3},{8,12},{9,13},{10,... | collective-permute-start | bytes 1671176 | tf_op jit(solution)/shard_map/ppermute | solution.py:39
  28.9 2.4 %collective-permute-start.10 = (bf16[128,2176]{1,0:T(8,128)(2,1)S(1)}, bf16[128,2176]{1,0:T(8,128)(2,1)S(1)}, u32[]{:S(2)}, u32[]{:S(2)}) collective-permute-start(bf16[128,2176]{1,0:T(8,128)(2,1)S(1)} %collective-permute-done.5.refs_1_.refs_2_), channel_id=1, source_target_pairs={{0,4},{1,5},{2,6},{3,7},{4,0},{5,1},{6,2},{7,3},{8,12},{9,13},{10,... | collective-permute-start | bytes 1671176 | tf_op jit(solution)/shard_map/ppermute | solution.py:39
  32.4 2.2 %collective-permute-start.12 = (bf16[128,2048]{1,0:T(8,128)(2,1)S(1)}, bf16[128,2048]{1,0:T(8,128)(2,1)S(1)}, u32[]{:S(2)}, u32[]{:S(2)}) collective-permute-start(bf16[128,2048]{1,0:T(8,128)(2,1)S(1)} %get-tuple-element.93), channel_id=1, source_target_pairs={{0,4},{1,5},{2,6},{3,7},{4,0},{5,1},{6,2},{7,3},{8,12},{9,13},{10,... | collective-permute-start | bytes 1572872 | tf_op jit(solution)/shard_map/ppermute | solution.py:39
  33.9 10.0 %collective-permute-start.11 = (bf16[128,2048]{1,0:T(8,128)(2,1)S(1)}, bf16[128,2048]{1,0:T(8,128)(2,1)S(1)}, u32[]{:S(2)}, u32[]{:S(2)}) collective-permute-start(bf16[128,2048]{1,0:T(8,128)(2,1)S(1)} %get-tuple-element.90), channel_id=1, source_target_pairs={{0,4},{1,5},{2,6},{3,7},{4,0},{5,1},{6,2},{7,3},{8,12},{9,13},{10,... | collective-permute-start | bytes 1572872 | tf_op jit(solution)/shard_map/ppermute | solution.py:39
  34.7 9.2 %collective-permute-start.13 = (bf16[128,2048]{1,0:T(8,128)(2,1)S(1)}, bf16[128,2048]{1,0:T(8,128)(2,1)S(1)}, u32[]{:S(2)}, u32[]{:S(2)}) collective-permute-start(bf16[128,2048]{1,0:T(8,128)(2,1)S(1)} %add_convert_fusion.2), channel_id=1, source_target_pairs={{0,16},{1,17},{2,18},{3,19},{4,12},{5,13},{6,14},{7,15},{8,24},{9,... | collective-permute-start | bytes 1572872 | tf_op jit(solution)/shard_map/ppermute | solution.py:39
  36.5 1.9 %collective-permute-start.16 = (bf16[128,2048]{1,0:T(8,128)(2,1)S(1)}, bf16[128,2048]{1,0:T(8,128)(2,1)S(1)}, u32[]{:S(2)}, u32[]{:S(2)}) collective-permute-start(bf16[128,2048]{1,0:T(8,128)(2,1)S(1)} %collective-permute-done.14.refs_0_), channel_id=1, source_target_pairs={{0,4},{1,5},{2,6},{3,7},{4,0},{5,1},{6,2},{7,3},{8,12},{9,13},{10,... | collective-permute-start | bytes 1572872 | tf_op jit(solution)/shard_map/ppermute | solution.py:39
  39.6 2.3 %collective-permute-start.17 = (bf16[128,2048]{1,0:T(8,128)(2,1)S(1)}, bf16[128,2048]{1,0:T(8,128)(2,1)S(1)}, u32[]{:S(2)}, u32[]{:S(2)}) collective-permute-start(bf16[128,2048]{1,0:T(8,128)(2,1)S(1)} %get-tuple-element.115), channel_id=1, source_target_pairs={{0,4},{1,5},{2,6},{3,7},{4,0},{5,1},{6,2},{7,3},{8,12},{9,13},{10,... | collective-permute-start | bytes 1572872 | tf_op jit(solution)/shard_map/ppermute | solution.py:39
  42.0 9.2 %collective-permute-start.19 = (bf16[128,2048]{1,0:T(8,128)(2,1)S(1)}, bf16[128,2048]{1,0:T(8,128)(2,1)S(1)}, u32[]{:S(2)}, u32[]{:S(2)}) collective-permute-start(bf16[128,2048]{1,0:T(8,128)(2,1)S(1)} %add_convert_fusion.1), channel_id=1, source_target_pairs={{0,16},{1,17},{2,18},{3,19},{4,12},{5,13},{6,14},{7,15},{8,24},{9,... | collective-permute-start | bytes 1572872 | tf_op jit(solution)/shard_map/ppermute | solution.py:39
  44.0 4.7 %collective-permute-start.18 = (bf16[128,2048]{1,0:T(8,128)(2,1)S(1)}, bf16[128,2048]{1,0:T(8,128)(2,1)S(1)}, u32[]{:S(2)}, u32[]{:S(2)}) collective-permute-start(bf16[128,2048]{1,0:T(8,128)(2,1)S(1)} %get-tuple-element.117), channel_id=1, source_target_pairs={{0,4},{1,5},{2,6},{3,7},{4,0},{5,1},{6,2},{7,3},{8,12},{9,13},{10,... | collective-permute-start | bytes 1572872 | tf_op jit(solution)/shard_map/ppermute | solution.py:39
  44.2 17.2 %collective-permute-start.23 = (bf16[32,2048]{1,0:T(8,128)(2,1)S(1)}, bf16[32,2048]{1,0:T(8,128)(2,1)S(1)}, u32[]{:S(2)}, u32[]{:S(2)}) collective-permute-start(bf16[32,2048]{1,0:T(8,128)(2,1)S(1)} %get-tuple-element.140), channel_id=1, source_target_pairs={{0,3},{1,2},{2,1},{3,0},{4,7},{5,6},{6,5},{7,4},{8,11},{9,10},{10,... | collective-permute-start | bytes 393224 | tf_op jit(solution)/shard_map/ppermute | solution.py:39
  46.8 15.7 %collective-permute-start.22 = (bf16[32,2048]{1,0:T(8,128)(2,1)S(1)}, bf16[32,2048]{1,0:T(8,128)(2,1)S(1)}, u32[]{:S(2)}, u32[]{:S(2)}) collective-permute-start(bf16[32,2048]{1,0:T(8,128)(2,1)S(1)} %get-tuple-element.141), channel_id=1, source_target_pairs={{0,2},{1,3},{2,0},{3,1},{4,6},{5,7},{6,4},{7,5},{8,10},{9,11},{10,... | collective-permute-start | bytes 393224 | tf_op jit(solution)/shard_map/ppermute | solution.py:39
  47.7 14.7 %collective-permute-start.21 = (bf16[32,2048]{1,0:T(8,128)(2,1)S(1)}, bf16[32,2048]{1,0:T(8,128)(2,1)S(1)}, u32[]{:S(2)}, u32[]{:S(2)}) collective-permute-start(bf16[32,2048]{1,0:T(8,128)(2,1)S(1)} %get-tuple-element.142), channel_id=1, source_target_pairs={{0,1},{1,0},{2,3},{3,2},{4,5},{5,4},{6,7},{7,6},{8,9},{9,8},{10,11... | collective-permute-start | bytes 393224 | tf_op jit(solution)/shard_map/ppermute | solution.py:39
  51.4 6.4 %collective-permute-start.20 = (bf16[64,2048]{1,0:T(8,128)(2,1)S(1)}, bf16[64,2048]{1,0:T(8,128)(2,1)S(1)}, u32[]{:S(2)}, u32[]{:S(2)}) collective-permute-start(bf16[64,2048]{1,0:T(8,128)(2,1)S(1)} %get-tuple-element.119), channel_id=1, source_target_pairs={{0,8},{1,9},{2,10},{3,11},{4,20},{5,21},{6,22},{7,23},{8,0},{9,1},... | collective-permute-start | bytes 786440 | tf_op jit(solution)/shard_map/ppermute | solution.py:39
  57.9 6.7 %collective-permute-start.27 = (bf16[16,2048]{1,0:T(8,128)(2,1)S(1)}, bf16[16,2048]{1,0:T(8,128)(2,1)S(1)}, u32[]{:S(2)}, u32[]{:S(2)}) collective-permute-start(bf16[16,2048]{1,0:T(8,128)(2,1)S(1)} %get-tuple-element.143), channel_id=1, source_target_pairs={{0,3},{1,2},{2,1},{3,0},{4,7},{5,6},{6,5},{7,4},{8,11},{9,10},{10,... | collective-permute-start | bytes 196616 | tf_op jit(solution)/shard_map/ppermute | solution.py:39
  60.3 5.9 %collective-permute-start.26 = (bf16[16,2048]{1,0:T(8,128)(2,1)S(1)}, bf16[16,2048]{1,0:T(8,128)(2,1)S(1)}, u32[]{:S(2)}, u32[]{:S(2)}) collective-permute-start(bf16[16,2048]{1,0:T(8,128)(2,1)S(1)} %get-tuple-element.144), channel_id=1, source_target_pairs={{0,2},{1,3},{2,0},{3,1},{4,6},{5,7},{6,4},{7,5},{8,10},{9,11},{10,... | collective-permute-start | bytes 196616 | tf_op jit(solution)/shard_map/ppermute | solution.py:39
  61.4 4.9 %collective-permute-start.25 = (bf16[16,2048]{1,0:T(8,128)(2,1)S(1)}, bf16[16,2048]{1,0:T(8,128)(2,1)S(1)}, u32[]{:S(2)}, u32[]{:S(2)}) collective-permute-start(bf16[16,2048]{1,0:T(8,128)(2,1)S(1)} %get-tuple-element.145), channel_id=1, source_target_pairs={{0,1},{1,0},{2,3},{3,2},{4,5},{5,4},{6,7},{7,6},{8,9},{9,8},{10,11... | collective-permute-start | bytes 196616 | tf_op jit(solution)/shard_map/ppermute | solution.py:39
  62.5 4.3 %collective-permute-start.24 = (bf16[16,2048]{1,0:T(8,128)(2,1)S(1)}, bf16[16,2048]{1,0:T(8,128)(2,1)S(1)}, u32[]{:S(2)}, u32[]{:S(2)}) collective-permute-start(bf16[16,2048]{1,0:T(8,128)(2,1)S(1)} %get-tuple-element.147), channel_id=1, source_target_pairs={{0,8},{1,9},{2,10},{3,11},{4,20},{5,21},{6,22},{7,23},{8,0},{9,1},... | collective-permute-start | bytes 196616 | tf_op jit(solution)/shard_map/ppermute | solution.py:39

commit v7 on v6

--- a/solution.py
+++ b/solution.py
@@ -171,9 +171,9 @@
         return nt(gate, self.refs[0][0]) + nt(up, self.refs[1][0])
 
 
-def join_kernel(blocks, flip, *refs):
+def join_kernel(blocks, order, *refs):
     at, out = 0, refs[-1]
-    arrays = (refs[0], *refs[-2:0:-1]) if flip else refs[:-1]
+    arrays = [refs[i] for i in order] if order else refs[:-1]
     for i in range(blocks):
         for ref in arrays:
             size = ref.shape[0] // blocks
@@ -181,10 +181,10 @@
             at += size
 
 
-def join(*arrays, blocks=1, flip=False, length=0.0):
+def join(*arrays, blocks=1, order=(), length=0.0):
     rows = sum(a.shape[0] for a in arrays)
     return pl.pallas_call(
-        functools.partial(join_kernel, blocks, flip),
+        functools.partial(join_kernel, blocks, order),
         in_specs=[WHOLE] * len(arrays),
         out_specs=WHOLE,
         out_shape=pltpu.VMEM((rows, arrays[0].shape[1]), BF16),
@@ -466,9 +466,9 @@
         weights = stage(*(after(w, own) for w in weights))
     for p in plane[:-1]:
         cot = join(cot, send(cot, p))
-    row_lane = join(after(own, weights[0], cot), *[send(own, p) for p in line[::-1]], flip=True)
+    row_lane = join(after(own, weights[0], cot), *[send(own, p) for p in line[::-1]], order=(0, *range(len(line), 0, -1)))
     cot = after(cot, row_lane)
-    cot_lane = join(cot, *[send(cot, p) for p in line], length=10.0)
+    pieces = [send(cot, p) for p in line]
     for p in plane[:-1]:
         row_lane = join(row_lane, send(row_lane, p), blocks=n_ex)
     n = row_lane.shape[0]
@@ -478,6 +478,11 @@
     def forward(kernel, *args):
         return functools.partial(kernel, experts, width), n, [expert], *args
 
+    *f_early_own, kept = over_rows(
+        *forward(forward_full_kernel, [(1, row_lane)], weights, each(1, units) + [wide_kept], 10.0)
+    )
+    order = (0, *range(2, len(line) + 1), 1)
+    cot_lane = join(after(cot, kept), *pieces[-1:], *pieces[:-1], order=order, length=10.0)
     cot_late = send(cot_lane, plane[-1])
     cot_other = send(cot_lane, core)
 
@@ -491,14 +496,15 @@
     row_late_other = send(row_late, core)
     f_own = over_rows(*forward(forward_hidden_kernel, [(1, row_late)], weights, each(1, units), 10.0))
     full = weights, each(1, units) + [wide], 10.0
-    *f_early_own, kept = over_rows(
-        *forward(forward_full_kernel, [(1, after(row_lane, f_own[0]))], weights, each(1, units) + [wide_kept], 10.0)
-    )
-    row_late_other_in = after(row_late_other, kept)
+    *f_early_other, given = over_rows(*forward(forward_full_kernel, [(1, after(row_other, f_own[0]))], *full))
+    row_late_other_in = after(row_late_other, given)
     *f_other, o_given = over_rows(*forward(forward_full_kernel, [(1, row_late_other_in)], *full))
     o_other = send(o_given, core)
-    *f_early_other, given = over_rows(*forward(forward_full_kernel, [(1, after(row_other, f_other[0]))], *full))
-    taken = [(1, f_own[0]), (1, after(f_own[3], given))]
+    taken = [(1, after(cot_lane, f_other[0]))] + with_units(f_early_own)
+    *b_early, g_kept = over_rows(
+        backward_full_kernel, n, [], taken, weights, each(1, cots) + [wide_kept], 10.0
+    )
+    taken = [(1, f_own[0]), (1, after(f_own[3], g_kept))]
     (o_own,) = over_rows(forward_out_kernel, n, [], taken, weights, [wide_kept])
     o_late = halve(o_own, o_other)
     o_early_other = send(given, core)
@@ -509,17 +515,13 @@
     taken = [(1, cot_late)] + with_units(f_own)
     b_own = over_rows(backward_hidden_kernel, n, [], taken, weights, each(1, cots), 10.0)
     full = weights, each(1, cots) + [wide], 10.0
-    taken = [(1, after(cot_lane, b_own[0]))] + with_units(f_early_own)
-    *b_early, g_kept = over_rows(
-        backward_full_kernel, n, [], taken, weights, each(1, cots) + [wide_kept], 10.0
-    )
-    taken = [(1, after(cot_late_other, g_kept))] + with_units(f_other)
+    taken = [(1, after(cot_other, b_own[0]))] + with_units(f_early_other)
+    *b_early_other, g_early = over_rows(backward_full_kernel, n, [], taken, *full)
+    taken = [(1, after(cot_late_other, g_early))] + with_units(f_other)
     *b_other, g_given = over_rows(backward_full_kernel, n, [], taken, *full)
     g_other = send(g_given, core)
-    taken = [(1, after(cot_other, b_other[0]))] + with_units(f_early_other)
-    *b_early_other, g_early = over_rows(backward_full_kernel, n, [], taken, *full)
-    taken = [(1, b_own[0]), (1, after(b_own[1], g_early))]
-    (g_own,) = over_rows(backward_rows_kernel, n, [], taken, weights, [wide_kept])
+    taken = [(1, b_own[0]), (1, after(b_own[1], b_other[0]))]
+    (g_own,) = over_rows(backward_rows_kernel, n, [], taken, weights, [wide_kept], 10.0)
     g_late = halve(g_own, g_other)
     g_early_other = send(after(g_early, g_late), core)
     g_back = send(g_late, plane[-1])
@@ -544,7 +546,7 @@
     g_lane = add(parts[0], after(parts[1], gate_grad, down_grad)).astype(BF16)
     g_terms = line_sends(g_lane)
     o_terms = line_sends(add(kept, o_early_other, o_back).astype(BF16))
-    parts = (join(after(o_terms[0], g_lane), length=20.0), *o_terms[:0:-1])
+    parts = (join(after(o_terms[0], g_lane), length=20.0), *o_terms[-1:], *o_terms[1:-1])
     for p in reversed(plane[:-1]):
         lane = add(*parts).astype(BF16)
         half = lane.shape[0] // 2

time: 67.9 us -> 67.2 us (0.990)
  starting transfers between devices: 31.4 us -> 30.4 us
    ppermute x28, starting transfers between devices: 31.4 us -> 30.4 us  [send(): return lax.ppermute(x, AXES, pairs)]
  transfers between devices with their start and end apart: 28 -> 28, of which waited for: 13 -> 15; matrix products, arithmetic and copies ran while one was open for 1% -> 1% of each run, Pallas kernels for 25% -> 25%
where the time goes in v7:
time: 67.2 us; the launch traced here: 67 us
  starting transfers between devices  30.4 us (45%)
  Pallas kernels  18.7 us (28%)
  waiting for transfers between devices  16.3 us (24%)
  between operations  1.06 us (2%)
    ppermute x28, starting transfers between devices, send(): return lax.ppermute(x, AXES, pairs)  30.4 us
    ppermute x28, waiting for transfers between devices, send(): return lax.ppermute(x, AXES, pairs)  16.3 us
    pallas_call x10, Pallas kernels, over_rows(): pl.pallas_call(run, out_shape=shaped(*[((f * n, w), t) for f, w, t in giv...  9.17 us
    pallas_call x2, Pallas kernels, gradients_by_chunks(): pl.pallas_call(functools.partial(chunk_kernel, over_left, chunks, [len(g)...  4.74 us
    pallas_call x1, Pallas kernels, stage(): pl.pallas_call(stage_kernel, in_specs=[ANY] * 3, out_specs=[WHOLE] * 2, o...  2.86 us
  transfers between devices with their start and end apart: 28, of which 15 were waited for; matrix products, arithmetic and copies ran while one was open for 1% of the time, Pallas kernels for 25%

profile of v7, /device:TPU:0, one launch (start us, length us, event | category | flops | bytes accessed | tf_op | source)
XLA Modules:
  0.0 67.0 jit_solution(4089980906844663825)
XLA Ops:
  0.6 0.9 %shard_map.110 = (bf16[16,2176]{1,0:T(8,128)(2,1)S(1)}, bf16[16,2048]{1,0:T(8,128)(2,1)S(1)}) custom-call(bf16[16,2048]{1,0:T(8,128)(2,1)} %tokens, bf16[16,2048]{1,0:T(8,128)(2,1)} %cotangent.1, s32[8,16]{1,0:T(8,128)} %bitcast.3, f32[8,16]{1,0:T(8,128)} %bitcast.4), custom_call_target="tpu_custom_call" | custom-call | tf_op jit(solution)/shard_map/pallas_call | solution.py:111
  1.6 5.1 %collective-permute-start.3 = (bf16[16,2176]{1,0:T(8,128)(2,1)S(1)}, bf16[16,2176]{1,0:T(8,128)(2,1)S(1)}, u32[]{:S(2)}, u32[]{:S(2)}) collective-permute-start(bf16[16,2176]{1,0:T(8,128)(2,1)S(1)} %get-tuple-element.80.refs_0_), channel_id=1, source_target_pairs={{0,3},{1,2},{2,1},{3,0},{4,7},{5,6},{6,5},{7,4},{8,11},{9,10},{10,... | collective-permute-start | bytes 208904 | tf_op jit(solution)/shard_map/ppermute | solution.py:39
  7.3 1.6 %collective-permute-start = (bf16[16,2048]{1,0:T(8,128)(2,1)S(1)}, bf16[16,2048]{1,0:T(8,128)(2,1)S(1)}, u32[]{:S(2)}, u32[]{:S(2)}) collective-permute-start(bf16[16,2048]{1,0:T(8,128)(2,1)S(1)} %get-tuple-element.79.refs_0_), channel_id=1, source_target_pairs={{0,8},{1,9},{2,10},{3,11},{4,20},{5,21},{6,22},{7,23},{8,0},{9,1},... | collective-permute-start | bytes 196616 | tf_op jit(solution)/shard_map/ppermute | solution.py:39
  9.0 2.9 %shard_map.111 = (bf16[3,2048,384]{2,1,0:T(8,128)(2,1)S(1)}, bf16[3,384,2048]{2,1,0:T(8,128)(2,1)S(1)}) custom-call(bf16[1,2048,384]{2,1,0:T(8,128)(2,1)} %gate, bf16[1,2048,384]{2,1,0:T(8,128)(2,1)} %up, bf16[1,384,2048]{2,1,0:T(8,128)(2,1)} %down), custom_call_target="tpu_custom_call" | custom-call | tf_op jit(solution)/shard_map/pallas_call | solution.py:142
  12.6 1.6 %collective-permute-start.4 = (bf16[64,2176]{1,0:T(8,128)(2,1)S(1)}, bf16[64,2176]{1,0:T(8,128)(2,1)S(1)}, u32[]{:S(2)}, u32[]{:S(2)}) collective-permute-start(bf16[64,2176]{1,0:T(8,128)(2,1)S(1)} %shard_map.113.refs_0_), channel_id=1, source_target_pairs={{0,8},{1,9},{2,10},{3,11},{4,20},{5,21},{6,22},{7,23},{8,0},{9,1},... | collective-permute-start | bytes 835592 | tf_op jit(solution)/shard_map/ppermute | solution.py:39
  14.2 1.3 %collective-permute-start.9 = (bf16[32,2048]{1,0:T(8,128)(2,1)S(1)}, bf16[32,2048]{1,0:T(8,128)(2,1)S(1)}, u32[]{:S(2)}, u32[]{:S(2)}) collective-permute-start(bf16[32,2048]{1,0:T(8,128)(2,1)S(1)} %shard_map.112.refs_0_), channel_id=1, source_target_pairs={{0,2},{1,3},{2,0},{3,1},{4,6},{5,7},{6,4},{7,5},{8,10},{9,11},{10,... | collective-permute-start | bytes 393224 | tf_op jit(solution)/shard_map/ppermute | solution.py:39
  15.5 2.1 %collective-permute-start.8 = (bf16[32,2048]{1,0:T(8,128)(2,1)S(1)}, bf16[32,2048]{1,0:T(8,128)(2,1)S(1)}, u32[]{:S(2)}, u32[]{:S(2)}) collective-permute-start(bf16[32,2048]{1,0:T(8,128)(2,1)S(1)} %shard_map.112.refs_0_), channel_id=1, source_target_pairs={{0,3},{1,2},{2,1},{3,0},{4,7},{5,6},{6,5},{7,4},{8,11},{9,10},{10,... | collective-permute-start | bytes 393224 | tf_op jit(solution)/shard_map/ppermute | solution.py:39
  17.7 1.6 %collective-permute-done.4.refs_1_ = bf16[64,2176]{1,0:T(8,128)(2,1)S(1)} collective-permute-done((bf16[64,2176]{1,0:T(8,128)(2,1)S(1)}, bf16[64,2176]{1,0:T(8,128)(2,1)S(1)}, u32[]{:S(2)}, u32[]{:S(2)}) %collective-permute-start.4) | collective-permute-done | bytes 278560 | tf_op jit(solution)/shard_map/ppermute | solution.py:39
  19.3 1.6 %collective-permute-start.6 = (bf16[128,2176]{1,0:T(8,128)(2,1)S(1)}, bf16[128,2176]{1,0:T(8,128)(2,1)S(1)}, u32[]{:S(2)}, u32[]{:S(2)}) collective-permute-start(bf16[128,2176]{1,0:T(8,128)(2,1)S(1)} %shard_map.114.refs_1_.refs_0_), channel_id=1, source_target_pairs={{0,16},{1,17},{2,18},{3,19},{4,12},{5,13},{6,14},{7,15},{8,24},{9,... | collective-permute-start | bytes 1671176 | tf_op jit(solution)/shard_map/ppermute | solution.py:39
  20.9 1.1 %shard_map.115 = (bf16[128,384]{1,0:T(8,128)(2,1)S(1)}, f32[128,384]{1,0:T(8,128)S(1)}, f32[128,384]{1,0:T(8,128)S(1)}, f32[128,128]{1,0:T(8,128)S(1)}, f32[128,2048]{1,0:T(8,128)S(1)}) custom-call(s32[1,1]{1,0:T(1,128)} %bitcast.refs_0_, bf16[128,2176]{1,0:T(8,128)(2,1)S(1)} %shard_map.114.refs_1_.refs_0_, ...), custom_call_target="tpu_custom_call" | custom-call | flops 11500000256 | tf_op jit(solution)/shard_map/pallas_call | solution.py:280
  22.0 3.5 %collective-permute-done.9.refs_3_ = bf16[32,2048]{1,0:T(8,128)(2,1)S(1)} collective-permute-done((bf16[32,2048]{1,0:T(8,128)(2,1)S(1)}, bf16[32,2048]{1,0:T(8,128)(2,1)S(1)}, u32[]{:S(2)}, u32[]{:S(2)}) %collective-permute-start.9) | collective-permute-done | bytes 131104 | tf_op jit(solution)/shard_map/ppermute | solution.py:39
  25.4 1.3 %collective-permute-done.7.refs_1_ = bf16[32,2048]{1,0:T(8,128)(2,1)S(1)} collective-permute-done((bf16[32,2048]{1,0:T(8,128)(2,1)S(1)}, bf16[32,2048]{1,0:T(8,128)(2,1)S(1)}, u32[]{:S(2)}, u32[]{:S(2)}) %collective-permute-start.7) | collective-permute-done | bytes 131104 | tf_op jit(solution)/shard_map/ppermute | solution.py:39
  27.4 1.5 %collective-permute-done.6.refs_1_.refs_2_ = bf16[128,2176]{1,0:T(8,128)(2,1)S(1)} collective-permute-done((bf16[128,2176]{1,0:T(8,128)(2,1)S(1)}, bf16[128,2176]{1,0:T(8,128)(2,1)S(1)}, u32[]{:S(2)}, u32[]{:S(2)}) %collective-permute-start.6) | collective-permute-done | bytes 557088 | tf_op jit(solution)/shard_map/ppermute | solution.py:39
  29.6 1.1 %shard_map.118 = (bf16[128,384]{1,0:T(8,128)(2,1)S(1)}, f32[128,384]{1,0:T(8,128)S(1)}, f32[128,384]{1,0:T(8,128)S(1)}, f32[128,128]{1,0:T(8,128)S(1)}, bf16[128,2048]{1,0:T(8,128)(2,1)S(1)}) custom-call(s32[1,1]{1,0:T(1,128)} %bitcast.refs_0_, bf16[128,2176]{1,0:T(8,128)(2,1)S(1)} %collective-permute-done.5.refs_1_, ...), custom_call_target="tpu_custom_call" | custom-call | flops 11500000256 | tf_op jit(solution)/shard_map/pallas_call | solution.py:280
  31.3 1.1 %shard_map.119 = (bf16[128,384]{1,0:T(8,128)(2,1)S(1)}, f32[128,384]{1,0:T(8,128)S(1)}, f32[128,384]{1,0:T(8,128)S(1)}, f32[128,128]{1,0:T(8,128)S(1)}, bf16[128,2048]{1,0:T(8,128)(2,1)S(1)}) custom-call(s32[1,1]{1,0:T(1,128)} %bitcast.refs_0_, bf16[128,2176]{1,0:T(8,128)(2,1)S(1)} %collective-permute-done.11.refs_1_.refs_3_, ...), custom_call_target="tpu_custom_call" | custom-call | flops 11500000256 | tf_op jit(solution)/shard_map/pallas_call | solution.py:280
  32.5 1.2 %shard_map.120 = (bf16[128,384]{1,0:T(8,128)(2,1)S(1)}, bf16[128,384]{1,0:T(8,128)(2,1)S(1)}, bf16[128,2048]{1,0:T(8,128)(2,1)S(1)}, f32[128,2048]{1,0:T(8,128)S(1)}) custom-call(bf16[128,2048]{1,0:T(8,128)(2,1)S(1)} %shard_map.116.refs_0_, f32[128,128]{1,0:T(8,128)S(1)} %get-tuple-element.93.refs_1_, f32[128,384]{1,0:T(8,128)S(1)} %get-tuple-element.94.refs_2_, ...), custom_call_target="tpu_custom_call" | custom-call | flops 11500000256 | tf_op jit(solution)/shard_map/pallas_call | solution.py:280
  34.5 1.6 %collective-permute-start.13 = (bf16[128,2048]{1,0:T(8,128)(2,1)S(1)}, bf16[128,2048]{1,0:T(8,128)(2,1)S(1)}, u32[]{:S(2)}, u32[]{:S(2)}) collective-permute-start(bf16[128,2048]{1,0:T(8,128)(2,1)S(1)} %add_convert_fusion.2), channel_id=1, source_target_pairs={{0,16},{1,17},{2,18},{3,19},{4,12},{5,13},{6,14},{7,15},{8,24},{9,... | collective-permute-start | bytes 1572872 | tf_op jit(solution)/shard_map/ppermute | solution.py:39
  36.6 1.2 %shard_map.123 = (bf16[128,384]{1,0:T(8,128)(2,1)S(1)}, bf16[128,384]{1,0:T(8,128)(2,1)S(1)}, bf16[128,2048]{1,0:T(8,128)(2,1)S(1)}, bf16[128,2048]{1,0:T(8,128)(2,1)S(1)}) custom-call(bf16[128,2048]{1,0:T(8,128)(2,1)S(1)} %collective-permute-done.16.refs_0_, f32[128,128]{1,0:T(8,128)S(1)} %get-tuple-element.105.refs_1_, ...), custom_call_target="tpu_custom_call" | custom-call | flops 11500000256 | tf_op jit(solution)/shard_map/pallas_call | solution.py:280
  38.0 1.2 %shard_map.124 = (bf16[128,384]{1,0:T(8,128)(2,1)S(1)}, bf16[128,384]{1,0:T(8,128)(2,1)S(1)}, bf16[128,2048]{1,0:T(8,128)(2,1)S(1)}, bf16[128,2048]{1,0:T(8,128)(2,1)S(1)}) custom-call(bf16[128,2048]{1,0:T(8,128)(2,1)S(1)} %collective-permute-done.15.refs_0_, f32[128,128]{1,0:T(8,128)S(1)} %get-tuple-element.110.refs_1_, ...), custom_call_target="tpu_custom_call" | custom-call | flops 11500000256 | tf_op jit(solution)/shard_map/pallas_call | solution.py:280
  40.3 0.9 %collective-permute-done.17 = bf16[128,2048]{1,0:T(8,128)(2,1)S(1)} collective-permute-done((bf16[128,2048]{1,0:T(8,128)(2,1)S(1)}, bf16[128,2048]{1,0:T(8,128)(2,1)S(1)}, u32[]{:S(2)}, u32[]{:S(2)}) %collective-permute-start.17) | collective-permute-done | bytes 524320 | tf_op jit(solution)/shard_map/ppermute | solution.py:39
  41.3 1.3 %collective-permute-start.19 = (bf16[128,2048]{1,0:T(8,128)(2,1)S(1)}, bf16[128,2048]{1,0:T(8,128)(2,1)S(1)}, u32[]{:S(2)}, u32[]{:S(2)}) collective-permute-start(bf16[128,2048]{1,0:T(8,128)(2,1)S(1)} %add_convert_fusion.1), channel_id=1, source_target_pairs={{0,16},{1,17},{2,18},{3,19},{4,12},{5,13},{6,14},{7,15},{8,24},{9,... | collective-permute-start | bytes 1572872 | tf_op jit(solution)/shard_map/ppermute | solution.py:39
  42.9 0.9 %collective-permute-done.13 = bf16[128,2048]{1,0:T(8,128)(2,1)S(1)} collective-permute-done((bf16[128,2048]{1,0:T(8,128)(2,1)S(1)}, bf16[128,2048]{1,0:T(8,128)(2,1)S(1)}, u32[]{:S(2)}, u32[]{:S(2)}) %collective-permute-start.13) | collective-permute-done | bytes 524320 | tf_op jit(solution)/shard_map/ppermute | solution.py:39
  44.0 1.5 %collective-permute-start.23 = (bf16[32,2048]{1,0:T(8,128)(2,1)S(1)}, bf16[32,2048]{1,0:T(8,128)(2,1)S(1)}, u32[]{:S(2)}, u32[]{:S(2)}) collective-permute-start(bf16[32,2048]{1,0:T(8,128)(2,1)S(1)} %get-tuple-element.140), channel_id=1, source_target_pairs={{0,2},{1,3},{2,0},{3,1},{4,6},{5,7},{6,4},{7,5},{8,10},{9,11},{10,... | collective-permute-start | bytes 393224 | tf_op jit(solution)/shard_map/ppermute | solution.py:39
  45.5 2.3 %collective-permute-start.22 = (bf16[32,2048]{1,0:T(8,128)(2,1)S(1)}, bf16[32,2048]{1,0:T(8,128)(2,1)S(1)}, u32[]{:S(2)}, u32[]{:S(2)}) collective-permute-start(bf16[32,2048]{1,0:T(8,128)(2,1)S(1)} %get-tuple-element.141), channel_id=1, source_target_pairs={{0,3},{1,2},{2,1},{3,0},{4,7},{5,6},{6,5},{7,4},{8,11},{9,10},{10,... | collective-permute-start | bytes 393224 | tf_op jit(solution)/shard_map/ppermute | solution.py:39
  47.9 2.7 %collective-permute-done.19.refs_2_ = bf16[128,2048]{1,0:T(8,128)(2,1)S(1)} collective-permute-done((bf16[128,2048]{1,0:T(8,128)(2,1)S(1)}, bf16[128,2048]{1,0:T(8,128)(2,1)S(1)}, u32[]{:S(2)}, u32[]{:S(2)}) %collective-permute-start.19) | collective-permute-done | bytes 524320 | tf_op jit(solution)/shard_map/ppermute | solution.py:39
  50.7 1.6 %collective-permute-start.20 = (bf16[64,2048]{1,0:T(8,128)(2,1)S(1)}, bf16[64,2048]{1,0:T(8,128)(2,1)S(1)}, u32[]{:S(2)}, u32[]{:S(2)}) collective-permute-start(bf16[64,2048]{1,0:T(8,128)(2,1)S(1)} %get-tuple-element.119), channel_id=1, source_target_pairs={{0,8},{1,9},{2,10},{3,11},{4,20},{5,21},{6,22},{7,23},{8,0},{9,1},... | collective-permute-start | bytes 786440 | tf_op jit(solution)/shard_map/ppermute | solution.py:39
  52.2 2.0 %shard_map.128 = bf16[1,384,2048]{2,1,0:T(8,128)(2,1)} custom-call(bf16[128,384]{1,0:T(8,128)(2,1)S(1)} %get-tuple-element.128.refs_0_, bf16[128,384]{1,0:T(8,128)(2,1)S(1)} %get-tuple-element.129.refs_1_, bf16[128,384]{1,0:T(8,128)(2,1)S(1)} %get-tuple-element.86.refs_0_.refs_2_, bf16[128,384]{1,0:T(8,128)(2,1)S(1)} %get-tuple-element.91.refs_3_, ...), custom_call_target="tpu_custom_call" | custom-call | flops 11500000256 | tf_op jit(solution)/shard_map/pallas_call | solution.py:380
  54.2 2.8 %shard_map.127 = (bf16[1,2048,384]{2,1,0:T(8,128)(2,1)}, bf16[1,2048,384]{2,1,0:T(8,128)(2,1)}) custom-call(bf16[128,2176]{1,0:T(8,128)(2,1)S(1)} %shard_map.114.refs_1_.refs_0_, bf16[128,2176]{1,0:T(8,128)(2,1)S(1)} %collective-permute-done.5.refs_1_, bf16[128,2176]{1,0:T(8,128)(2,1)S(1)} %collective-permute-done.6.refs_1_.refs_2_, ...), custom_call_target="tpu_custom_call" | custom-call | flops 11500000256 | tf_op jit(solution)/shard_map/pallas_call | solution.py:380
  57.2 3.0 %collective-permute-start.27 = (bf16[16,2048]{1,0:T(8,128)(2,1)S(1)}, bf16[16,2048]{1,0:T(8,128)(2,1)S(1)}, u32[]{:S(2)}, u32[]{:S(2)}) collective-permute-start(bf16[16,2048]{1,0:T(8,128)(2,1)S(1)} %get-tuple-element.143), channel_id=1, source_target_pairs={{0,3},{1,2},{2,1},{3,0},{4,7},{5,6},{6,5},{7,4},{8,11},{9,10},{10,... | collective-permute-start | bytes 196616 | tf_op jit(solution)/shard_map/ppermute | solution.py:39
  60.8 1.0 %collective-permute-start.25 = (bf16[16,2048]{1,0:T(8,128)(2,1)S(1)}, bf16[16,2048]{1,0:T(8,128)(2,1)S(1)}, u32[]{:S(2)}, u32[]{:S(2)}) collective-permute-start(bf16[16,2048]{1,0:T(8,128)(2,1)S(1)} %get-tuple-element.145), channel_id=1, source_target_pairs={{0,1},{1,0},{2,3},{3,2},{4,5},{5,4},{6,7},{7,6},{8,9},{9,8},{10,11... | collective-permute-start | bytes 196616 | tf_op jit(solution)/shard_map/ppermute | solution.py:39
  61.9 1.6 %collective-permute-start.24 = (bf16[16,2048]{1,0:T(8,128)(2,1)S(1)}, bf16[16,2048]{1,0:T(8,128)(2,1)S(1)}, u32[]{:S(2)}, u32[]{:S(2)}) collective-permute-start(bf16[16,2048]{1,0:T(8,128)(2,1)S(1)} %get-tuple-element.147), channel_id=1, source_target_pairs={{0,8},{1,9},{2,10},{3,11},{4,20},{5,21},{6,22},{7,23},{8,0},{9,1},... | collective-permute-start | bytes 196616 | tf_op jit(solution)/shard_map/ppermute | solution.py:39
  63.5 2.2 %collective-permute-done.26.refs_2_ = bf16[16,2048]{1,0:T(8,128)(2,1)S(1)} collective-permute-done((bf16[16,2048]{1,0:T(8,128)(2,1)S(1)}, bf16[16,2048]{1,0:T(8,128)(2,1)S(1)}, u32[]{:S(2)}, u32[]{:S(2)}) %collective-permute-start.26) | collective-permute-done | bytes 65568 | tf_op jit(solution)/shard_map/ppermute | solution.py:39
  (54 shorter events, 9.1 us)
Async XLA Ops:
  1.6 10.3 %collective-permute-start.3 = (bf16[16,2176]{1,0:T(8,128)(2,1)S(1)}, bf16[16,2176]{1,0:T(8,128)(2,1)S(1)}, u32[]{:S(2)}, u32[]{:S(2)}) collective-permute-start(bf16[16,2176]{1,0:T(8,128)(2,1)S(1)} %get-tuple-element.80.refs_0_), channel_id=1, source_target_pairs={{0,3},{1,2},{2,1},{3,0},{4,7},{5,6},{6,5},{7,4},{8,11},{9,10},{10,... | collective-permute-start | bytes 208904 | tf_op jit(solution)/shard_map/ppermute | solution.py:39
  6.7 5.9 %collective-permute-start.2 = (bf16[16,2176]{1,0:T(8,128)(2,1)S(1)}, bf16[16,2176]{1,0:T(8,128)(2,1)S(1)}, u32[]{:S(2)}, u32[]{:S(2)}) collective-permute-start(bf16[16,2176]{1,0:T(8,128)(2,1)S(1)} %get-tuple-element.80.refs_0_), channel_id=1, source_target_pairs={{0,2},{1,3},{2,0},{3,1},{4,6},{5,7},{6,4},{7,5},{8,10},{9,11},{10,... | collective-permute-start | bytes 208904 | tf_op jit(solution)/shard_map/ppermute | solution.py:39
  6.7 5.9 %collective-permute-start.1 = (bf16[16,2176]{1,0:T(8,128)(2,1)S(1)}, bf16[16,2176]{1,0:T(8,128)(2,1)S(1)}, u32[]{:S(2)}, u32[]{:S(2)}) collective-permute-start(bf16[16,2176]{1,0:T(8,128)(2,1)S(1)} %get-tuple-element.80.refs_0_), channel_id=1, source_target_pairs={{0,1},{1,0},{2,3},{3,2},{4,5},{5,4},{6,7},{7,6},{8,9},{9,8},{10,11... | collective-permute-start | bytes 208904 | tf_op jit(solution)/shard_map/ppermute | solution.py:39
  7.3 4.5 %collective-permute-start = (bf16[16,2048]{1,0:T(8,128)(2,1)S(1)}, bf16[16,2048]{1,0:T(8,128)(2,1)S(1)}, u32[]{:S(2)}, u32[]{:S(2)}) collective-permute-start(bf16[16,2048]{1,0:T(8,128)(2,1)S(1)} %get-tuple-element.79.refs_0_), channel_id=1, source_target_pairs={{0,8},{1,9},{2,10},{3,11},{4,20},{5,21},{6,22},{7,23},{8,0},{9,1},... | collective-permute-start | bytes 196616 | tf_op jit(solution)/shard_map/ppermute | solution.py:39
  12.6 6.6 %collective-permute-start.4 = (bf16[64,2176]{1,0:T(8,128)(2,1)S(1)}, bf16[64,2176]{1,0:T(8,128)(2,1)S(1)}, u32[]{:S(2)}, u32[]{:S(2)}) collective-permute-start(bf16[64,2176]{1,0:T(8,128)(2,1)S(1)} %shard_map.113.refs_0_), channel_id=1, source_target_pairs={{0,8},{1,9},{2,10},{3,11},{4,20},{5,21},{6,22},{7,23},{8,0},{9,1},... | collective-permute-start | bytes 835592 | tf_op jit(solution)/shard_map/ppermute | solution.py:39
  14.2 11.2 %collective-permute-start.9 = (bf16[32,2048]{1,0:T(8,128)(2,1)S(1)}, bf16[32,2048]{1,0:T(8,128)(2,1)S(1)}, u32[]{:S(2)}, u32[]{:S(2)}) collective-permute-start(bf16[32,2048]{1,0:T(8,128)(2,1)S(1)} %shard_map.112.refs_0_), channel_id=1, source_target_pairs={{0,2},{1,3},{2,0},{3,1},{4,6},{5,7},{6,4},{7,5},{8,10},{9,11},{10,... | collective-permute-start | bytes 393224 | tf_op jit(solution)/shard_map/ppermute | solution.py:39
  15.5 9.9 %collective-permute-start.8 = (bf16[32,2048]{1,0:T(8,128)(2,1)S(1)}, bf16[32,2048]{1,0:T(8,128)(2,1)S(1)}, u32[]{:S(2)}, u32[]{:S(2)}) collective-permute-start(bf16[32,2048]{1,0:T(8,128)(2,1)S(1)} %shard_map.112.refs_0_), channel_id=1, source_target_pairs={{0,3},{1,2},{2,1},{3,0},{4,7},{5,6},{6,5},{7,4},{8,11},{9,10},{10,... | collective-permute-start | bytes 393224 | tf_op jit(solution)/shard_map/ppermute | solution.py:39
  17.6 9.1 %collective-permute-start.7 = (bf16[32,2048]{1,0:T(8,128)(2,1)S(1)}, bf16[32,2048]{1,0:T(8,128)(2,1)S(1)}, u32[]{:S(2)}, u32[]{:S(2)}) collective-permute-start(bf16[32,2048]{1,0:T(8,128)(2,1)S(1)} %shard_map.112.refs_0_), channel_id=1, source_target_pairs={{0,1},{1,0},{2,3},{3,2},{4,5},{5,4},{6,7},{7,6},{8,9},{9,8},{10,11... | collective-permute-start | bytes 393224 | tf_op jit(solution)/shard_map/ppermute | solution.py:39
  19.3 9.6 %collective-permute-start.6 = (bf16[128,2176]{1,0:T(8,128)(2,1)S(1)}, bf16[128,2176]{1,0:T(8,128)(2,1)S(1)}, u32[]{:S(2)}, u32[]{:S(2)}) collective-permute-start(bf16[128,2176]{1,0:T(8,128)(2,1)S(1)} %shard_map.114.refs_1_.refs_0_), channel_id=1, source_target_pairs={{0,16},{1,17},{2,18},{3,19},{4,12},{5,13},{6,14},{7,15},{8,24},{9,... | collective-permute-start | bytes 1671176 | tf_op jit(solution)/shard_map/ppermute | solution.py:39
  20.9 8.7 %collective-permute-start.5 = (bf16[128,2176]{1,0:T(8,128)(2,1)S(1)}, bf16[128,2176]{1,0:T(8,128)(2,1)S(1)}, u32[]{:S(2)}, u32[]{:S(2)}) collective-permute-start(bf16[128,2176]{1,0:T(8,128)(2,1)S(1)} %shard_map.114.refs_1_.refs_0_), channel_id=1, source_target_pairs={{0,4},{1,5},{2,6},{3,7},{4,0},{5,1},{6,2},{7,3},{8,12},{9,13},{10,... | collective-permute-start | bytes 1671176 | tf_op jit(solution)/shard_map/ppermute | solution.py:39
  26.7 9.9 %collective-permute-start.16 = (bf16[128,2048]{1,0:T(8,128)(2,1)S(1)}, bf16[128,2048]{1,0:T(8,128)(2,1)S(1)}, u32[]{:S(2)}, u32[]{:S(2)}) collective-permute-start(bf16[128,2048]{1,0:T(8,128)(2,1)S(1)} %shard_map.116.refs_0_), channel_id=1, source_target_pairs={{0,4},{1,5},{2,6},{3,7},{4,0},{5,1},{6,2},{7,3},{8,12},{9,13},{10,... | collective-permute-start | bytes 1572872 | tf_op jit(solution)/shard_map/ppermute | solution.py:39
  26.8 9.3 %collective-permute-start.14 = (bf16[128,2048]{1,0:T(8,128)(2,1)S(1)}, bf16[128,2048]{1,0:T(8,128)(2,1)S(1)}, u32[]{:S(2)}, u32[]{:S(2)}) collective-permute-start(bf16[128,2048]{1,0:T(8,128)(2,1)S(1)} %shard_map.116.refs_0_), channel_id=1, source_target_pairs={{0,16},{1,17},{2,18},{3,19},{4,12},{5,13},{6,14},{7,15},{8,24},{9,... | collective-permute-start | bytes 1572872 | tf_op jit(solution)/shard_map/ppermute | solution.py:39
  28.9 2.4 %collective-permute-start.11 = (bf16[128,2176]{1,0:T(8,128)(2,1)S(1)}, bf16[128,2176]{1,0:T(8,128)(2,1)S(1)}, u32[]{:S(2)}, u32[]{:S(2)}) collective-permute-start(bf16[128,2176]{1,0:T(8,128)(2,1)S(1)} %collective-permute-done.6.refs_1_.refs_2_), channel_id=1, source_target_pairs={{0,4},{1,5},{2,6},{3,7},{4,0},{5,1},{6,2},{7,3},{8,12},{9,13},{10,... | collective-permute-start | bytes 1671176 | tf_op jit(solution)/shard_map/ppermute | solution.py:39
  30.7 13.0 %collective-permute-start.10 = (bf16[128,2048]{1,0:T(8,128)(2,1)S(1)}, bf16[128,2048]{1,0:T(8,128)(2,1)S(1)}, u32[]{:S(2)}, u32[]{:S(2)}) collective-permute-start(bf16[128,2048]{1,0:T(8,128)(2,1)S(1)} %get-tuple-element.88), channel_id=1, source_target_pairs={{0,4},{1,5},{2,6},{3,7},{4,0},{5,1},{6,2},{7,3},{8,12},{9,13},{10,... | collective-permute-start | bytes 1572872 | tf_op jit(solution)/shard_map/ppermute | solution.py:39
  32.4 2.0 %collective-permute-start.12 = (bf16[128,2048]{1,0:T(8,128)(2,1)S(1)}, bf16[128,2048]{1,0:T(8,128)(2,1)S(1)}, u32[]{:S(2)}, u32[]{:S(2)}) collective-permute-start(bf16[128,2048]{1,0:T(8,128)(2,1)S(1)} %get-tuple-element.98), channel_id=1, source_target_pairs={{0,4},{1,5},{2,6},{3,7},{4,0},{5,1},{6,2},{7,3},{8,12},{9,13},{10,... | collective-permute-start | bytes 1572872 | tf_op jit(solution)/shard_map/ppermute | solution.py:39
  34.5 9.2 %collective-permute-start.13 = (bf16[128,2048]{1,0:T(8,128)(2,1)S(1)}, bf16[128,2048]{1,0:T(8,128)(2,1)S(1)}, u32[]{:S(2)}, u32[]{:S(2)}) collective-permute-start(bf16[128,2048]{1,0:T(8,128)(2,1)S(1)} %add_convert_fusion.2), channel_id=1, source_target_pairs={{0,16},{1,17},{2,18},{3,19},{4,12},{5,13},{6,14},{7,15},{8,24},{9,... | collective-permute-start | bytes 1572872 | tf_op jit(solution)/shard_map/ppermute | solution.py:39
  36.1 1.9 %collective-permute-start.15 = (bf16[128,2048]{1,0:T(8,128)(2,1)S(1)}, bf16[128,2048]{1,0:T(8,128)(2,1)S(1)}, u32[]{:S(2)}, u32[]{:S(2)}) collective-permute-start(bf16[128,2048]{1,0:T(8,128)(2,1)S(1)} %collective-permute-done.14.refs_0_), channel_id=1, source_target_pairs={{0,4},{1,5},{2,6},{3,7},{4,0},{5,1},{6,2},{7,3},{8,12},{9,13},{10,... | collective-permute-start | bytes 1572872 | tf_op jit(solution)/shard_map/ppermute | solution.py:39
  39.2 2.0 %collective-permute-start.17 = (bf16[128,2048]{1,0:T(8,128)(2,1)S(1)}, bf16[128,2048]{1,0:T(8,128)(2,1)S(1)}, u32[]{:S(2)}, u32[]{:S(2)}) collective-permute-start(bf16[128,2048]{1,0:T(8,128)(2,1)S(1)} %get-tuple-element.115), channel_id=1, source_target_pairs={{0,4},{1,5},{2,6},{3,7},{4,0},{5,1},{6,2},{7,3},{8,12},{9,13},{10,... | collective-permute-start | bytes 1572872 | tf_op jit(solution)/shard_map/ppermute | solution.py:39
  41.3 9.2 %collective-permute-start.19 = (bf16[128,2048]{1,0:T(8,128)(2,1)S(1)}, bf16[128,2048]{1,0:T(8,128)(2,1)S(1)}, u32[]{:S(2)}, u32[]{:S(2)}) collective-permute-start(bf16[128,2048]{1,0:T(8,128)(2,1)S(1)} %add_convert_fusion.1), channel_id=1, source_target_pairs={{0,16},{1,17},{2,18},{3,19},{4,12},{5,13},{6,14},{7,15},{8,24},{9,... | collective-permute-start | bytes 1572872 | tf_op jit(solution)/shard_map/ppermute | solution.py:39
  42.6 5.3 %collective-permute-start.18 = (bf16[128,2048]{1,0:T(8,128)(2,1)S(1)}, bf16[128,2048]{1,0:T(8,128)(2,1)S(1)}, u32[]{:S(2)}, u32[]{:S(2)}) collective-permute-start(bf16[128,2048]{1,0:T(8,128)(2,1)S(1)} %get-tuple-element.117), channel_id=1, source_target_pairs={{0,4},{1,5},{2,6},{3,7},{4,0},{5,1},{6,2},{7,3},{8,12},{9,13},{10,... | collective-permute-start | bytes 1572872 | tf_op jit(solution)/shard_map/ppermute | solution.py:39
  44.0 16.8 %collective-permute-start.23 = (bf16[32,2048]{1,0:T(8,128)(2,1)S(1)}, bf16[32,2048]{1,0:T(8,128)(2,1)S(1)}, u32[]{:S(2)}, u32[]{:S(2)}) collective-permute-start(bf16[32,2048]{1,0:T(8,128)(2,1)S(1)} %get-tuple-element.140), channel_id=1, source_target_pairs={{0,2},{1,3},{2,0},{3,1},{4,6},{5,7},{6,4},{7,5},{8,10},{9,11},{10,... | collective-permute-start | bytes 393224 | tf_op jit(solution)/shard_map/ppermute | solution.py:39
  45.5 16.3 %collective-permute-start.22 = (bf16[32,2048]{1,0:T(8,128)(2,1)S(1)}, bf16[32,2048]{1,0:T(8,128)(2,1)S(1)}, u32[]{:S(2)}, u32[]{:S(2)}) collective-permute-start(bf16[32,2048]{1,0:T(8,128)(2,1)S(1)} %get-tuple-element.141), channel_id=1, source_target_pairs={{0,3},{1,2},{2,1},{3,0},{4,7},{5,6},{6,5},{7,4},{8,11},{9,10},{10,... | collective-permute-start | bytes 393224 | tf_op jit(solution)/shard_map/ppermute | solution.py:39
  47.8 13.9 %collective-permute-start.21 = (bf16[32,2048]{1,0:T(8,128)(2,1)S(1)}, bf16[32,2048]{1,0:T(8,128)(2,1)S(1)}, u32[]{:S(2)}, u32[]{:S(2)}) collective-permute-start(bf16[32,2048]{1,0:T(8,128)(2,1)S(1)} %get-tuple-element.142), channel_id=1, source_target_pairs={{0,1},{1,0},{2,3},{3,2},{4,5},{5,4},{6,7},{7,6},{8,9},{9,8},{10,11... | collective-permute-start | bytes 393224 | tf_op jit(solution)/shard_map/ppermute | solution.py:39
  50.7 6.4 %collective-permute-start.20 = (bf16[64,2048]{1,0:T(8,128)(2,1)S(1)}, bf16[64,2048]{1,0:T(8,128)(2,1)S(1)}, u32[]{:S(2)}, u32[]{:S(2)}) collective-permute-start(bf16[64,2048]{1,0:T(8,128)(2,1)S(1)} %get-tuple-element.119), channel_id=1, source_target_pairs={{0,8},{1,9},{2,10},{3,11},{4,20},{5,21},{6,22},{7,23},{8,0},{9,1},... | collective-permute-start | bytes 786440 | tf_op jit(solution)/shard_map/ppermute | solution.py:39
  57.2 6.2 %collective-permute-start.27 = (bf16[16,2048]{1,0:T(8,128)(2,1)S(1)}, bf16[16,2048]{1,0:T(8,128)(2,1)S(1)}, u32[]{:S(2)}, u32[]{:S(2)}) collective-permute-start(bf16[16,2048]{1,0:T(8,128)(2,1)S(1)} %get-tuple-element.143), channel_id=1, source_target_pairs={{0,3},{1,2},{2,1},{3,0},{4,7},{5,6},{6,5},{7,4},{8,11},{9,10},{10,... | collective-permute-start | bytes 196616 | tf_op jit(solution)/shard_map/ppermute | solution.py:39
  60.2 5.4 %collective-permute-start.26 = (bf16[16,2048]{1,0:T(8,128)(2,1)S(1)}, bf16[16,2048]{1,0:T(8,128)(2,1)S(1)}, u32[]{:S(2)}, u32[]{:S(2)}) collective-permute-start(bf16[16,2048]{1,0:T(8,128)(2,1)S(1)} %get-tuple-element.144), channel_id=1, source_target_pairs={{0,2},{1,3},{2,0},{3,1},{4,6},{5,7},{6,4},{7,5},{8,10},{9,11},{10,... | collective-permute-start | bytes 196616 | tf_op jit(solution)/shard_map/ppermute | solution.py:39
  60.8 5.0 %collective-permute-start.25 = (bf16[16,2048]{1,0:T(8,128)(2,1)S(1)}, bf16[16,2048]{1,0:T(8,128)(2,1)S(1)}, u32[]{:S(2)}, u32[]{:S(2)}) collective-permute-start(bf16[16,2048]{1,0:T(8,128)(2,1)S(1)} %get-tuple-element.145), channel_id=1, source_target_pairs={{0,1},{1,0},{2,3},{3,2},{4,5},{5,4},{6,7},{7,6},{8,9},{9,8},{10,11... | collective-permute-start | bytes 196616 | tf_op jit(solution)/shard_map/ppermute | solution.py:39
  61.9 4.3 %collective-permute-start.24 = (bf16[16,2048]{1,0:T(8,128)(2,1)S(1)}, bf16[16,2048]{1,0:T(8,128)(2,1)S(1)}, u32[]{:S(2)}, u32[]{:S(2)}) collective-permute-start(bf16[16,2048]{1,0:T(8,128)(2,1)S(1)} %get-tuple-element.147), channel_id=1, source_target_pairs={{0,8},{1,9},{2,10},{3,11},{4,20},{5,21},{6,22},{7,23},{8,0},{9,1},... | collective-permute-start | bytes 196616 | tf_op jit(solution)/shard_map/ppermute | solution.py:39
